TPU v7x, 512 devices: a whole 4x8x8 slice. The times are simulated.
512 devices in a mesh: grp: 16 (over y_hi, x, core), env: 32 (over z, y_lo).
Axes of the slice: x: 4, y: 8 (y_hi: 2, y_lo: 4; y = y_hi * 4 + y_lo), z: 8, core: 2. Of those that a mesh axis runs over, the one named last changes fastest.
Arguments:
- wavefunction: bfloat16 [8192, 4096], P('grp', 'env'), may hold values from -6 to 6
- left_tiles: bfloat16 [8192, 128, 128], P(('grp', 'env')), may hold values from -0.5 to 0.5
- right_tiles: bfloat16 [26, 4096, 128], P(None, 'env'), may hold values from -0.5 to 0.5
- term_source: int32 [8192], P('grp'), may hold values from 0 to 63
- term_target: int32 [8192], P('grp'), may hold values from 0 to 63
- right_index: int32 [8192], P('grp'), may hold values from 0 to 25
- term_sector: int32 [8192, 1], P('grp'), may hold values from 0 to 31; in each aligned block of 16 rows (0 to 15, 16 to 31, ...) at most 4 rows name the same one
- column_sector: int32 [32], replicated, may hold values from 0 to 31
Outputs:
- applied: bfloat16 [8192, 4096], P('grp', 'env')
Inputs may be any that keep to these rules, and one draw needn't show every extreme that they name: `term_sector`: within each aligned block of 16 terms (the terms of one device) no sector appears more than 4 times, and every sector appears somewhere.
All inputs are finite; a program needn't handle non-finite values.
Results may differ from a plain program's by a relative error of at most 0.009.
Values may be sent and summed in bfloat16 or wider, within the bound.
No kernel may reach another device: no remote copies, remote signals or barrier semaphores. Data moves between devices by JAX's collectives and lax.ppermute only.
A program may use at most 64 MiB of HBM per device.

v0:
```python
import math

import jax
import jax.numpy as jnp
from jax import lax
from jax.sharding import PartitionSpec as P


def contribute(
    running, left_pick, source_rows, target_rows, right_rows, kept_mask, blocks, right_tiles
):
    source_blocks = blocks[source_rows]
    block_product = jnp.einsum(
        "kab,kbc->kac", left_pick, source_blocks, preferred_element_type=jnp.float32
    ).astype(jnp.bfloat16)
    term_image = jnp.einsum(
        "kac,kcd->kad", block_product, right_tiles[right_rows], preferred_element_type=jnp.float32
    )
    term_image = term_image * kept_mask[:, None, None]
    return running.at[target_rows].add(term_image)


def shards(
    wavefunction,
    left_tiles,
    right_tiles,
    term_source,
    term_target,
    right_index,
    term_sector,
    column_sector,
):
    tile_size = left_tiles.shape[1]
    env_place = lax.axis_index("env")
    sectors = term_sector[:, 0]
    my_sector = column_sector[env_place]
    gathered = lax.all_gather(wavefunction, "grp", axis=0, tiled=True)
    block_count = gathered.shape[0] // tile_size
    blocks = gathered.reshape(block_count, tile_size, tile_size)
    running = jnp.zeros((block_count, tile_size, tile_size), jnp.float32)
    summed_rows = running
    shard_piece = lax.all_gather(left_tiles, "env", axis=0, tiled=True)
    piece_count = shard_piece.shape[0]
    block_len = math.gcd(piece_count, 32)
    groups_len = piece_count // block_len

    def select(values):
        return values.reshape(groups_len, block_len)

    kept_mask = (select(sectors) == my_sector).astype(jnp.float32)
    slices = (
        shard_piece.reshape(groups_len, block_len, tile_size, tile_size),
        select(term_source),
        select(term_target),
        select(right_index),
        kept_mask,
    )

    def accumulate(partial_rows, sliced):
        return (
            contribute(
                partial_rows,
                sliced[0],
                sliced[1],
                sliced[2],
                sliced[3],
                sliced[4],
                blocks,
                right_tiles,
            ),
            None,
        )

    summed_rows, ignored_out = lax.scan(accumulate, summed_rows, slices)
    running = summed_rows
    summed = lax.psum_scatter(
        running.reshape(block_count * tile_size, tile_size).astype(jnp.bfloat16),
        "grp",
        scatter_dimension=0,
        tiled=True,
    )
    return summed


def solution(mesh):
    placed = (
        P("grp", "env"),
        P(("grp", "env"), None, None),
        P(None, "env", None),
        P("grp"),
        P("grp"),
        P("grp"),
        P("grp", None),
        P(),
    )
    return jax.shard_map(
        shards, mesh=mesh, in_specs=placed, out_specs=P("grp", "env"), check_vma=False
    )
```

profile of v0, /device:TPU:56, one launch (start us, length us, event | category | flops | bytes accessed | tf_op | source)
XLA Modules:
  0.0 776.7 jit_solution(16551627581653641004)
XLA Ops:
  13.0 64.1 %all-gather.5.cloned.1.call-done = bf16[8192,128]{1,0:T(8,128)(2,1)} async-done(((bf16[512,128]{1,0:T(8,128)(2,1)}), bf16[8192,128]{1,0:T(8,128)(2,1)}) %all-gather.5.cloned.1.call-update) | async-done | bytes 2097168 | tf_op jit(solution)/shard_map/all_gather | solution.py:37
  77.1 376.8 %all-gather.3.cloned.1.call-done = bf16[512,128,128]{2,1,0:T(8,128)(2,1)} async-done(((bf16[16,128,128]{2,1,0:T(8,128)(2,1)}), bf16[512,128,128]{2,1,0:T(8,128)(2,1)}) %all-gather.3.cloned.1.call-update) | async-done | bytes 16777232 | tf_op jit(solution)/shard_map/all_gather | solution.py:42
  456.3 220.1 %while.10 = (s32[]{:T(128)}, f32[64,128,128]{2,1,0:T(8,128)}, s32[16,32]{1,0:T(8,128)S(1)}, bf16[16,32,128,128]{3,2,1,0:T(8,128)(2,1)}, s32[16,32]{1,0:T(8,128)S...) while((s32[]{:T(128)}, f32[64,128,128]{2,1,0:T(8,128)}, ...), condition=%wide.region_2.3_spmd, body=%wide.region_0.2_spmd.sunk | while | flops 270010656 | bytes 15738749 | solution.py:74
  458.8 2.8 gather_fusion
  463.8 6.2 scatter_fusion
  472.5 2.8 gather_fusion
  477.5 6.2 scatter_fusion
  486.2 2.8 gather_fusion
  491.3 6.4 scatter_fusion
  505.1 6.2 scatter_fusion
  518.9 6.3 scatter_fusion
  532.7 6.2 scatter_fusion
  546.4 6.2 scatter_fusion
  560.1 6.2 scatter_fusion
  573.9 6.3 scatter_fusion
  587.7 6.3 scatter_fusion
  601.4 6.2 scatter_fusion
  615.2 6.3 scatter_fusion
  628.9 6.2 scatter_fusion
  642.7 6.2 scatter_fusion
  656.5 6.2 scatter_fusion
  670.2 6.2 scatter_fusion
  676.4 3.9 convert_element_type.17
  680.3 89.8 %reduce-scatter.2.cloned.1.call-done = bf16[512,128]{1,0:T(8,128)(2,1)} async-done(((bf16[8192,128]{1,0:T(8,128)(2,1)}), bf16[512,128]{1,0:T(8,128)(2,1)}) %reduce-scatter.2.cloned.1.call-update) | async-done | bytes 131088 | tf_op jit(solution)/shard_map/reduce_scatter | solution.py:76
  (138 shorter events, 119.8 us)
Async XLA Ops:
  6.5 70.6 %all-gather.5.cloned.1.call-start = ((), (), s32[]{:S(2)}) async-start(), calls=%async_computation.2 | async-start | bytes 2228224 | tf_op jit(solution)/shard_map/all_gather | solution.py:37
  7.3 446.6 %all-gather.3.cloned.1.call-start = ((), (), s32[]{:S(2)}) async-start(), calls=%async_computation.1 | async-start | bytes 17301504 | tf_op jit(solution)/shard_map/all_gather | solution.py:42
  8.0 762.1 %reduce-scatter.2.cloned.1.call-start = ((), (), s32[]{:S(2)}) async-start(), calls=%async_computation.3 | async-start | bytes 2228224 | tf_op jit(solution)/shard_map/reduce_scatter | solution.py:76
Sparse Core Ops, SparseCore 0:
  10.7 66.3 all-gather.4
  79.2 374.6 all-gather.2
  680.5 89.6 reduce-scatter.1
where the time goes:
time: 784 us; the launch traced here: 777 us
  waiting for transfers between devices  532 us (68%)
  other arithmetic  106 us (14%)
  local copies, waits for them, and re-layouts  89 us (11%)
  matrix products  36 us (5%)
  between operations  13.1 us (2%)
    all_gather x1, waiting for transfers between devices, shards(): shard_piece = lax.all_gather(left_tiles, 'env', axis=0, tiled=True)  377 us
    scatter-add x16, other arithmetic, contribute(): return running.at[target_rows].add(term_image)  100 us
    reduce_scatter x1, waiting for transfers between devices, shards(): lax.psum_scatter(running.reshape(block_count * tile_size, tile_size).asty...  89.8 us
    all_gather x1, waiting for transfers between devices, shards(): gathered = lax.all_gather(wavefunction, 'grp', axis=0, tiled=True)  64.1 us
    gather x16, local copies, waits for them, and re-layouts, contribute(): right_tiles[right_rows]  45.4 us
    gather x16, local copies, waits for them, and re-layouts, contribute(): source_blocks = blocks[source_rows]  37.4 us
    dot_general x16, matrix products, contribute(): jnp.einsum('kac,kcd->kad', block_product, right_tiles[right_rows], prefer...  36 us
  transfers between devices with their start and end apart: 3, of which 3 were waited for; matrix products, arithmetic and copies ran while one was open for 1% of the time, Pallas kernels for 0%

commit v1 on v0

v1 whole, which is shorter than its diff:
```python
import jax
import jax.numpy as jnp
from jax import lax
from jax.experimental import pallas as pl
from jax.experimental.pallas import tpu as pltpu
from jax.sharding import PartitionSpec as P

SLOTS = 4
UNROLL = 4


def pack_kernel(per, sector, column, tiles, out, heads, nexts, counts):
    place = lax.axis_index("env")
    columns = column.shape[0]
    sectors = heads.shape[0]

    def clear(s, carry):
        heads[s] = -1
        counts[s] = 0
        return carry

    lax.fori_loop(0, sectors, clear, 0)

    def chain(c, carry):
        s = column[c]
        nexts[c] = heads[s]
        heads[s] = c
        return carry

    lax.fori_loop(0, columns, chain, 0)

    def tile(i, carry):
        s = sector[place * per + i]
        k = counts[s]
        counts[s] = k + 1

        def send(c):
            out[c * SLOTS + k] = tiles[i]
            return nexts[c]

        lax.while_loop(lambda c: c >= 0, send, heads[s])
        return carry

    lax.fori_loop(0, per, tile, 0)


def apply_kernel(
    per, sector, source, target, index, column, tiles, blocks, rights, out, picked, acc
):
    wanted = column[lax.axis_index("env")]
    groups = sector.shape[0] // per

    def scan(b, n):
        k = jnp.int32(0)
        for i in range(per):
            t = b * per + i
            match = (sector[t] == wanted).astype(jnp.int32)
            picked[n] = t * SLOTS + k
            n = n + match
            k = k + match
        return n

    n = lax.fori_loop(0, groups, scan, jnp.int32(0))
    for j in range(UNROLL):
        picked[n + j] = -1
    count = out.shape[0]

    def clear(r, carry):
        acc[r] = jnp.zeros(acc.shape[1:], acc.dtype)
        return carry

    lax.fori_loop(0, count, clear, 0)

    def terms(j, carry):
        for u in range(UNROLL):
            entry = picked[j * UNROLL + u]
            kept = jnp.maximum(entry, 0)
            t = kept // SLOTS
            slot = (t // per) * SLOTS + kept % SLOTS
            row = jnp.where(entry < 0, count, target[t])
            product = jnp.dot(
                tiles[slot], blocks[source[t]], preferred_element_type=jnp.float32
            ).astype(jnp.bfloat16)
            acc[row] += jnp.dot(
                product, rights[index[t]], preferred_element_type=jnp.float32
            )
        return carry

    lax.fori_loop(0, (n + UNROLL - 1) // UNROLL, terms, 0)

    def finish(r, carry):
        out[r] = acc[r].astype(out.dtype)
        return carry

    lax.fori_loop(0, count, finish, 0)


def shards(
    wavefunction,
    left_tiles,
    right_tiles,
    term_source,
    term_target,
    right_index,
    term_sector,
    column_sector,
):
    per, size, _ = left_tiles.shape
    columns = column_sector.shape[0]
    slots = columns * SLOTS
    smem = pl.BlockSpec(memory_space=pltpu.SMEM)
    vmem = pl.BlockSpec(memory_space=pltpu.VMEM)
    sectors = term_sector[:, 0]
    blocks = lax.all_gather(wavefunction, "grp", axis=0, tiled=True)
    count = blocks.shape[0] // size
    blocks = blocks.reshape(count, size, size)
    packed = pl.pallas_call(
        lambda *refs: pack_kernel(per, *refs),
        out_shape=jax.ShapeDtypeStruct((slots, size, size), jnp.bfloat16),
        in_specs=[smem, smem, vmem],
        out_specs=vmem,
        scratch_shapes=[
            pltpu.SMEM((columns,), jnp.int32),
            pltpu.SMEM((columns,), jnp.int32),
            pltpu.SMEM((columns,), jnp.int32),
        ],
        compiler_params=pltpu.CompilerParams(vmem_limit_bytes=16 * 2**20),
    )(sectors, column_sector, left_tiles)
    tiles = lax.all_to_all(packed, "env", 0, 0, tiled=True)
    partial = pl.pallas_call(
        lambda *refs: apply_kernel(per, *refs),
        out_shape=jax.ShapeDtypeStruct((count, size, size), jnp.bfloat16),
        in_specs=[smem] * 5 + [vmem] * 3,
        out_specs=vmem,
        scratch_shapes=[
            pltpu.SMEM((sectors.shape[0] + UNROLL,), jnp.int32),
            pltpu.VMEM((count + 1, size, size), jnp.float32),
        ],
        compiler_params=pltpu.CompilerParams(vmem_limit_bytes=32 * 2**20),
    )(
        sectors,
        term_source,
        term_target,
        right_index,
        column_sector,
        tiles,
        blocks,
        right_tiles,
    )
    parts = lax.all_to_all(partial, "grp", 0, 0, tiled=True)
    groups = lax.axis_size("grp")
    parts = parts.reshape(groups, -1, size)
    return jnp.sum(parts.astype(jnp.float32), axis=0).astype(jnp.bfloat16)


def solution(mesh):
    placed = (
        P("grp", "env"),
        P(("grp", "env"), None, None),
        P(None, "env", None),
        P("grp"),
        P("grp"),
        P("grp"),
        P("grp", None),
        P(),
    )
    return jax.shard_map(
        shards, mesh=mesh, in_specs=placed, out_specs=P("grp", "env"), check_vma=False
    )
```

time: 784 us -> 252 us (0.32)
  the two profiles are of different devices: /device:TPU:56 before, /device:TPU:328 now
where the time goes in v1:
time: 252 us
  waiting for transfers between devices  114 us (45%)
  blocking collectives  101 us (40%)
  between operations  13.5 us (5%)
  starting transfers between devices  9.72 us (4%)
  Pallas kernels  7.33 us (3%)
  local copies, waits for them, and re-layouts  5.96 us (2%)
    all_to_all x1, blocking collectives, shards(): parts = lax.all_to_all(partial, 'grp', 0, 0, tiled=True)  101 us
    all_gather x1, waiting for transfers between devices, shards(): blocks = lax.all_gather(wavefunction, 'grp', axis=0, tiled=True)  79 us
    all_to_all x1, waiting for transfers between devices, shards(): tiles = lax.all_to_all(packed, 'env', 0, 0, tiled=True)  33.9 us
    all_to_all x1, starting transfers between devices, shards(): tiles = lax.all_to_all(packed, 'env', 0, 0, tiled=True)  9.68 us
    unnamed x22, local copies, waits for them, and re-layouts  5.96 us
    pallas_call x1, Pallas kernels, shards(): pl.pallas_call(lambda *refs: apply_kernel(per, *refs), out_shape=jax.Shap...  5.9 us
  transfers between devices with their start and end apart: 2, of which 2 were waited for; matrix products, arithmetic and copies ran while one was open for 0% of the time, Pallas kernels for 0%

profile of v1, /device:TPU:328, one launch (start us, length us, event | category | flops | bytes accessed | tf_op | source)
XLA Modules:
  0.0 251.7 jit_solution(17056733188598565751)
XLA Ops:
  6.5 1.0 copy-done.3
  7.6 0.7 copy-done.4
  8.3 0.7 copy-done.6
  8.9 1.4 shard_map.82
  10.4 0.0 copy-start
  10.4 2.0 copy-done
  12.3 0.0 copy-start.9
  12.4 0.0 copy-start.10
  12.4 9.7 %all-to-all-start = ((bf16[128,128,128]{2,1,0:T(8,128)(2,1)}), bf16[128,128,128]{2,1,0:T(8,128)(2,1)}, u32[]{:S(2)}, u32[]{:S(2)}) async-start(bf16[128,128,128]{2,1,0:T(8,128)(2,1)} %copy-done), calls=%async_computation | async-start | bytes 8388608 | tf_op jit(solution)/shard_map/all_to_all | solution.py:129
  22.0 0.0 all-gather.2.cloned.1.call-start
  22.1 0.7 all-gather.2.cloned.1.call-update
  22.8 79.0 %all-gather.2.cloned.1.call-done = bf16[8192,128]{1,0:T(8,128)(2,1)} async-done(((bf16[512,128]{1,0:T(8,128)(2,1)}), bf16[8192,128]{1,0:T(8,128)(2,1)}) %all-gather.2.cloned.1.call-update) | async-done | bytes 2097168 | tf_op jit(solution)/shard_map/all_gather | solution.py:114
  101.8 33.9 %all-to-all-done.refs_5_ = bf16[128,128,128]{2,1,0:T(8,128)(2,1)} async-done(((bf16[128,128,128]{2,1,0:T(8,128)(2,1)}), bf16[128,128,128]{2,1,0:T(8,128)(2,1)}, u32[]{:S(2)}, u32[]{:S(2)}) %all-to-all-start) | async-done | bytes 4194336 | tf_op jit(solution)/shard_map/all_to_all | solution.py:129
  135.7 0.0 copy-done.2
  135.7 0.0 copy-done.5
  135.7 0.0 copy-done.7
  135.7 0.0 copy-done.8
  135.7 0.0 copy-done.9
  135.7 0.0 copy-done.10
  135.7 0.0 copy-start.1
  135.7 1.6 copy-done.1
  137.3 5.9 %shard_map.83 = bf16[64,128,128]{2,1,0:T(8,128)(2,1)S(1)} custom-call(s32[512]{0:T(512)S(1)} %bitcast.7, s32[512]{0:T(512)S(1)} %copy-done.8, s32[512]{0:T(512)S(1)} %copy-done.9, s32[512]{0:T(512)S(1)} %copy-done.10, s32[32]{0:T(128)S(1)} %copy-done.7, bf16[128,128,128]{2,1,0:T(8,128)(2,1)} %all-to-all-done.refs_5_, bf16[64,128,128]{2,1,0:T(8,128)(2,1)S(1)} %bitcast.5, ...), custom_call_target="tpu_custom_call" | custom-call | tf_op jit(solution)/shard_map/pallas_call | solution.py:130
  143.2 100.7 %all_to_all.10 = bf16[64,128,128]{2,1,0:T(8,128)(2,1)S(1)} all-to-all(bf16[64,128,128]{2,1,0:T(8,128)(2,1)S(1)} %shard_map.83), channel_id=1, replica_groups=mesh['grp'=16,'env'=32] {'grp'}, dimensions={0} | all-to-all | bytes 4194304 | tf_op jit(solution)/shard_map/all_to_all | solution.py:150
  243.9 0.9 bitcast_reduce_fusion
  (7 shorter events, 0.0 us)
Async XLA Ops:
  6.5 1.0 copy-start.3
  7.6 0.7 copy-start.4
  8.3 0.7 copy-start.6
  10.4 2.0 copy-start
  12.3 123.4 %copy-start.2 = (bf16[26,128,128]{2,1,0:T(8,128)(2,1)S(1)}, bf16[26,128,128]{2,1,0:T(8,128)(2,1)}, u32[]{:S(2)}) copy-start(bf16[26,128,128]{2,1,0:T(8,128)(2,1)} %refs_7_.1) | copy-start | bytes 2555908
  12.3 123.4 %copy-start.5 = (s32[512,1]{0,1:T(1,128)S(1)}, s32[512,1]{0,1:T(1,128)}, u32[]{:S(2)}) copy-start(s32[512,1]{0,1:T(1,128)} %param.14) | copy-start | bytes 6148
  12.3 123.4 %copy-start.7 = (s32[32]{0:T(128)S(1)}, s32[32]{0:T(128)}, u32[]{:S(2)}) copy-start(s32[32]{0:T(128)} %refs_4_.1) | copy-start | bytes 388
  12.3 123.4 %copy-start.8 = (s32[512]{0:T(512)S(1)}, s32[512]{0:T(512)}, u32[]{:S(2)}) copy-start(s32[512]{0:T(512)} %refs_1_.3) | copy-start | bytes 6148
  12.3 123.4 %copy-start.9 = (s32[512]{0:T(512)S(1)}, s32[512]{0:T(512)}, u32[]{:S(2)}) copy-start(s32[512]{0:T(512)} %refs_2_.3) | copy-start | bytes 6148
  12.4 123.4 %copy-start.10 = (s32[512]{0:T(512)S(1)}, s32[512]{0:T(512)}, u32[]{:S(2)}) copy-start(s32[512]{0:T(512)} %refs_3_.1) | copy-start | bytes 6148
  12.4 123.3 %all-to-all-start = ((bf16[128,128,128]{2,1,0:T(8,128)(2,1)}), bf16[128,128,128]{2,1,0:T(8,128)(2,1)}, u32[]{:S(2)}, u32[]{:S(2)}) async-start(bf16[128,128,128]{2,1,0:T(8,128)(2,1)} %copy-done), calls=%async_computation | async-start | bytes 8388608 | tf_op jit(solution)/shard_map/all_to_all | solution.py:129
  22.0 79.8 %all-gather.2.cloned.1.call-start = ((), (), s32[]{:S(2)}) async-start(), calls=%async_computation.2 | async-start | bytes 2228224 | tf_op jit(solution)/shard_map/all_gather | solution.py:114
  135.7 1.6 copy-start.1
Sparse Core Ops, SparseCore 0:
  26.2 75.5 all-gather.1

commit v2 on v1

v2 whole, which is shorter than its diff:
```python
import jax
import jax.numpy as jnp
from jax import lax
from jax.experimental import pallas as pl
from jax.experimental.pallas import tpu as pltpu
from jax.sharding import Mesh
from jax.sharding import PartitionSpec as P

GRP = ("y_hi", "x", "core")
ENV = ("z", "y_lo")
HALVES, XS, CORES = 2, 4, 2
DEEP, LOW = 8, 4
ROWS_DEV = 4
SLOTS = 4
UNROLL = 4


def env_place():
    return lax.axis_index("z") * lax.axis_size("y_lo") + lax.axis_index("y_lo")


def pack_kernel(per, sector, column, tiles, out, heads, nexts, counts):
    place = env_place()
    columns = column.shape[0]
    sectors = heads.shape[0]

    def clear(s, carry):
        heads[s] = -1
        counts[s] = 0
        return carry

    lax.fori_loop(0, sectors, clear, 0)

    def chain(c, carry):
        s = column[c]
        nexts[c] = heads[s]
        heads[s] = c
        return carry

    lax.fori_loop(0, columns, chain, 0)

    def tile(i, carry):
        s = sector[place * per + i]
        k = counts[s]
        counts[s] = k + 1

        def send(c):
            out[c * SLOTS + k] = tiles[i]
            return nexts[c]

        lax.while_loop(lambda c: c >= 0, send, heads[s])
        return carry

    lax.fori_loop(0, per, tile, 0)


def place_of(row, core):
    group = row // ROWS_DEV
    rest = row % ROWS_DEV
    other = (group % CORES) ^ core
    return ((other * XS + (group // CORES) % XS) * HALVES + group // (CORES * XS)) * ROWS_DEV + rest


def apply_kernel(
    per, sector, source, target, index, column, tiles, near, far, rights, mine, theirs, picked, acc, blocks
):
    wanted = column[env_place()]
    core = lax.axis_index("core")
    half = near.shape[0]
    count = 2 * half

    def gather(r, carry):
        blocks[r] = near[r]
        blocks[half + r] = far[r]
        return carry

    lax.fori_loop(0, half, gather, 0)
    groups = sector.shape[0] // per

    def scan(b, n):
        k = jnp.int32(0)
        for i in range(per):
            t = b * per + i
            match = (sector[t] == wanted).astype(jnp.int32)
            picked[n] = t * SLOTS + k
            n = n + match
            k = k + match
        return n

    n = lax.fori_loop(0, groups, scan, jnp.int32(0))
    for j in range(UNROLL):
        picked[n + j] = -1

    def clear(r, carry):
        acc[r] = jnp.zeros(acc.shape[1:], acc.dtype)
        return carry

    lax.fori_loop(0, count, clear, 0)

    def terms(j, carry):
        for u in range(UNROLL):
            entry = picked[j * UNROLL + u]
            kept = jnp.maximum(entry, 0)
            t = kept // SLOTS
            slot = (t // per) * SLOTS + kept % SLOTS
            row = jnp.where(entry < 0, count, place_of(target[t], core))
            product = jnp.dot(
                tiles[slot], blocks[place_of(source[t], core)], preferred_element_type=jnp.float32
            ).astype(jnp.bfloat16)
            acc[row] += jnp.dot(
                product, rights[index[t]], preferred_element_type=jnp.float32
            )
        return carry

    lax.fori_loop(0, (n + UNROLL - 1) // UNROLL, terms, 0)

    def finish(r, carry):
        mine[r] = acc[r].astype(mine.dtype)
        theirs[r] = acc[half + r].astype(theirs.dtype)
        return carry

    lax.fori_loop(0, half, finish, 0)


def shards(
    wavefunction,
    left_tiles,
    right_tiles,
    term_source,
    term_target,
    right_index,
    term_sector,
    column_sector,
):
    per, size, _ = left_tiles.shape
    columns = column_sector.shape[0]
    slots = columns * SLOTS
    smem = pl.BlockSpec(memory_space=pltpu.SMEM)
    vmem = pl.BlockSpec(memory_space=pltpu.VMEM)
    sectors = term_sector[:, 0]
    psi = wavefunction.reshape(-1, size, size)
    near = lax.all_gather(psi, "y_hi", axis=0, tiled=True)
    near = lax.all_gather(near, "x", axis=0, tiled=True)
    swap = [(0, 1), (1, 0)]
    far = lax.ppermute(near, "core", swap)
    half = near.shape[0]
    packed = pl.pallas_call(
        lambda *refs: pack_kernel(per, *refs),
        out_shape=jax.ShapeDtypeStruct((slots, size, size), jnp.bfloat16),
        in_specs=[smem, smem, vmem],
        out_specs=vmem,
        scratch_shapes=[
            pltpu.SMEM((columns,), jnp.int32),
            pltpu.SMEM((columns,), jnp.int32),
            pltpu.SMEM((columns,), jnp.int32),
        ],
        compiler_params=pltpu.CompilerParams(vmem_limit_bytes=16 * 2**20),
    )(sectors, column_sector, left_tiles)
    tiles = lax.all_to_all(packed, ENV, 0, 0, tiled=True)
    block = jax.ShapeDtypeStruct((half, size, size), jnp.bfloat16)
    mine, theirs = pl.pallas_call(
        lambda *refs: apply_kernel(per, *refs),
        out_shape=(block, block),
        in_specs=[smem] * 5 + [vmem] * 4,
        out_specs=(vmem, vmem),
        scratch_shapes=[
            pltpu.SMEM((sectors.shape[0] + UNROLL,), jnp.int32),
            pltpu.VMEM((2 * half + 1, size, size), jnp.float32),
            pltpu.VMEM((2 * half, size, size), jnp.bfloat16),
        ],
        compiler_params=pltpu.CompilerParams(vmem_limit_bytes=40 * 2**20),
    )(
        sectors,
        term_source,
        term_target,
        right_index,
        column_sector,
        tiles,
        near,
        far,
        right_tiles,
    )
    total = mine.astype(jnp.float32) + lax.ppermute(theirs, "core", swap).astype(
        jnp.float32
    )
    for axis in ("x", "y_hi"):
        parts = lax.all_to_all(total.astype(jnp.bfloat16), axis, 0, 0, tiled=True)
        parts = parts.reshape((lax.axis_size(axis), -1) + parts.shape[1:])
        total = jnp.sum(parts.astype(jnp.float32), axis=0)
    return total.astype(jnp.bfloat16).reshape(wavefunction.shape)


def solution(mesh):
    physical = Mesh(
        mesh.devices.reshape(HALVES, XS, CORES, DEEP, LOW), GRP + ENV
    )
    placed = (
        P(GRP, ENV),
        P(GRP + ENV, None, None),
        P(None, ENV, None),
        P(GRP),
        P(GRP),
        P(GRP),
        P(GRP, None),
        P(),
    )
    return jax.shard_map(
        shards, mesh=physical, in_specs=placed, out_specs=P(GRP, ENV), check_vma=False
    )
```

time: 252 us -> 225 us (0.89)
  the two profiles are of different devices: /device:TPU:328 before, /device:TPU:136 now
where the time goes in v2:
time: 225 us
  blocking collectives  106 us (47%)
  waiting for transfers between devices  69.7 us (31%)
  starting transfers between devices  16.3 us (7%)
  between operations  13.5 us (6%)
  Pallas kernels  12.1 us (5%)
  local copies, waits for them, and re-layouts  5.59 us (2%)
    all_gather x1, blocking collectives, shards(): near = lax.all_gather(psi, 'y_hi', axis=0, tiled=True)  73 us
    all_gather x1, waiting for transfers between devices, shards(): near = lax.all_gather(near, 'x', axis=0, tiled=True)  64.4 us
    all_to_all x2, blocking collectives, shards(): parts = lax.all_to_all(total.astype(jnp.bfloat16), axis, 0, 0, tiled=True)  33.2 us
    all_to_all x1, starting transfers between devices, shards(): tiles = lax.all_to_all(packed, ENV, 0, 0, tiled=True)  12.4 us
    pallas_call x1, Pallas kernels, shards(): pl.pallas_call(lambda *refs: apply_kernel(per, *refs), out_shape=(block,...  10.6 us
    unnamed x24, local copies, waits for them, and re-layouts  5.59 us
  transfers between devices with their start and end apart: 4, of which 3 were waited for; matrix products, arithmetic and copies ran while one was open for 0% of the time, Pallas kernels for 0%

profile of v2, /device:TPU:136, one launch (start us, length us, event | category | flops | bytes accessed | tf_op | source)
XLA Modules:
  0.0 224.8 jit_solution(15065575249223078347)
XLA Ops:
  6.5 1.0 copy-done.3
  7.6 0.7 copy-done.4
  8.3 0.7 copy-done.9
  8.9 1.5 shard_map.82
  10.4 2.0 copy-done
  12.4 0.0 copy-start.7
  12.4 0.0 copy-start.8
  12.4 0.0 copy-start.10
  12.4 12.4 %all-to-all-start = ((bf16[128,128,128]{2,1,0:T(8,128)(2,1)}), bf16[128,128,128]{2,1,0:T(8,128)(2,1)}, u32[]{:S(2)}, u32[]{:S(2)}) async-start(bf16[128,128,128]{2,1,0:T(8,128)(2,1)} %copy-done), calls=%async_computation | async-start | bytes 8388608 | tf_op jit(solution)/shard_map/all_to_all | solution.py:159
  24.8 0.0 all-gather.2.cloned.1.call-start
  24.8 73.0 %all_gather.6 = bf16[8,128,128]{2,1,0:T(8,128)(2,1)} all-gather(bf16[4,128,128]{2,1,0:T(8,128)(2,1)S(1)} %bitcast.9), channel_id=1, replica_groups=mesh['y_hi'=2,'x'=4,'core'=2,'z'=8,'y_lo'=4] {'y_hi'}, dimensions={0}, use_global_device_ids=true | all-gather | bytes 393216 | tf_op jit(solution)/shard_map/all_gather | solution.py:142
  97.9 0.0 all-gather.2.cloned.1.call-update
  97.9 64.4 %all-gather.2.cloned.1.call-done.refs_6_ = bf16[32,128,128]{2,1,0:T(8,128)(2,1)} async-done(((bf16[8,128,128]{2,1,0:T(8,128)(2,1)}), bf16[32,128,128]{2,1,0:T(8,128)(2,1)}) %all-gather.2.cloned.1.call-update) | async-done | bytes 1048592 | tf_op jit(solution)/shard_map/all_gather | solution.py:143
  162.3 1.9 collective-permute-start
  164.2 2.8 %collective-permute-done.refs_7_ = bf16[32,128,128]{2,1,0:T(8,128)(2,1)S(1)} collective-permute-done((bf16[32,128,128]{2,1,0:T(8,128)(2,1)}, bf16[32,128,128]{2,1,0:T(8,128)(2,1)S(1)}, u32[]{:S(2)}, u32[]{:S(2)}) %collective-permute-start) | collective-permute-done | bytes 1048608 | tf_op jit(solution)/shard_map/ppermute | solution.py:145
  167.1 1.2 copy-done.1
  168.3 10.6 %shard_map.83 = (bf16[32,128,128]{2,1,0:T(8,128)(2,1)S(1)}, bf16[32,128,128]{2,1,0:T(8,128)(2,1)S(1)}) custom-call(s32[512]{0:T(512)S(1)} %bitcast.6, s32[512]{0:T(512)S(1)} %copy-done.6, s32[512]{0:T(512)S(1)} %copy-done.7, s32[512]{0:T(512)S(1)} %copy-done.8, s32[32]{0:T(128)S(1)} %copy-done.10, bf16[128,128,128]{2,1,0:T(8,128)(2,1)} %all-to-all-done.refs_5_, ...), custom_call_target="tpu_custom_call" | custom-call | tf_op jit(solution)/shard_map/pallas_call | solution.py:161
  178.9 2.0 collective-permute-start.1
  180.9 2.5 %collective-permute-done.1 = bf16[32,128,128]{2,1,0:T(8,128)(2,1)S(1)} collective-permute-done((bf16[32,128,128]{2,1,0:T(8,128)(2,1)S(1)}, bf16[32,128,128]{2,1,0:T(8,128)(2,1)S(1)}, u32[]{:S(2)}, u32[]{:S(2)}) %collective-permute-start.1) | collective-permute-done | bytes 1048608 | tf_op jit(solution)/shard_map/ppermute | solution.py:183
  183.5 0.4 add_convert_fusion
  183.8 18.6 %all_to_all.15 = bf16[32,128,128]{2,1,0:T(8,128)(2,1)S(1)} all-to-all(bf16[32,128,128]{2,1,0:T(8,128)(2,1)S(1)} %add_convert_fusion), channel_id=1, replica_groups=mesh['y_hi'=2,'x'=4,'core'=2,'z'=8,'y_lo'=4] {'x'}, dimensions={0} | all-to-all | bytes 2097152 | tf_op jit(solution)/shard_map/all_to_all | solution.py:187
  202.5 0.2 reduce_sum.24
  202.7 14.6 %all_to_all.16 = bf16[8,128,128]{2,1,0:T(8,128)(2,1)S(1)} all-to-all(bf16[8,128,128]{2,1,0:T(8,128)(2,1)S(1)} %reduce_sum.24), channel_id=1, replica_groups=mesh['y_hi'=2,'x'=4,'core'=2,'z'=8,'y_lo'=4] {'y_hi'}, dimensions={0} | all-to-all | bytes 524288 | tf_op jit(solution)/shard_map/all_to_all | solution.py:187
  217.3 0.7 reduce_sum.25
  (17 shorter events, 0.0 us)
Async XLA Ops:
  6.5 1.0 copy-start.3
  7.6 0.7 copy-start.4
  8.3 0.7 copy-start.9
  10.4 2.0 copy-start
  12.4 12.5 %copy-start.11 = (bf16[512,128]{1,0:T(8,128)(2,1)S(1)}, bf16[512,128]{1,0:T(8,128)(2,1)}, u32[]{:S(2)}) copy-start(bf16[512,128]{1,0:T(8,128)(2,1)} %param.8) | copy-start | bytes 393220
  12.4 154.7 %copy-start.2 = (bf16[26,128,128]{2,1,0:T(8,128)(2,1)S(1)}, bf16[26,128,128]{2,1,0:T(8,128)(2,1)}, u32[]{:S(2)}) copy-start(bf16[26,128,128]{2,1,0:T(8,128)(2,1)} %refs_8_.1) | copy-start | bytes 2555908
  12.4 154.7 %copy-start.5 = (s32[512,1]{0,1:T(1,128)S(1)}, s32[512,1]{0,1:T(1,128)}, u32[]{:S(2)}) copy-start(s32[512,1]{0,1:T(1,128)} %param.14) | copy-start | bytes 6148
  12.4 154.7 %copy-start.6 = (s32[512]{0:T(512)S(1)}, s32[512]{0:T(512)}, u32[]{:S(2)}) copy-start(s32[512]{0:T(512)} %refs_1_.3) | copy-start | bytes 6148
  12.4 154.7 %copy-start.7 = (s32[512]{0:T(512)S(1)}, s32[512]{0:T(512)}, u32[]{:S(2)}) copy-start(s32[512]{0:T(512)} %refs_2_.3) | copy-start | bytes 6148
  12.4 154.7 %copy-start.8 = (s32[512]{0:T(512)S(1)}, s32[512]{0:T(512)}, u32[]{:S(2)}) copy-start(s32[512]{0:T(512)} %refs_3_.1) | copy-start | bytes 6148
  12.4 154.7 %copy-start.10 = (s32[32]{0:T(128)S(1)}, s32[32]{0:T(128)}, u32[]{:S(2)}) copy-start(s32[32]{0:T(128)} %refs_4_.1) | copy-start | bytes 388
  12.4 154.6 %all-to-all-start = ((bf16[128,128,128]{2,1,0:T(8,128)(2,1)}), bf16[128,128,128]{2,1,0:T(8,128)(2,1)}, u32[]{:S(2)}, u32[]{:S(2)}) async-start(bf16[128,128,128]{2,1,0:T(8,128)(2,1)} %copy-done), calls=%async_computation | async-start | bytes 8388608 | tf_op jit(solution)/shard_map/all_to_all | solution.py:159
  24.8 137.5 %all-gather.2.cloned.1.call-start = ((), (), s32[]{:S(2)}) async-start(), calls=%async_computation.3 | async-start | bytes 1310720 | tf_op jit(solution)/shard_map/all_gather | solution.py:143
  162.3 4.8 %collective-permute-start = (bf16[32,128,128]{2,1,0:T(8,128)(2,1)}, bf16[32,128,128]{2,1,0:T(8,128)(2,1)S(1)}, u32[]{:S(2)}, u32[]{:S(2)}) collective-permute-start(bf16[32,128,128]{2,1,0:T(8,128)(2,1)} %all-gather.2.cloned.1.call-done.refs_6_), channel_id=1, source_target_pairs={{0,32},{32,0},{1,33},{33,1},{2,34},{34,2},{3,35},{35,3},{4,36},{36... | collective-permute-start | bytes 3145736 | tf_op jit(solution)/shard_map/ppermute | solution.py:145
  167.1 1.2 copy-start.1
  178.9 4.6 %collective-permute-start.1 = (bf16[32,128,128]{2,1,0:T(8,128)(2,1)S(1)}, bf16[32,128,128]{2,1,0:T(8,128)(2,1)S(1)}, u32[]{:S(2)}, u32[]{:S(2)}) collective-permute-start(bf16[32,128,128]{2,1,0:T(8,128)(2,1)S(1)} %get-tuple-element.8), channel_id=1, source_target_pairs={{0,32},{32,0},{1,33},{33,1},{2,34},{34,2},{3,35},{35,3},{4,36},{36... | collective-permute-start | bytes 3145736 | tf_op jit(solution)/shard_map/ppermute | solution.py:183
Sparse Core Ops, SparseCore 0:
  98.0 64.1 all-gather.1

commit v3 on v2

v3 whole, which is shorter than its diff:
```python
import jax
import jax.numpy as jnp
from jax import lax
from jax.experimental import pallas as pl
from jax.experimental.pallas import tpu as pltpu
from jax.sharding import Mesh
from jax.sharding import PartitionSpec as P

GRP = ("y_hi", "x", "core")
ENV = ("z", "y_lo")
HALVES, XS, CORES = 2, 4, 2
DEEP, LOW = 8, 4
ROWS_DEV = 4
SLOTS = 4
UNROLL = 4
LANES = 128


def env_place():
    return lax.axis_index("z") * LOW + lax.axis_index("y_lo")


def pack_kernel(per, sector, column, sector_rows, tiles, out, need, heads, nexts, counts):
    place = env_place()
    columns = column.shape[0]
    sectors = heads.shape[0]

    rows = sector_rows[...]
    lane = lax.broadcasted_iota(jnp.int32, rows.shape, 1) % per
    rank = jnp.ones(rows.shape, jnp.int32)
    for step in range(1, per):
        same = (pltpu.roll(rows, step, 1) == rows) & (lane >= step)
        rank = rank + same.astype(jnp.int32)
    wanted = rows == column[0]
    for c in range(1, columns):
        wanted = wanted | (rows == column[c])
    slots = jnp.maximum(jnp.max(jnp.where(wanted, rank, 0)), 1)
    need[0] = slots

    def clear(s, carry):
        heads[s] = -1
        counts[s] = 0
        return carry

    lax.fori_loop(0, sectors, clear, 0)

    def chain(c, carry):
        s = column[c]
        nexts[c] = heads[s]
        heads[s] = c
        return carry

    lax.fori_loop(0, columns, chain, 0)

    def tile(i, carry):
        s = sector[place * per + i]
        k = counts[s]
        counts[s] = k + 1

        def send(c):
            out[c * slots + k] = tiles[i]
            return nexts[c]

        lax.while_loop(lambda c: c >= 0, send, heads[s])
        return carry

    lax.fori_loop(0, per, tile, 0)


def apply_kernel(
    per,
    sector,
    source,
    target,
    index,
    column,
    need,
    tiles,
    near,
    far,
    rights,
    mine,
    theirs,
    picked,
    acc,
    blocks,
):
    wanted = column[env_place()]
    slots = need[0]
    half_at, x_at, core_at = (lax.axis_index(a) for a in GRP)
    groups = sector.shape[0] // per
    half = near.shape[0]
    count = 2 * half

    def read_place(row):
        group = row // ROWS_DEV
        core = (group % CORES) ^ core_at
        x = (x_at - (group // CORES) % XS) % XS
        y = group // (CORES * XS) ^ half_at
        return ((core * XS + x) * HALVES + y) * ROWS_DEV + row % ROWS_DEV

    def write_place(row):
        group = row // ROWS_DEV
        core = (group % CORES) ^ core_at
        x = (group // CORES) % XS
        y = group // (CORES * XS)
        return ((core * XS + x) * HALVES + y) * ROWS_DEV + row % ROWS_DEV

    def fill(r, carry):
        blocks[r] = near[r]
        blocks[half + r] = far[r]
        acc[r] = jnp.zeros(acc.shape[1:], acc.dtype)
        acc[half + r] = jnp.zeros(acc.shape[1:], acc.dtype)
        return carry

    lax.fori_loop(0, half, fill, 0)

    def scan(b, n):
        k = jnp.int32(0)
        for i in range(per):
            t = b * per + i
            match = (sector[t] == wanted).astype(jnp.int32)
            picked[n] = t * SLOTS + k
            n = n + match
            k = k + match
        return n

    n = lax.fori_loop(0, groups, scan, jnp.int32(0))
    for j in range(UNROLL):
        picked[n + j] = -1

    def terms(j, carry):
        for u in range(UNROLL):
            entry = picked[j * UNROLL + u]
            kept = jnp.maximum(entry, 0)
            t = kept // SLOTS
            slot = (t // per) * slots + kept % SLOTS
            row = jnp.where(entry < 0, count, write_place(target[t]))
            product = jnp.dot(
                tiles[slot],
                blocks[read_place(source[t])],
                preferred_element_type=jnp.float32,
            ).astype(jnp.bfloat16)
            acc[row] += jnp.dot(
                product, rights[index[t]], preferred_element_type=jnp.float32
            )
        return carry

    lax.fori_loop(0, (n + UNROLL - 1) // UNROLL, terms, 0)

    def finish(r, carry):
        mine[r] = acc[r].astype(mine.dtype)
        theirs[r] = acc[half + r].astype(theirs.dtype)
        return carry

    lax.fori_loop(0, half, finish, 0)


def swap(value, axis):
    return lax.ppermute(value, axis, [(0, 1), (1, 0)])


def step_x(value, step):
    return lax.ppermute(value, "x", [(i, (i + step) % XS) for i in range(XS)])


def exchange(slots):
    def run(packed):
        got = lax.all_to_all(packed[: DEEP * LOW * slots], ENV, 0, 0, tiled=True)
        if slots == SLOTS:
            return got
        rest = jnp.zeros((packed.shape[0] - got.shape[0],) + got.shape[1:], got.dtype)
        return jnp.concatenate([got, rest])

    return run


def shards(
    wavefunction,
    left_tiles,
    right_tiles,
    term_source,
    term_target,
    right_index,
    term_sector,
    column_sector,
):
    per, size, _ = left_tiles.shape
    columns = column_sector.shape[0]
    smem = pl.BlockSpec(memory_space=pltpu.SMEM)
    vmem = pl.BlockSpec(memory_space=pltpu.VMEM)
    sectors = term_sector[:, 0]

    psi = wavefunction.reshape(-1, size, size)
    pair = jnp.concatenate([psi, swap(psi, "y_hi")])
    packed, need = pl.pallas_call(
        lambda *refs: pack_kernel(per, *refs),
        out_shape=(
            jax.ShapeDtypeStruct((columns * SLOTS, size, size), jnp.bfloat16),
            jax.ShapeDtypeStruct((1,), jnp.int32),
        ),
        in_specs=[smem, smem, vmem, vmem],
        out_specs=(vmem, smem),
        scratch_shapes=[pltpu.SMEM((columns,), jnp.int32)] * 3,
        compiler_params=pltpu.CompilerParams(vmem_limit_bytes=16 * 2**20),
        cost_estimate=pl.CostEstimate(
            flops=0, bytes_accessed=8 * 2**20, transcendentals=0
        ),
    )(sectors, column_sector, sectors.reshape(-1, LANES), left_tiles)
    packed, pair = lax.optimization_barrier((packed, pair))
    near = [pair] + [step_x(pair, step) for step in range(1, XS)]
    tiles = lax.switch(need[0] - 1, [exchange(k + 1) for k in range(SLOTS)], packed)
    tiles, near = lax.optimization_barrier((tiles, near))
    near = jnp.concatenate(near)
    far = swap(near, "core")
    half = near.shape[0]
    block = jax.ShapeDtypeStruct((half, size, size), jnp.bfloat16)
    mine, theirs = pl.pallas_call(
        lambda *refs: apply_kernel(per, *refs),
        out_shape=(block, block),
        in_specs=[smem] * 6 + [vmem] * 4,
        out_specs=(vmem, vmem),
        scratch_shapes=[
            pltpu.SMEM((sectors.shape[0] + UNROLL,), jnp.int32),
            pltpu.VMEM((2 * half + 1, size, size), jnp.float32),
            pltpu.VMEM((2 * half, size, size), jnp.bfloat16),
        ],
        compiler_params=pltpu.CompilerParams(vmem_limit_bytes=40 * 2**20),
    )(
        sectors,
        term_source,
        term_target,
        right_index,
        column_sector,
        need,
        tiles,
        near,
        far,
        right_tiles,
    )
    total = mine.astype(jnp.float32) + swap(theirs, "core").astype(jnp.float32)
    for axis in ("x", "y_hi"):
        parts = lax.all_to_all(total.astype(jnp.bfloat16), axis, 0, 0, tiled=True)
        parts = parts.reshape((lax.axis_size(axis), -1) + parts.shape[1:])
        total = jnp.sum(parts.astype(jnp.float32), axis=0)
    return total.astype(jnp.bfloat16).reshape(wavefunction.shape)


def solution(mesh):
    physical = Mesh(mesh.devices.reshape(HALVES, XS, CORES, DEEP, LOW), GRP + ENV)
    placed = (
        P(GRP, ENV),
        P(GRP + ENV, None, None),
        P(None, ENV, None),
        P(GRP),
        P(GRP),
        P(GRP),
        P(GRP, None),
        P(),
    )
    return jax.shard_map(
        shards, mesh=physical, in_specs=placed, out_specs=P(GRP, ENV), check_vma=False
    )
```

time: 225 us -> 193 us (0.86)
  the two profiles are of different devices: /device:TPU:136 before, /device:TPU:56 now
where the time goes in v3:
time: 193 us; the launch traced here: 189 us
  blocking collectives  136 us (70%)
  Pallas kernels  19.9 us (10%)
  starting transfers between devices  18.8 us (10%)
  waiting for transfers between devices  8.02 us (4%)
  local copies, waits for them, and re-layouts  2.54 us (1%)
  other arithmetic  2.2 us (1%)
    all_to_all x1, blocking collectives, run(): got = lax.all_to_all(packed[:DEEP * LOW * slots], ENV, 0, 0, tiled=True)  108 us
    all_to_all x2, blocking collectives, shards(): parts = lax.all_to_all(total.astype(jnp.bfloat16), axis, 0, 0, tiled=True)  29 us
    pallas_call x1, Pallas kernels, shards(): pl.pallas_call(lambda *refs: apply_kernel(per, *refs), out_shape=(block,...  16.2 us
    ppermute x3, starting transfers between devices, step_x(): return lax.ppermute(value, 'x', [(i, (i + step) % XS) for i in range(XS)])  10.2 us
    ppermute x3, starting transfers between devices, swap(): return lax.ppermute(value, axis, [(0, 1), (1, 0)])  8.66 us
    ppermute x3, waiting for transfers between devices, swap(): return lax.ppermute(value, axis, [(0, 1), (1, 0)])  8.01 us
  transfers between devices with their start and end apart: 6, of which 3 were waited for; matrix products, arithmetic and copies ran while one was open for 0% of the time, Pallas kernels for 2%

profile of v3, /device:TPU:56, one launch (start us, length us, event | category | flops | bytes accessed | tf_op | source)
XLA Modules:
  0.0 188.9 jit_solution(3938096500628342181)
XLA Ops:
  0.0 4.7 %collective-permute-start = (bf16[4,128,128]{2,1,0:T(8,128)(2,1)}, bf16[4,128,128]{2,1,0:T(8,128)(2,1)S(1)}, u32[]{:S(2)}, u32[]{:S(2)}) collective-permute-start(bf16[4,128,128]{2,1,0:T(8,128)(2,1)} %bitcast.12), channel_id=1, source_target_pairs={{0,256},{256,0},{1,257},{257,1},{2,258},{258,2},{3,259},{259,3},{4... | collective-permute-start | bytes 393224 | tf_op jit(solution)/shard_map/ppermute | solution.py:160
  4.7 1.0 copy-done.1
  5.8 0.7 copy-done.2
  6.4 0.7 copy-done.7
  7.1 3.7 %shard_map.82 = (bf16[128,128,128]{2,1,0:T(8,128)(2,1)}, s32[1]{0:T(128)}) custom-call(s32[512]{0:T(512)S(1)} %bitcast.7, s32[32]{0:T(128)S(1)} %copy-done.7, s32[4,128]{1,0:T(4,128)S(1)} %bitcast.8, bf16[16,128,128]{2,1,0:T(8,128)(2,1)S(1)} %copy-done.1), custom_call_target="tpu_custom_call" | custom-call | bytes 8388608 | tf_op jit(solution)/shard_map/pallas_call | solution.py:196
  10.8 2.9 %collective-permute-done = bf16[4,128,128]{2,1,0:T(8,128)(2,1)S(1)} collective-permute-done((bf16[4,128,128]{2,1,0:T(8,128)(2,1)}, bf16[4,128,128]{2,1,0:T(8,128)(2,1)S(1)}, u32[]{:S(2)}, u32[]{:S(2)}) %collective-permute-start) | collective-permute-done | bytes 131104 | tf_op jit(solution)/shard_map/ppermute | solution.py:160
  13.7 0.9 pad_maximum_fusion
  14.6 4.7 %collective-permute-start.3 = (bf16[8,128,128]{2,1,0:T(8,128)(2,1)S(1)}, bf16[8,128,128]{2,1,0:T(8,128)(2,1)S(1)}, u32[]{:S(2)}, u32[]{:S(2)}) collective-permute-start(bf16[8,128,128]{2,1,0:T(8,128)(2,1)S(1)} %pad_maximum_fusion), channel_id=1, source_target_pairs={{0,192},{64,0},{128,64},{192,128},{1,193},{65,1},{129,65},{193,129... | collective-permute-start | bytes 786440 | tf_op jit(solution)/shard_map/ppermute | solution.py:164
  19.3 2.7 %collective-permute-start.2 = (bf16[8,128,128]{2,1,0:T(8,128)(2,1)S(1)}, bf16[8,128,128]{2,1,0:T(8,128)(2,1)S(1)}, u32[]{:S(2)}, u32[]{:S(2)}) collective-permute-start(bf16[8,128,128]{2,1,0:T(8,128)(2,1)S(1)} %pad_maximum_fusion), channel_id=1, source_target_pairs={{0,128},{64,192},{128,0},{192,64},{1,129},{65,193},{129,1},{193,65... | collective-permute-start | bytes 786440 | tf_op jit(solution)/shard_map/ppermute | solution.py:164
  22.0 2.8 %collective-permute-start.1 = (bf16[8,128,128]{2,1,0:T(8,128)(2,1)S(1)}, bf16[8,128,128]{2,1,0:T(8,128)(2,1)S(1)}, u32[]{:S(2)}, u32[]{:S(2)}) collective-permute-start(bf16[8,128,128]{2,1,0:T(8,128)(2,1)S(1)} %pad_maximum_fusion), channel_id=1, source_target_pairs={{0,64},{64,128},{128,192},{192,0},{1,65},{65,129},{129,193},{193,1... | collective-permute-start | bytes 786440 | tf_op jit(solution)/shard_map/ppermute | solution.py:164
  25.5 0.0 copy-start
  25.5 0.0 copy-start.3
  25.5 107.6 %conditional.1 = (bf16[128,128,128]{2,1,0:T(8,128)(2,1)}) conditional(s32[]{:T(128)} %bitcast.2, bf16[128,128,128]{2,1,0:T(8,128)(2,1)} %get-tuple-element.27, bf16[128,128,128]{2,1,0:T(8,128)(2,1)} %get-tuple-element.27, bf16[128,128,128]{2,1,0:T(8,128)(2,1)} %get-tuple-element.27, ...), branch_computations={%region_0.0_spmd, %region_1.0_spmd, %region_2.0_spmd, %region_3.0_... | conditional | bytes 19922954 | solution.py:212
  25.6 107.5 %all_to_all.29 = bf16[128,128,128]{2,1,0:T(8,128)(2,1)} all-to-all(bf16[128,128,128]{2,1,0:T(8,128)(2,1)} %param.3), channel_id=1, replica_groups=mesh['y_hi'=2,'x'=4,'core'=2,'z'=8,'y_lo'=4] {'z','y_lo'}, dimensions={0} | all-to-all | bytes 8388608 | tf_op jit(solution)/shard_map/cond/branch_3_fun/all_to_all | solution.py:169
  133.3 1.9 %collective-permute-start.4 = (bf16[32,128,128]{2,1,0:T(8,128)(2,1)S(1)}, bf16[32,128,128]{2,1,0:T(8,128)(2,1)S(1)}, u32[]{:S(2)}, u32[]{:S(2)}) collective-permute-start(bf16[32,128,128]{2,1,0:T(8,128)(2,1)S(1)} %constant_dynamic-update-slice_fusion.refs_7_), channel_id=1, source_target_pairs={{0,32},{32,0},{1,33},{33,1},{2,34},{34,2},{3,35},{35,3},{4,36},{36... | collective-permute-start | bytes 3145736 | tf_op jit(solution)/shard_map/ppermute | solution.py:160
  135.2 2.6 %collective-permute-done.4.refs_8_ = bf16[32,128,128]{2,1,0:T(8,128)(2,1)S(1)} collective-permute-done((bf16[32,128,128]{2,1,0:T(8,128)(2,1)S(1)}, bf16[32,128,128]{2,1,0:T(8,128)(2,1)S(1)}, u32[]{:S(2)}, u32[]{:S(2)}) %collective-permute-start.4) | collective-permute-done | bytes 1048608 | tf_op jit(solution)/shard_map/ppermute | solution.py:160
  137.9 16.2 %shard_map.83 = (bf16[32,128,128]{2,1,0:T(8,128)(2,1)S(1)}, bf16[32,128,128]{2,1,0:T(8,128)(2,1)S(1)}) custom-call(s32[512]{0:T(512)S(1)} %bitcast.9, s32[512]{0:T(512)S(1)} %copy-done.4, s32[512]{0:T(512)S(1)} %copy-done.5, s32[512]{0:T(512)S(1)} %copy-done.6, s32[32]{0:T(128)S(1)} %copy-done.8, s32[1]{0:T(128)} %get-tuple-element.25.refs_5_, ...), custom_call_target="tpu_custom_call" | custom-call | tf_op jit(solution)/shard_map/pallas_call | solution.py:218
  154.1 2.0 %collective-permute-start.5 = (bf16[32,128,128]{2,1,0:T(8,128)(2,1)S(1)}, bf16[32,128,128]{2,1,0:T(8,128)(2,1)S(1)}, u32[]{:S(2)}, u32[]{:S(2)}) collective-permute-start(bf16[32,128,128]{2,1,0:T(8,128)(2,1)S(1)} %get-tuple-element.35), channel_id=1, source_target_pairs={{0,32},{32,0},{1,33},{33,1},{2,34},{34,2},{3,35},{35,3},{4,36},{36... | collective-permute-start | bytes 3145736 | tf_op jit(solution)/shard_map/ppermute | solution.py:160
  156.1 2.5 %collective-permute-done.5 = bf16[32,128,128]{2,1,0:T(8,128)(2,1)S(1)} collective-permute-done((bf16[32,128,128]{2,1,0:T(8,128)(2,1)S(1)}, bf16[32,128,128]{2,1,0:T(8,128)(2,1)S(1)}, u32[]{:S(2)}, u32[]{:S(2)}) %collective-permute-start.5) | collective-permute-done | bytes 1048608 | tf_op jit(solution)/shard_map/ppermute | solution.py:160
  158.6 0.4 add_convert_fusion
  159.0 18.8 %all_to_all.30 = bf16[32,128,128]{2,1,0:T(8,128)(2,1)S(1)} all-to-all(bf16[32,128,128]{2,1,0:T(8,128)(2,1)S(1)} %add_convert_fusion), channel_id=1, replica_groups=mesh['y_hi'=2,'x'=4,'core'=2,'z'=8,'y_lo'=4] {'x'}, dimensions={0} | all-to-all | bytes 2097152 | tf_op jit(solution)/shard_map/all_to_all | solution.py:243
  177.8 0.2 reduce_sum.24
  178.0 10.2 %all_to_all.31 = bf16[8,128,128]{2,1,0:T(8,128)(2,1)S(1)} all-to-all(bf16[8,128,128]{2,1,0:T(8,128)(2,1)S(1)} %reduce_sum.24), channel_id=1, replica_groups=mesh['y_hi'=2,'x'=4,'core'=2,'z'=8,'y_lo'=4] {'y_hi'}, dimensions={0} | all-to-all | bytes 524288 | tf_op jit(solution)/shard_map/all_to_all | solution.py:243
  188.2 0.7 reduce_sum.25
  (20 shorter events, 0.2 us)
Async XLA Ops:
  0.0 13.7 %collective-permute-start = (bf16[4,128,128]{2,1,0:T(8,128)(2,1)}, bf16[4,128,128]{2,1,0:T(8,128)(2,1)S(1)}, u32[]{:S(2)}, u32[]{:S(2)}) collective-permute-start(bf16[4,128,128]{2,1,0:T(8,128)(2,1)} %bitcast.12), channel_id=1, source_target_pairs={{0,256},{256,0},{1,257},{257,1},{2,258},{258,2},{3,259},{259,3},{4... | collective-permute-start | bytes 393224 | tf_op jit(solution)/shard_map/ppermute | solution.py:160
  4.7 1.0 copy-start.1
  5.8 0.7 copy-start.2
  6.4 0.7 copy-start.7
  14.6 118.5 %collective-permute-start.3 = (bf16[8,128,128]{2,1,0:T(8,128)(2,1)S(1)}, bf16[8,128,128]{2,1,0:T(8,128)(2,1)S(1)}, u32[]{:S(2)}, u32[]{:S(2)}) collective-permute-start(bf16[8,128,128]{2,1,0:T(8,128)(2,1)S(1)} %pad_maximum_fusion), channel_id=1, source_target_pairs={{0,192},{64,0},{128,64},{192,128},{1,193},{65,1},{129,65},{193,129... | collective-permute-start | bytes 786440 | tf_op jit(solution)/shard_map/ppermute | solution.py:164
  19.3 113.8 %collective-permute-start.2 = (bf16[8,128,128]{2,1,0:T(8,128)(2,1)S(1)}, bf16[8,128,128]{2,1,0:T(8,128)(2,1)S(1)}, u32[]{:S(2)}, u32[]{:S(2)}) collective-permute-start(bf16[8,128,128]{2,1,0:T(8,128)(2,1)S(1)} %pad_maximum_fusion), channel_id=1, source_target_pairs={{0,128},{64,192},{128,0},{192,64},{1,129},{65,193},{129,1},{193,65... | collective-permute-start | bytes 786440 | tf_op jit(solution)/shard_map/ppermute | solution.py:164
  22.0 111.1 %collective-permute-start.1 = (bf16[8,128,128]{2,1,0:T(8,128)(2,1)S(1)}, bf16[8,128,128]{2,1,0:T(8,128)(2,1)S(1)}, u32[]{:S(2)}, u32[]{:S(2)}) collective-permute-start(bf16[8,128,128]{2,1,0:T(8,128)(2,1)S(1)} %pad_maximum_fusion), channel_id=1, source_target_pairs={{0,64},{64,128},{128,192},{192,0},{1,65},{65,129},{129,193},{193,1... | collective-permute-start | bytes 786440 | tf_op jit(solution)/shard_map/ppermute | solution.py:164
  25.5 112.4 %copy-start = (bf16[26,128,128]{2,1,0:T(8,128)(2,1)S(1)}, bf16[26,128,128]{2,1,0:T(8,128)(2,1)}, u32[]{:S(2)}) copy-start(bf16[26,128,128]{2,1,0:T(8,128)(2,1)} %refs_9_.1) | copy-start | bytes 2555908
  25.5 112.4 %copy-start.3 = (s32[512,1]{0,1:T(1,128)S(1)}, s32[512,1]{0,1:T(1,128)}, u32[]{:S(2)}) copy-start(s32[512,1]{0,1:T(1,128)} %param.18) | copy-start | bytes 6148
  25.5 112.4 %copy-start.4 = (s32[512]{0:T(512)S(1)}, s32[512]{0:T(512)}, u32[]{:S(2)}) copy-start(s32[512]{0:T(512)} %refs_1_.3) | copy-start | bytes 6148
  25.5 112.3 %copy-start.5 = (s32[512]{0:T(512)S(1)}, s32[512]{0:T(512)}, u32[]{:S(2)}) copy-start(s32[512]{0:T(512)} %refs_2_.1) | copy-start | bytes 6148
  25.5 112.3 %copy-start.6 = (s32[512]{0:T(512)S(1)}, s32[512]{0:T(512)}, u32[]{:S(2)}) copy-start(s32[512]{0:T(512)} %refs_3_.3) | copy-start | bytes 6148
  25.5 112.3 %copy-start.8 = (s32[32]{0:T(128)S(1)}, s32[32]{0:T(128)}, u32[]{:S(2)}) copy-start(s32[32]{0:T(128)} %refs_4_.1) | copy-start | bytes 388
  133.3 4.6 %collective-permute-start.4 = (bf16[32,128,128]{2,1,0:T(8,128)(2,1)S(1)}, bf16[32,128,128]{2,1,0:T(8,128)(2,1)S(1)}, u32[]{:S(2)}, u32[]{:S(2)}) collective-permute-start(bf16[32,128,128]{2,1,0:T(8,128)(2,1)S(1)} %constant_dynamic-update-slice_fusion.refs_7_), channel_id=1, source_target_pairs={{0,32},{32,0},{1,33},{33,1},{2,34},{34,2},{3,35},{35,3},{4,36},{36... | collective-permute-start | bytes 3145736 | tf_op jit(solution)/shard_map/ppermute | solution.py:160
  154.1 4.6 %collective-permute-start.5 = (bf16[32,128,128]{2,1,0:T(8,128)(2,1)S(1)}, bf16[32,128,128]{2,1,0:T(8,128)(2,1)S(1)}, u32[]{:S(2)}, u32[]{:S(2)}) collective-permute-start(bf16[32,128,128]{2,1,0:T(8,128)(2,1)S(1)} %get-tuple-element.35), channel_id=1, source_target_pairs={{0,32},{32,0},{1,33},{33,1},{2,34},{34,2},{3,35},{35,3},{4,36},{36... | collective-permute-start | bytes 3145736 | tf_op jit(solution)/shard_map/ppermute | solution.py:160

commit v4 on v3

v4 whole, which is shorter than its diff:
```python
import jax
import jax.numpy as jnp
from jax import lax
from jax.experimental import pallas as pl
from jax.experimental.pallas import tpu as pltpu
from jax.sharding import Mesh
from jax.sharding import PartitionSpec as P

GRP = ("y_hi", "x", "core")
ENV = ("z", "y_lo")
HALVES, XS, CORES = 2, 4, 2
DEEP, LOW = 8, 4
ROWS_DEV = 4
SLOTS = 4
UNROLL = 4
LANES = 128


def env_place():
    return lax.axis_index("z") * LOW + lax.axis_index("y_lo")


def pack_kernel(
    per,
    sector,
    column,
    sector_rows,
    tiles,
    out_1,
    out_2,
    out_3,
    out_4,
    need,
    picked,
    heads,
    nexts,
    counts,
    started,
    copies,
):
    place = env_place()
    columns = column.shape[0]
    sectors = heads.shape[0]

    rows = sector_rows[...]
    lane = lax.broadcasted_iota(jnp.int32, rows.shape, 1) % per
    rank = jnp.ones(rows.shape, jnp.int32)
    for step in range(1, per):
        same = (pltpu.roll(rows, step, 1) == rows) & (lane >= step)
        rank = rank + same.astype(jnp.int32)
    wanted = rows == column[0]
    for c in range(1, columns):
        wanted = wanted | (rows == column[c])
    slots = jnp.maximum(jnp.max(jnp.where(wanted, rank, 0)), 1)
    need[0] = slots

    def clear(s, carry):
        heads[s] = -1
        counts[s] = 0
        return carry

    lax.fori_loop(0, sectors, clear, 0, unroll=8)

    def chain(c, carry):
        s = column[c]
        nexts[c] = heads[s]
        heads[s] = c
        return carry

    lax.fori_loop(0, columns, chain, 0, unroll=8)

    outs = (out_1, out_2, out_3, out_4)

    def move(i, out, slot, place):
        return pltpu.make_async_copy(tiles.at[i], out.at[place], copies.at[slot])

    def tile(i, n):
        s = sector[place * per + i]
        k = counts[s]
        counts[s] = k + 1

        def send(state):
            c, n = state
            slot = c * slots + k
            for size in range(1, SLOTS + 1):

                @pl.when(slots == size)
                def _(size=size):
                    move(i, outs[size - 1], slot, slot).start()

            started[n] = slot
            return nexts[c], n + 1

        return lax.while_loop(lambda state: state[0] >= 0, send, (heads[s], n))[1]

    sent = lax.fori_loop(0, per, tile, jnp.int32(0))

    mine = column[place]

    def scan(b, n):
        k = b * slots
        for i in range(per):
            t = b * per + i
            match = (sector[t] == mine).astype(jnp.int32)
            picked[n] = t * LANES + k
            n = n + match
            k = k + match
        return n

    n = lax.fori_loop(0, sector.shape[0] // per, scan, jnp.int32(1))
    for j in range(UNROLL):
        picked[n + j] = -1
    picked[0] = n - 1

    def finish(j, carry):
        move(0, out_1, started[j], 0).wait()
        return carry

    lax.fori_loop(0, sent, finish, 0)


def apply_kernel(
    source,
    target,
    index,
    picked,
    tiles,
    part_0,
    part_1,
    part_2,
    part_3,
    rights,
    out_stay,
    out_cross,
    out_other_stay,
    out_other_cross,
    held,
    acc,
    blocks,
    copied,
):
    load = pltpu.make_async_copy(tiles, held, copied)
    load.start()
    half_at, x_at, core_at = (lax.axis_index(a) for a in GRP)
    quarter = out_stay.shape[0]
    count = 4 * quarter

    def read_place(row):
        group = row // ROWS_DEV
        core = (group % CORES) ^ core_at
        x = (x_at - (group // CORES) % XS + XS) % XS
        y = group // (CORES * XS) ^ half_at
        return ((x * CORES + core) * HALVES + y) * ROWS_DEV + row % ROWS_DEV

    def write_place(row):
        group = row // ROWS_DEV
        core = (group % CORES) ^ core_at
        x = (group // CORES) % XS
        y = group // (CORES * XS) ^ half_at
        return ((core * HALVES + y) * XS + x) * ROWS_DEV + row % ROWS_DEV

    parts = (part_0, part_1, part_2, part_3)
    part = part_0.shape[0]

    def fill(r, carry):
        for x in range(XS):
            blocks[x * part + r] = parts[x][r]
            acc[x * part + r] = jnp.zeros(acc.shape[1:], acc.dtype)
        return carry

    lax.fori_loop(0, part, fill, 0)
    load.wait()

    def terms(j, carry):
        for u in range(UNROLL):
            entry = picked[1 + j * UNROLL + u]
            kept = jnp.maximum(entry, 0)
            t = kept // LANES
            slot = kept % LANES
            row = jnp.where(entry < 0, count, write_place(target[t]))
            product = jnp.dot(
                held[slot],
                blocks[read_place(source[t])],
                preferred_element_type=jnp.float32,
            ).astype(jnp.bfloat16)
            acc[row] += jnp.dot(
                product, rights[index[t]], preferred_element_type=jnp.float32
            )
        return carry

    lax.fori_loop(0, (picked[0] + UNROLL - 1) // UNROLL, terms, 0)

    def finish(r, carry):
        for place, out in enumerate(
            (out_stay, out_cross, out_other_stay, out_other_cross)
        ):
            out[r] = acc[place * quarter + r].astype(out.dtype)
        return carry

    lax.fori_loop(0, quarter, finish, 0)


def place_kernel(got, out, copied):
    move = pltpu.make_async_copy(got, out.at[pl.ds(0, got.shape[0])], copied)
    move.start()
    move.wait()


def swap(value, axis):
    return lax.ppermute(value, axis, [(0, 1), (1, 0)])


def sum_x(own, got):
    total = own.astype(jnp.float32) + got.astype(jnp.float32)
    parts = lax.all_to_all(total.astype(jnp.bfloat16), "x", 0, 0, tiled=True)
    parts = parts.reshape((XS, -1) + parts.shape[1:])
    return jnp.sum(parts.astype(jnp.float32), axis=0)


def step_x(value, step):
    return lax.ppermute(value, "x", [(i, (i + step) % XS) for i in range(XS)])


def exchange(slots, packing):
    def run(*packed):
        got = lax.all_to_all(packed[slots - 1], ENV, 0, 0, tiled=True)
        if slots == SLOTS:
            return got
        return pl.pallas_call(
            place_kernel,
            out_shape=packing,
            in_specs=[pl.BlockSpec(memory_space=pltpu.VMEM)],
            out_specs=pl.BlockSpec(memory_space=pl.ANY),
            scratch_shapes=[pltpu.SemaphoreType.DMA],
        )(got)

    return run


def shards(
    wavefunction,
    left_tiles,
    right_tiles,
    term_source,
    term_target,
    right_index,
    term_sector,
    column_sector,
):
    per, size, _ = left_tiles.shape
    columns = column_sector.shape[0]
    smem = pl.BlockSpec(memory_space=pltpu.SMEM)
    vmem = pl.BlockSpec(memory_space=pltpu.VMEM)
    anywhere = pl.BlockSpec(memory_space=pl.ANY)
    sectors = term_sector[:, 0]
    slots = columns * SLOTS
    packing = jax.ShapeDtypeStruct((slots, size, size), jnp.bfloat16)

    psi = wavefunction.reshape(-1, size, size)
    pair = jnp.concatenate([psi, swap(psi, "y_hi")])
    *packed, need, picked = pl.pallas_call(
        lambda *refs: pack_kernel(per, *refs),
        out_shape=(
            *[
                jax.ShapeDtypeStruct((columns * (k + 1), size, size), jnp.bfloat16)
                for k in range(SLOTS)
            ],
            jax.ShapeDtypeStruct((1,), jnp.int32),
            jax.ShapeDtypeStruct((sectors.shape[0] + 1 + UNROLL,), jnp.int32),
        ),
        in_specs=[smem, smem, vmem, vmem],
        out_specs=(*[anywhere] * SLOTS, smem, smem),
        scratch_shapes=[pltpu.SMEM((columns,), jnp.int32)] * 3
        + [pltpu.SMEM((slots,), jnp.int32), pltpu.SemaphoreType.DMA((slots,))],
        cost_estimate=pl.CostEstimate(
            flops=0, bytes_accessed=8 * 2**20, transcendentals=0
        ),
    )(sectors, column_sector, sectors.reshape(-1, LANES), left_tiles)
    packed, pair = lax.optimization_barrier((packed, pair))
    quad = jnp.concatenate([pair, swap(pair, "core")])
    parts = [quad] + [step_x(quad, step) for step in range(1, XS)]
    tiles = lax.switch(
        need[0] - 1, [exchange(k + 1, packing) for k in range(SLOTS)], *packed
    )
    tiles, parts = lax.optimization_barrier((tiles, parts))
    quarter = quad.shape[0]
    block = jax.ShapeDtypeStruct(quad.shape, jnp.bfloat16)
    stay, cross, other_stay, other_cross = pl.pallas_call(
        apply_kernel,
        out_shape=[block] * 4,
        in_specs=[smem] * 4 + [anywhere] + [vmem] * 5,
        out_specs=[vmem] * 4,
        scratch_shapes=[
            pltpu.VMEM(packing.shape, jnp.bfloat16),
            pltpu.VMEM((4 * quarter + 1, size, size), jnp.float32),
            pltpu.VMEM((4 * quarter, size, size), jnp.bfloat16),
            pltpu.SemaphoreType.DMA,
        ],
        compiler_params=pltpu.CompilerParams(vmem_limit_bytes=40 * 2**20),
    )(
        term_source,
        term_target,
        right_index,
        picked,
        tiles,
        *parts,
        right_tiles,
    )
    cross = sum_x(cross, swap(other_cross, "core"))
    crossed = swap(cross.astype(jnp.bfloat16), "y_hi")
    stay = sum_x(stay, swap(other_stay, "core"))
    total = stay + crossed.astype(jnp.float32)
    return total.astype(jnp.bfloat16).reshape(wavefunction.shape)


def solution(mesh):
    physical = Mesh(mesh.devices.reshape(HALVES, XS, CORES, DEEP, LOW), GRP + ENV)
    placed = (
        P(GRP, ENV),
        P(GRP + ENV, None, None),
        P(None, ENV, None),
        P(GRP),
        P(GRP),
        P(GRP),
        P(GRP, None),
        P(),
    )
    return jax.shard_map(
        shards, mesh=physical, in_specs=placed, out_specs=P(GRP, ENV), check_vma=False
    )
```

time: 193 us -> 183 us (0.948)
  blocking collectives: 136 us -> 109 us
  starting transfers between devices: 18.8 us -> 32.6 us
  waiting for transfers between devices: 8.02 us -> 20.9 us
  Pallas kernels: 19.9 us -> 12.5 us
  local copies, waits for them, and re-layouts: 2.54 us -> 0.09 us
    all_to_all x3 -> x1, blocking collectives: 136 us -> 109 us  [run(): got = lax.all_to_all(packed[slots - 1], ENV, 0, 0, tiled=True)]
    all_to_all x0 -> x2, waiting for transfers between devices: none -> 13.2 us  [sum_x(): parts = lax.all_to_all(total.astype(jnp.bfloat16), 'x', 0, 0, tiled=True)]
    pallas_call x2, Pallas kernels: 19.9 us -> 12.5 us  [the longest x1 7.15 us: shards(): pl.pallas_call(apply_kernel, out_shape=[block] * 4, in_specs=[smem] * 4 +...]
    all_to_all x0 -> x2, starting transfers between devices: none -> 7.09 us  [sum_x(): parts = lax.all_to_all(total.astype(jnp.bfloat16), 'x', 0, 0, tiled=True)]
    ppermute x3 -> x5, starting transfers between devices: 8.66 us -> 15.4 us  [swap(): return lax.ppermute(value, axis, [(0, 1), (1, 0)])]
    unnamed x21 -> x11, local copies, waits for them, and re-layouts: 2.5 us -> 0.05 us
    convert_element_type x1 -> x3, other arithmetic: 0.37 us -> 2.57 us  [the longest x2 1.88 us: sum_x(): parts = lax.all_to_all(total.astype(jnp.bfloat16), 'x', 0, 0, tiled=True)]
    ppermute x3 -> x5, waiting for transfers between devices: 8.01 us -> 7.73 us  [swap(): return lax.ppermute(value, axis, [(0, 1), (1, 0)])]
  transfers between devices with their start and end apart: 6 -> 10, of which waited for: 3 -> 5; matrix products, arithmetic and copies ran while one was open for 0% -> 1% of each run, Pallas kernels for 2% -> 3%
where the time goes in v4:
time: 183 us; the launch traced here: 180 us
  blocking collectives  109 us (60%)
  starting transfers between devices  32.6 us (18%)
  waiting for transfers between devices  20.9 us (11%)
  Pallas kernels  12.5 us (7%)
  other arithmetic  3.66 us (2%)
    all_to_all x1, blocking collectives, run(): got = lax.all_to_all(packed[slots - 1], ENV, 0, 0, tiled=True)  109 us
    ppermute x5, starting transfers between devices, swap(): return lax.ppermute(value, axis, [(0, 1), (1, 0)])  15.4 us
    all_to_all x2, waiting for transfers between devices, sum_x(): parts = lax.all_to_all(total.astype(jnp.bfloat16), 'x', 0, 0, tiled=True)  13.2 us
    ppermute x3, starting transfers between devices, step_x(): return lax.ppermute(value, 'x', [(i, (i + step) % XS) for i in range(XS)])  10.2 us
    ppermute x5, waiting for transfers between devices, swap(): return lax.ppermute(value, axis, [(0, 1), (1, 0)])  7.73 us
    pallas_call x1, Pallas kernels, shards(): pl.pallas_call(apply_kernel, out_shape=[block] * 4, in_specs=[smem] * 4 +...  7.15 us
    all_to_all x2, starting transfers between devices, sum_x(): parts = lax.all_to_all(total.astype(jnp.bfloat16), 'x', 0, 0, tiled=True)  7.09 us
    pallas_call x1, Pallas kernels, shards(): pl.pallas_call(lambda *refs: pack_kernel(per, *refs), out_shape=(*[jax.Sh...  5.37 us
  transfers between devices with their start and end apart: 10, of which 5 were waited for; matrix products, arithmetic and copies ran while one was open for 1% of the time, Pallas kernels for 3%

profile of v4, /device:TPU:56, one launch (start us, length us, event | category | flops | bytes accessed | tf_op | source)
XLA Modules:
  0.0 179.9 jit_solution(12813368525232552625)
XLA Ops:
  0.0 4.7 %collective-permute-start = (bf16[4,128,128]{2,1,0:T(8,128)(2,1)}, bf16[4,128,128]{2,1,0:T(8,128)(2,1)S(1)}, u32[]{:S(2)}, u32[]{:S(2)}) collective-permute-start(bf16[4,128,128]{2,1,0:T(8,128)(2,1)} %bitcast.10), channel_id=1, source_target_pairs={{0,256},{256,0},{1,257},{257,1},{2,258},{258,2},{3,259},{259,3},{4... | collective-permute-start | bytes 393224 | tf_op jit(solution)/shard_map/ppermute | solution.py:210
  4.7 5.4 %shard_map.82 = (bf16[32,128,128]{2,1,0:T(8,128)(2,1)}, bf16[64,128,128]{2,1,0:T(8,128)(2,1)}, bf16[96,128,128]{2,1,0:T(8,128)(2,1)}, bf16[128,128,128]{2,1,0:T(8,128)(2,1)}, s32[1]{0:T(128)}, /*index=5*/s32[517]{0:T(1024)}) custom-call(s32[512]{0:T(512)} %bitcast.12, s32[32]{0:T(128)} %refs_1_.1, s32[4,128]{1,0:T(4,128)} %bitcast.13, ...), custom_call_target="tpu_custom_call" | custom-call | bytes 8388608 | tf_op jit(solution)/shard_map/pallas_call | solution.py:261
  10.1 3.6 %collective-permute-done = bf16[4,128,128]{2,1,0:T(8,128)(2,1)S(1)} collective-permute-done((bf16[4,128,128]{2,1,0:T(8,128)(2,1)}, bf16[4,128,128]{2,1,0:T(8,128)(2,1)S(1)}, u32[]{:S(2)}, u32[]{:S(2)}) %collective-permute-start) | collective-permute-done | bytes 131104 | tf_op jit(solution)/shard_map/ppermute | solution.py:210
  13.7 0.9 pad_maximum_fusion
  14.6 1.9 %collective-permute-start.1 = (bf16[8,128,128]{2,1,0:T(8,128)(2,1)S(1)}, bf16[8,128,128]{2,1,0:T(8,128)(2,1)S(1)}, u32[]{:S(2)}, u32[]{:S(2)}) collective-permute-start(bf16[8,128,128]{2,1,0:T(8,128)(2,1)S(1)} %pad_maximum_fusion), channel_id=1, source_target_pairs={{0,32},{32,0},{1,33},{33,1},{2,34},{34,2},{3,35},{35,3},{4,36},{36... | collective-permute-start | bytes 786440 | tf_op jit(solution)/shard_map/ppermute | solution.py:210
  16.6 1.5 collective-permute-done.1
  18.1 4.7 %collective-permute-start.4 = (bf16[16,128,128]{2,1,0:T(8,128)(2,1)S(1)}, bf16[16,128,128]{2,1,0:T(8,128)(2,1)S(1)}, u32[]{:S(2)}, u32[]{:S(2)}) collective-permute-start(bf16[16,128,128]{2,1,0:T(8,128)(2,1)S(1)} %constant_dynamic-update-slice_fusion.part_0), channel_id=1, source_target_pairs={{0,192},{64,0},{128,64},{192,128},{1,193},{65,1},{129,65},{193,129... | collective-permute-start | bytes 1572872 | tf_op jit(solution)/shard_map/ppermute | solution.py:221
  22.8 2.7 %collective-permute-start.3 = (bf16[16,128,128]{2,1,0:T(8,128)(2,1)S(1)}, bf16[16,128,128]{2,1,0:T(8,128)(2,1)S(1)}, u32[]{:S(2)}, u32[]{:S(2)}) collective-permute-start(bf16[16,128,128]{2,1,0:T(8,128)(2,1)S(1)} %constant_dynamic-update-slice_fusion.part_0), channel_id=1, source_target_pairs={{0,128},{64,192},{128,0},{192,64},{1,129},{65,193},{129,1},{193,65... | collective-permute-start | bytes 1572872 | tf_op jit(solution)/shard_map/ppermute | solution.py:221
  25.5 2.8 %collective-permute-start.2 = (bf16[16,128,128]{2,1,0:T(8,128)(2,1)S(1)}, bf16[16,128,128]{2,1,0:T(8,128)(2,1)S(1)}, u32[]{:S(2)}, u32[]{:S(2)}) collective-permute-start(bf16[16,128,128]{2,1,0:T(8,128)(2,1)S(1)} %constant_dynamic-update-slice_fusion.part_0), channel_id=1, source_target_pairs={{0,64},{64,128},{128,192},{192,0},{1,65},{65,129},{129,193},{193,1... | collective-permute-start | bytes 1572872 | tf_op jit(solution)/shard_map/ppermute | solution.py:221
  29.0 109.3 %conditional.1 = (bf16[128,128,128]{2,1,0:T(8,128)(2,1)}) conditional(s32[]{:T(128)} %bitcast.2, bf16[32,128,128]{2,1,0:T(8,128)(2,1)} %get-tuple-element.40, bf16[64,128,128]{2,1,0:T(8,128)(2,1)} %get-tuple-element.41, bf16[96,128,128]{2,1,0:T(8,128)(2,1)} %get-tuple-element.42, ...), branch_computations={%region_0.0_spmd, %region_1.0_spmd, %region_2.0_spmd, %region_3.0_... | conditional | bytes 8388616 | solution.py:282
  29.1 109.2 %all_to_all.29 = bf16[128,128,128]{2,1,0:T(8,128)(2,1)} all-to-all(bf16[128,128,128]{2,1,0:T(8,128)(2,1)} %param.3), channel_id=1, replica_groups=mesh['y_hi'=2,'x'=4,'core'=2,'z'=8,'y_lo'=4] {'z','y_lo'}, dimensions={0} | all-to-all | bytes 8388608 | tf_op jit(solution)/shard_map/cond/branch_3_fun/all_to_all | solution.py:226
  138.4 7.2 %shard_map.83 = (bf16[16,128,128]{2,1,0:T(8,128)(2,1)S(1)}, bf16[16,128,128]{2,1,0:T(8,128)(2,1)S(1)}, bf16[16,128,128]{2,1,0:T(8,128)(2,1)}, bf16[16,128,128]{2,1,0:T(8,128)(2,1)S(1)}) custom-call(s32[512]{0:T(512)S(1)} %copy-done.2, s32[512]{0:T(512)S(1)} %copy-done.3, s32[512]{0:T(512)S(1)} %copy-done.4, s32[517]{0:T(1024)S(1)} %copy-done.1, ...), custom_call_target="tpu_custom_call" | custom-call | tf_op jit(solution)/shard_map/pallas_call | solution.py:288
  145.5 1.9 %collective-permute-start.6 = (bf16[16,128,128]{2,1,0:T(8,128)(2,1)S(1)}, bf16[16,128,128]{2,1,0:T(8,128)(2,1)S(1)}, u32[]{:S(2)}, u32[]{:S(2)}) collective-permute-start(bf16[16,128,128]{2,1,0:T(8,128)(2,1)S(1)} %get-tuple-element.53), channel_id=1, source_target_pairs={{0,32},{32,0},{1,33},{33,1},{2,34},{34,2},{3,35},{35,3},{4,36},{36... | collective-permute-start | bytes 1572872 | tf_op jit(solution)/shard_map/ppermute | solution.py:210
  147.4 2.4 %collective-permute-start.5 = (bf16[16,128,128]{2,1,0:T(8,128)(2,1)}, bf16[16,128,128]{2,1,0:T(8,128)(2,1)S(1)}, u32[]{:S(2)}, u32[]{:S(2)}) collective-permute-start(bf16[16,128,128]{2,1,0:T(8,128)(2,1)} %get-tuple-element.51), channel_id=1, source_target_pairs={{0,32},{32,0},{1,33},{33,1},{2,34},{34,2},{3,35},{35,3},{4,36},{36... | collective-permute-start | bytes 1572872 | tf_op jit(solution)/shard_map/ppermute | solution.py:210
  149.9 0.9 add_convert_fusion
  150.8 3.6 %all-to-all-start.5 = ((bf16[16,128,128]{2,1,0:T(8,128)(2,1)}), bf16[16,128,128]{2,1,0:T(8,128)(2,1)S(1)}, u32[]{:S(2)}, u32[]{:S(2)}) async-start(bf16[16,128,128]{2,1,0:T(8,128)(2,1)} %add_convert_fusion), calls=%async_computation.5 | async-start | bytes 1048576 | tf_op jit(solution)/shard_map/all_to_all | solution.py:215
  154.4 0.9 add_convert_fusion.1
  155.4 8.8 %all-to-all-done.5 = bf16[16,128,128]{2,1,0:T(8,128)(2,1)S(1)} async-done(((bf16[16,128,128]{2,1,0:T(8,128)(2,1)}), bf16[16,128,128]{2,1,0:T(8,128)(2,1)S(1)}, u32[]{:S(2)}, u32[]{:S(2)}) %all-to-all-start.5) | async-done | bytes 524320 | tf_op jit(solution)/shard_map/all_to_all | solution.py:215
  164.2 3.5 %all-to-all-start.4 = ((bf16[16,128,128]{2,1,0:T(8,128)(2,1)}), bf16[16,128,128]{2,1,0:T(8,128)(2,1)S(1)}, u32[]{:S(2)}, u32[]{:S(2)}) async-start(bf16[16,128,128]{2,1,0:T(8,128)(2,1)} %add_convert_fusion.1), calls=%async_computation.4 | async-start | bytes 1048576 | tf_op jit(solution)/shard_map/all_to_all | solution.py:215
  167.7 0.1 reduce_sum.22
  167.8 4.4 %collective-permute-start.7 = (bf16[4,128,128]{2,1,0:T(8,128)(2,1)S(1)}, bf16[4,128,128]{2,1,0:T(8,128)(2,1)S(1)}, u32[]{:S(2)}, u32[]{:S(2)}) collective-permute-start(bf16[4,128,128]{2,1,0:T(8,128)(2,1)S(1)} %reduce_sum.22), channel_id=1, source_target_pairs={{0,256},{256,0},{1,257},{257,1},{2,258},{258,2},{3,259},{259,3},{4... | collective-permute-start | bytes 393224 | tf_op jit(solution)/shard_map/ppermute | solution.py:210
  172.2 4.3 %all-to-all-done.4 = bf16[16,128,128]{2,1,0:T(8,128)(2,1)S(1)} async-done(((bf16[16,128,128]{2,1,0:T(8,128)(2,1)}), bf16[16,128,128]{2,1,0:T(8,128)(2,1)S(1)}, u32[]{:S(2)}, u32[]{:S(2)}) %all-to-all-start.4) | async-done | bytes 524320 | tf_op jit(solution)/shard_map/all_to_all | solution.py:215
  176.6 2.6 %collective-permute-done.7 = bf16[4,128,128]{2,1,0:T(8,128)(2,1)S(1)} collective-permute-done((bf16[4,128,128]{2,1,0:T(8,128)(2,1)S(1)}, bf16[4,128,128]{2,1,0:T(8,128)(2,1)S(1)}, u32[]{:S(2)}, u32[]{:S(2)}) %collective-permute-start.7) | collective-permute-done | bytes 131104 | tf_op jit(solution)/shard_map/ppermute | solution.py:210
  179.2 0.7 add_convert_fusion.2
  (18 shorter events, 0.2 us)
Async XLA Ops:
  0.0 13.7 %collective-permute-start = (bf16[4,128,128]{2,1,0:T(8,128)(2,1)}, bf16[4,128,128]{2,1,0:T(8,128)(2,1)S(1)}, u32[]{:S(2)}, u32[]{:S(2)}) collective-permute-start(bf16[4,128,128]{2,1,0:T(8,128)(2,1)} %bitcast.10), channel_id=1, source_target_pairs={{0,256},{256,0},{1,257},{257,1},{2,258},{258,2},{3,259},{259,3},{4... | collective-permute-start | bytes 393224 | tf_op jit(solution)/shard_map/ppermute | solution.py:210
  14.6 3.4 %collective-permute-start.1 = (bf16[8,128,128]{2,1,0:T(8,128)(2,1)S(1)}, bf16[8,128,128]{2,1,0:T(8,128)(2,1)S(1)}, u32[]{:S(2)}, u32[]{:S(2)}) collective-permute-start(bf16[8,128,128]{2,1,0:T(8,128)(2,1)S(1)} %pad_maximum_fusion), channel_id=1, source_target_pairs={{0,32},{32,0},{1,33},{33,1},{2,34},{34,2},{3,35},{35,3},{4,36},{36... | collective-permute-start | bytes 786440 | tf_op jit(solution)/shard_map/ppermute | solution.py:210
  18.1 120.2 %collective-permute-start.4 = (bf16[16,128,128]{2,1,0:T(8,128)(2,1)S(1)}, bf16[16,128,128]{2,1,0:T(8,128)(2,1)S(1)}, u32[]{:S(2)}, u32[]{:S(2)}) collective-permute-start(bf16[16,128,128]{2,1,0:T(8,128)(2,1)S(1)} %constant_dynamic-update-slice_fusion.part_0), channel_id=1, source_target_pairs={{0,192},{64,0},{128,64},{192,128},{1,193},{65,1},{129,65},{193,129... | collective-permute-start | bytes 1572872 | tf_op jit(solution)/shard_map/ppermute | solution.py:221
  22.8 115.5 %collective-permute-start.3 = (bf16[16,128,128]{2,1,0:T(8,128)(2,1)S(1)}, bf16[16,128,128]{2,1,0:T(8,128)(2,1)S(1)}, u32[]{:S(2)}, u32[]{:S(2)}) collective-permute-start(bf16[16,128,128]{2,1,0:T(8,128)(2,1)S(1)} %constant_dynamic-update-slice_fusion.part_0), channel_id=1, source_target_pairs={{0,128},{64,192},{128,0},{192,64},{1,129},{65,193},{129,1},{193,65... | collective-permute-start | bytes 1572872 | tf_op jit(solution)/shard_map/ppermute | solution.py:221
  25.5 112.8 %collective-permute-start.2 = (bf16[16,128,128]{2,1,0:T(8,128)(2,1)S(1)}, bf16[16,128,128]{2,1,0:T(8,128)(2,1)S(1)}, u32[]{:S(2)}, u32[]{:S(2)}) collective-permute-start(bf16[16,128,128]{2,1,0:T(8,128)(2,1)S(1)} %constant_dynamic-update-slice_fusion.part_0), channel_id=1, source_target_pairs={{0,64},{64,128},{128,192},{192,0},{1,65},{65,129},{129,193},{193,1... | collective-permute-start | bytes 1572872 | tf_op jit(solution)/shard_map/ppermute | solution.py:221
  29.0 109.3 %copy-start = (bf16[26,128,128]{2,1,0:T(8,128)(2,1)S(1)}, bf16[26,128,128]{2,1,0:T(8,128)(2,1)}, u32[]{:S(2)}) copy-start(bf16[26,128,128]{2,1,0:T(8,128)(2,1)} %rights.1) | copy-start | bytes 2555908
  29.0 109.3 %copy-start.1 = (s32[517]{0:T(1024)S(1)}, s32[517]{0:T(1024)}, u32[]{:S(2)}) copy-start(s32[517]{0:T(1024)} %get-tuple-element.34.picked) | copy-start | bytes 6208
  29.0 109.3 %copy-start.2 = (s32[512]{0:T(512)S(1)}, s32[512]{0:T(512)}, u32[]{:S(2)}) copy-start(s32[512]{0:T(512)} %source.1) | copy-start | bytes 6148
  29.0 109.3 %copy-start.3 = (s32[512]{0:T(512)S(1)}, s32[512]{0:T(512)}, u32[]{:S(2)}) copy-start(s32[512]{0:T(512)} %target.1) | copy-start | bytes 6148
  29.0 109.3 %copy-start.4 = (s32[512]{0:T(512)S(1)}, s32[512]{0:T(512)}, u32[]{:S(2)}) copy-start(s32[512]{0:T(512)} %index.1) | copy-start | bytes 6148
  145.5 4.3 %collective-permute-start.6 = (bf16[16,128,128]{2,1,0:T(8,128)(2,1)S(1)}, bf16[16,128,128]{2,1,0:T(8,128)(2,1)S(1)}, u32[]{:S(2)}, u32[]{:S(2)}) collective-permute-start(bf16[16,128,128]{2,1,0:T(8,128)(2,1)S(1)} %get-tuple-element.53), channel_id=1, source_target_pairs={{0,32},{32,0},{1,33},{33,1},{2,34},{34,2},{3,35},{35,3},{4,36},{36... | collective-permute-start | bytes 1572872 | tf_op jit(solution)/shard_map/ppermute | solution.py:210
  147.4 7.0 %collective-permute-start.5 = (bf16[16,128,128]{2,1,0:T(8,128)(2,1)}, bf16[16,128,128]{2,1,0:T(8,128)(2,1)S(1)}, u32[]{:S(2)}, u32[]{:S(2)}) collective-permute-start(bf16[16,128,128]{2,1,0:T(8,128)(2,1)} %get-tuple-element.51), channel_id=1, source_target_pairs={{0,32},{32,0},{1,33},{33,1},{2,34},{34,2},{3,35},{35,3},{4,36},{36... | collective-permute-start | bytes 1572872 | tf_op jit(solution)/shard_map/ppermute | solution.py:210
  150.8 13.4 %all-to-all-start.5 = ((bf16[16,128,128]{2,1,0:T(8,128)(2,1)}), bf16[16,128,128]{2,1,0:T(8,128)(2,1)S(1)}, u32[]{:S(2)}, u32[]{:S(2)}) async-start(bf16[16,128,128]{2,1,0:T(8,128)(2,1)} %add_convert_fusion), calls=%async_computation.5 | async-start | bytes 1048576 | tf_op jit(solution)/shard_map/all_to_all | solution.py:215
  164.2 12.3 %all-to-all-start.4 = ((bf16[16,128,128]{2,1,0:T(8,128)(2,1)}), bf16[16,128,128]{2,1,0:T(8,128)(2,1)S(1)}, u32[]{:S(2)}, u32[]{:S(2)}) async-start(bf16[16,128,128]{2,1,0:T(8,128)(2,1)} %add_convert_fusion.1), calls=%async_computation.4 | async-start | bytes 1048576 | tf_op jit(solution)/shard_map/all_to_all | solution.py:215
  167.8 11.5 %collective-permute-start.7 = (bf16[4,128,128]{2,1,0:T(8,128)(2,1)S(1)}, bf16[4,128,128]{2,1,0:T(8,128)(2,1)S(1)}, u32[]{:S(2)}, u32[]{:S(2)}) collective-permute-start(bf16[4,128,128]{2,1,0:T(8,128)(2,1)S(1)} %reduce_sum.22), channel_id=1, source_target_pairs={{0,256},{256,0},{1,257},{257,1},{2,258},{258,2},{3,259},{259,3},{4... | collective-permute-start | bytes 393224 | tf_op jit(solution)/shard_map/ppermute | solution.py:210

commit v5 on v4

--- a/solution.py
+++ b/solution.py
@@ -139,8 +139,12 @@
     blocks,
     copied,
 ):
-    load = pltpu.make_async_copy(tiles, held, copied)
-    load.start()
+    loads = [pltpu.make_async_copy(tiles, held, copied.at[XS])]
+    for x, part in enumerate((part_0, part_1, part_2, part_3)):
+        at = blocks.at[pl.ds(x * part.shape[0], part.shape[0])]
+        loads.append(pltpu.make_async_copy(part, at, copied.at[x]))
+    for load in loads:
+        load.start()
     half_at, x_at, core_at = (lax.axis_index(a) for a in GRP)
     quarter = out_stay.shape[0]
     count = 4 * quarter
@@ -155,21 +159,18 @@
     def write_place(row):
         group = row // ROWS_DEV
         core = (group % CORES) ^ core_at
+        y = group // (CORES * XS) ^ half_at
         x = (group // CORES) % XS
-        y = group // (CORES * XS) ^ half_at
+        x = jnp.where(y == 0, (x - x_at + XS) % XS, x)
         return ((core * HALVES + y) * XS + x) * ROWS_DEV + row % ROWS_DEV
 
-    parts = (part_0, part_1, part_2, part_3)
-    part = part_0.shape[0]
-
-    def fill(r, carry):
-        for x in range(XS):
-            blocks[x * part + r] = parts[x][r]
-            acc[x * part + r] = jnp.zeros(acc.shape[1:], acc.dtype)
-        return carry
-
-    lax.fori_loop(0, part, fill, 0)
-    load.wait()
+    def clear(r, carry):
+        acc[r] = jnp.zeros(acc.shape[1:], acc.dtype)
+        return carry
+
+    lax.fori_loop(0, count, clear, 0, unroll=4)
+    for load in loads:
+        load.wait()
 
     def terms(j, carry):
         for u in range(UNROLL):
@@ -210,11 +211,9 @@
     return lax.ppermute(value, axis, [(0, 1), (1, 0)])
 
 
-def sum_x(own, got):
-    total = own.astype(jnp.float32) + got.astype(jnp.float32)
-    parts = lax.all_to_all(total.astype(jnp.bfloat16), "x", 0, 0, tiled=True)
-    parts = parts.reshape((XS, -1) + parts.shape[1:])
-    return jnp.sum(parts.astype(jnp.float32), axis=0)
+def add(left, right):
+    total = left.astype(jnp.float32) + right.astype(jnp.float32)
+    return total.astype(jnp.bfloat16)
 
 
 def step_x(value, step):
@@ -257,7 +256,8 @@
     packing = jax.ShapeDtypeStruct((slots, size, size), jnp.bfloat16)
 
     psi = wavefunction.reshape(-1, size, size)
-    pair = jnp.concatenate([psi, swap(psi, "y_hi")])
+    across = swap(psi, "y_hi")
+    beside = swap(psi, "core")
     *packed, need, picked = pl.pallas_call(
         lambda *refs: pack_kernel(per, *refs),
         out_shape=(
@@ -276,8 +276,8 @@
             flops=0, bytes_accessed=8 * 2**20, transcendentals=0
         ),
     )(sectors, column_sector, sectors.reshape(-1, LANES), left_tiles)
-    packed, pair = lax.optimization_barrier((packed, pair))
-    quad = jnp.concatenate([pair, swap(pair, "core")])
+    packed, across = lax.optimization_barrier((packed, across))
+    quad = jnp.concatenate([psi, across, beside, swap(across, "core")])
     parts = [quad] + [step_x(quad, step) for step in range(1, XS)]
     tiles = lax.switch(
         need[0] - 1, [exchange(k + 1, packing) for k in range(SLOTS)], *packed
@@ -288,13 +288,13 @@
     stay, cross, other_stay, other_cross = pl.pallas_call(
         apply_kernel,
         out_shape=[block] * 4,
-        in_specs=[smem] * 4 + [anywhere] + [vmem] * 5,
+        in_specs=[smem] * 4 + [anywhere] * (1 + XS) + [vmem],
         out_specs=[vmem] * 4,
         scratch_shapes=[
             pltpu.VMEM(packing.shape, jnp.bfloat16),
             pltpu.VMEM((4 * quarter + 1, size, size), jnp.float32),
             pltpu.VMEM((4 * quarter, size, size), jnp.bfloat16),
-            pltpu.SemaphoreType.DMA,
+            pltpu.SemaphoreType.DMA((1 + XS,)),
         ],
         compiler_params=pltpu.CompilerParams(vmem_limit_bytes=40 * 2**20),
     )(
@@ -306,10 +306,15 @@
         *parts,
         right_tiles,
     )
-    cross = sum_x(cross, swap(other_cross, "core"))
+    cross = add(cross, swap(other_cross, "core"))
+    cross = lax.all_to_all(cross, "x", 0, 0, tiled=True)
+    cross = jnp.sum(cross.reshape((XS,) + psi.shape).astype(jnp.float32), axis=0)
     crossed = swap(cross.astype(jnp.bfloat16), "y_hi")
-    stay = sum_x(stay, swap(other_stay, "core"))
-    total = stay + crossed.astype(jnp.float32)
+    stay = add(stay, swap(other_stay, "core")).reshape((XS,) + psi.shape)
+    total = stay[0].astype(jnp.float32)
+    for step in range(1, XS):
+        total = total + step_x(stay[step], step).astype(jnp.float32)
+    total = total + crossed.astype(jnp.float32)
     return total.astype(jnp.bfloat16).reshape(wavefunction.shape)
 
 

time: 183 us -> 183 us (level)
  the two profiles are of different devices: /device:TPU:56 before, /device:TPU:138 now
where the time goes in v5:
time: 183 us; the launch traced here: 182 us
  blocking collectives  105 us (57%)
  starting transfers between devices  46.5 us (25%)
  Pallas kernels  20 us (11%)
  waiting for transfers between devices  6.92 us (4%)
  other arithmetic  2.88 us (2%)
    all_to_all x1, blocking collectives, run(): got = lax.all_to_all(packed[slots - 1], ENV, 0, 0, tiled=True)  105 us
    ppermute x6, starting transfers between devices, step_x(): return lax.ppermute(value, 'x', [(i, (i + step) % XS) for i in range(XS)])  20.9 us
    ppermute x6, starting transfers between devices, swap(): return lax.ppermute(value, axis, [(0, 1), (1, 0)])  20.3 us
    pallas_call x1, Pallas kernels, shards(): pl.pallas_call(apply_kernel, out_shape=[block] * 4, in_specs=[smem] * 4 +...  14.7 us
    ppermute x6, waiting for transfers between devices, swap(): return lax.ppermute(value, axis, [(0, 1), (1, 0)])  6.9 us
    pallas_call x1, Pallas kernels, shards(): pl.pallas_call(lambda *refs: pack_kernel(per, *refs), out_shape=(*[jax.Sh...  5.32 us
    all_to_all x1, starting transfers between devices, shards(): cross = lax.all_to_all(cross, 'x', 0, 0, tiled=True)  5.28 us
  transfers between devices with their start and end apart: 13, of which 2 were waited for; matrix products, arithmetic and copies ran while one was open for 1% of the time, Pallas kernels for 3%

profile of v5, /device:TPU:138, one launch (start us, length us, event | category | flops | bytes accessed | tf_op | source)
XLA Modules:
  0.0 182.2 jit_solution(2748636632015078997)
XLA Ops:
  0.0 6.8 %collective-permute-start = (bf16[4,128,128]{2,1,0:T(8,128)(2,1)}, bf16[4,128,128]{2,1,0:T(8,128)(2,1)S(1)}, u32[]{:S(2)}, u32[]{:S(2)}) collective-permute-start(bf16[4,128,128]{2,1,0:T(8,128)(2,1)} %bitcast.7), channel_id=1, source_target_pairs={{0,256},{256,0},{1,257},{257,1},{2,258},{258,2},{3,259},{259,3},{4... | collective-permute-start | bytes 393224 | tf_op jit(solution)/shard_map/ppermute | solution.py:211
  6.8 1.9 %collective-permute-start.1 = (bf16[4,128,128]{2,1,0:T(8,128)(2,1)}, bf16[4,128,128]{2,1,0:T(8,128)(2,1)S(1)}, u32[]{:S(2)}, u32[]{:S(2)}) collective-permute-start(bf16[4,128,128]{2,1,0:T(8,128)(2,1)} %bitcast.8), channel_id=1, source_target_pairs={{0,32},{32,0},{1,33},{33,1},{2,34},{34,2},{3,35},{35,3},{4,36},{36... | collective-permute-start | bytes 393224 | tf_op jit(solution)/shard_map/ppermute | solution.py:211
  8.8 5.3 %shard_map.82 = (bf16[32,128,128]{2,1,0:T(8,128)(2,1)}, bf16[64,128,128]{2,1,0:T(8,128)(2,1)}, bf16[96,128,128]{2,1,0:T(8,128)(2,1)}, bf16[128,128,128]{2,1,0:T(8,128)(2,1)}, s32[1]{0:T(128)}, /*index=5*/s32[517]{0:T(1024)}) custom-call(s32[512]{0:T(512)} %bitcast.10, s32[32]{0:T(128)} %refs_1_.1, s32[4,128]{1,0:T(4,128)} %bitcast.11, ...), custom_call_target="tpu_custom_call" | custom-call | bytes 8388608 | tf_op jit(solution)/shard_map/pallas_call | solution.py:261
  14.1 2.5 %collective-permute-start.2 = (bf16[4,128,128]{2,1,0:T(8,128)(2,1)S(1)}, bf16[4,128,128]{2,1,0:T(8,128)(2,1)S(1)}, u32[]{:S(2)}, u32[]{:S(2)}) collective-permute-start(bf16[4,128,128]{2,1,0:T(8,128)(2,1)S(1)} %collective-permute-done), channel_id=1, source_target_pairs={{0,32},{32,0},{1,33},{33,1},{2,34},{34,2},{3,35},{35,3},{4,36},{36... | collective-permute-start | bytes 393224 | tf_op jit(solution)/shard_map/ppermute | solution.py:211
  16.6 1.0 collective-permute-done.2
  17.5 1.0 pad_maximum_fusion.part_0
  18.5 3.4 %collective-permute-start.3 = (bf16[16,128,128]{2,1,0:T(8,128)(2,1)S(1)}, bf16[16,128,128]{2,1,0:T(8,128)(2,1)S(1)}, u32[]{:S(2)}, u32[]{:S(2)}) collective-permute-start(bf16[16,128,128]{2,1,0:T(8,128)(2,1)S(1)} %pad_maximum_fusion.part_0), channel_id=1, source_target_pairs={{0,64},{64,128},{128,192},{192,0},{1,65},{65,129},{129,193},{193,1... | collective-permute-start | bytes 1572872 | tf_op jit(solution)/shard_map/ppermute | solution.py:220
  21.9 3.1 %collective-permute-start.4 = (bf16[16,128,128]{2,1,0:T(8,128)(2,1)S(1)}, bf16[16,128,128]{2,1,0:T(8,128)(2,1)S(1)}, u32[]{:S(2)}, u32[]{:S(2)}) collective-permute-start(bf16[16,128,128]{2,1,0:T(8,128)(2,1)S(1)} %pad_maximum_fusion.part_0), channel_id=1, source_target_pairs={{0,128},{64,192},{128,0},{192,64},{1,129},{65,193},{129,1},{193,65... | collective-permute-start | bytes 1572872 | tf_op jit(solution)/shard_map/ppermute | solution.py:220
  24.9 4.1 %collective-permute-start.5 = (bf16[16,128,128]{2,1,0:T(8,128)(2,1)S(1)}, bf16[16,128,128]{2,1,0:T(8,128)(2,1)S(1)}, u32[]{:S(2)}, u32[]{:S(2)}) collective-permute-start(bf16[16,128,128]{2,1,0:T(8,128)(2,1)S(1)} %pad_maximum_fusion.part_0), channel_id=1, source_target_pairs={{0,192},{64,0},{128,64},{192,128},{1,193},{65,1},{129,65},{193,129... | collective-permute-start | bytes 1572872 | tf_op jit(solution)/shard_map/ppermute | solution.py:220
  29.7 104.9 %conditional.1 = (bf16[128,128,128]{2,1,0:T(8,128)(2,1)}) conditional(s32[]{:T(128)} %bitcast.2, bf16[32,128,128]{2,1,0:T(8,128)(2,1)} %get-tuple-element.40, bf16[64,128,128]{2,1,0:T(8,128)(2,1)} %get-tuple-element.41, bf16[96,128,128]{2,1,0:T(8,128)(2,1)} %get-tuple-element.42, ...), branch_computations={%region_0.0_spmd, %region_1.0_spmd, %region_2.0_spmd, %region_3.0_... | conditional | bytes 8388616 | solution.py:282
  29.7 104.9 %all_to_all.24 = bf16[128,128,128]{2,1,0:T(8,128)(2,1)} all-to-all(bf16[128,128,128]{2,1,0:T(8,128)(2,1)} %param.3), channel_id=1, replica_groups=mesh['y_hi'=2,'x'=4,'core'=2,'z'=8,'y_lo'=4] {'z','y_lo'}, dimensions={0} | all-to-all | bytes 8388608 | tf_op jit(solution)/shard_map/cond/branch_3_fun/all_to_all | solution.py:225
  134.6 14.7 %shard_map.83 = (bf16[16,128,128]{2,1,0:T(8,128)(2,1)S(1)}, bf16[16,128,128]{2,1,0:T(8,128)(2,1)S(1)}, bf16[16,128,128]{2,1,0:T(8,128)(2,1)}, bf16[16,128,128]{2,1,0:T(8,128)(2,1)S(1)}) custom-call(s32[512]{0:T(512)S(1)} %copy-done.2, s32[512]{0:T(512)S(1)} %copy-done.3, s32[512]{0:T(512)S(1)} %copy-done.4, s32[517]{0:T(1024)S(1)} %copy-done.1, ...), custom_call_target="tpu_custom_call" | custom-call | tf_op jit(solution)/shard_map/pallas_call | solution.py:288
  149.3 1.9 %collective-permute-start.10 = (bf16[16,128,128]{2,1,0:T(8,128)(2,1)S(1)}, bf16[16,128,128]{2,1,0:T(8,128)(2,1)S(1)}, u32[]{:S(2)}, u32[]{:S(2)}) collective-permute-start(bf16[16,128,128]{2,1,0:T(8,128)(2,1)S(1)} %get-tuple-element.53), channel_id=1, source_target_pairs={{0,32},{32,0},{1,33},{33,1},{2,34},{34,2},{3,35},{35,3},{4,36},{36... | collective-permute-start | bytes 1572872 | tf_op jit(solution)/shard_map/ppermute | solution.py:211
  151.3 2.4 %collective-permute-start.6 = (bf16[16,128,128]{2,1,0:T(8,128)(2,1)}, bf16[16,128,128]{2,1,0:T(8,128)(2,1)S(1)}, u32[]{:S(2)}, u32[]{:S(2)}) collective-permute-start(bf16[16,128,128]{2,1,0:T(8,128)(2,1)} %get-tuple-element.51), channel_id=1, source_target_pairs={{0,32},{32,0},{1,33},{33,1},{2,34},{34,2},{3,35},{35,3},{4,36},{36... | collective-permute-start | bytes 1572872 | tf_op jit(solution)/shard_map/ppermute | solution.py:211
  153.7 0.9 add_convert_fusion
  154.6 5.3 %all-to-all-start.4 = ((bf16[16,128,128]{2,1,0:T(8,128)(2,1)}), bf16[16,128,128]{2,1,0:T(8,128)(2,1)S(1)}, u32[]{:S(2)}, u32[]{:S(2)}) async-start(bf16[16,128,128]{2,1,0:T(8,128)(2,1)} %add_convert_fusion), calls=%async_computation.4 | async-start | bytes 1048576 | tf_op jit(solution)/shard_map/all_to_all | solution.py:310
  159.9 0.1 add_convert_fusion.1
  160.1 2.0 %collective-permute-start.9 = (bf16[4,128,128]{2,1,0:T(8,128)(2,1)S(1)}, bf16[4,128,128]{2,1,0:T(8,128)(2,1)S(1)}, u32[]{:S(2)}, u32[]{:S(2)}) collective-permute-start(bf16[4,128,128]{2,1,0:T(8,128)(2,1)S(1)} %get-tuple-element.55), channel_id=1, source_target_pairs={{0,192},{64,0},{128,64},{192,128},{1,193},{65,1},{129,65},{193,129... | collective-permute-start | bytes 393224 | tf_op jit(solution)/shard_map/ppermute | solution.py:220
  162.1 4.8 %collective-permute-start.8 = (bf16[4,128,128]{2,1,0:T(8,128)(2,1)S(1)}, bf16[4,128,128]{2,1,0:T(8,128)(2,1)S(1)}, u32[]{:S(2)}, u32[]{:S(2)}) collective-permute-start(bf16[4,128,128]{2,1,0:T(8,128)(2,1)S(1)} %get-tuple-element.56), channel_id=1, source_target_pairs={{0,128},{64,192},{128,0},{192,64},{1,129},{65,193},{129,1},{193,65... | collective-permute-start | bytes 393224 | tf_op jit(solution)/shard_map/ppermute | solution.py:220
  166.9 3.7 %collective-permute-start.7 = (bf16[4,128,128]{2,1,0:T(8,128)(2,1)S(1)}, bf16[4,128,128]{2,1,0:T(8,128)(2,1)S(1)}, u32[]{:S(2)}, u32[]{:S(2)}) collective-permute-start(bf16[4,128,128]{2,1,0:T(8,128)(2,1)S(1)} %get-tuple-element.54), channel_id=1, source_target_pairs={{0,64},{64,128},{128,192},{192,0},{1,65},{65,129},{129,193},{193,1... | collective-permute-start | bytes 393224 | tf_op jit(solution)/shard_map/ppermute | solution.py:220
  170.6 0.1 reduce_sum.12
  170.7 4.8 %collective-permute-start.11 = (bf16[4,128,128]{2,1,0:T(8,128)(2,1)S(1)}, bf16[4,128,128]{2,1,0:T(8,128)(2,1)S(1)}, u32[]{:S(2)}, u32[]{:S(2)}) collective-permute-start(bf16[4,128,128]{2,1,0:T(8,128)(2,1)S(1)} %reduce_sum.12), channel_id=1, source_target_pairs={{0,256},{256,0},{1,257},{257,1},{2,258},{258,2},{3,259},{259,3},{4... | collective-permute-start | bytes 393224 | tf_op jit(solution)/shard_map/ppermute | solution.py:211
  175.5 5.9 %collective-permute-done.11 = bf16[4,128,128]{2,1,0:T(8,128)(2,1)S(1)} collective-permute-done((bf16[4,128,128]{2,1,0:T(8,128)(2,1)S(1)}, bf16[4,128,128]{2,1,0:T(8,128)(2,1)S(1)}, u32[]{:S(2)}, u32[]{:S(2)}) %collective-permute-start.11) | collective-permute-done | bytes 131104 | tf_op jit(solution)/shard_map/ppermute | solution.py:211
  181.4 0.7 add_convert_fusion.2
  (22 shorter events, 0.1 us)
Async XLA Ops:
  0.0 14.1 %collective-permute-start = (bf16[4,128,128]{2,1,0:T(8,128)(2,1)}, bf16[4,128,128]{2,1,0:T(8,128)(2,1)S(1)}, u32[]{:S(2)}, u32[]{:S(2)}) collective-permute-start(bf16[4,128,128]{2,1,0:T(8,128)(2,1)} %bitcast.7), channel_id=1, source_target_pairs={{0,256},{256,0},{1,257},{257,1},{2,258},{258,2},{3,259},{259,3},{4... | collective-permute-start | bytes 393224 | tf_op jit(solution)/shard_map/ppermute | solution.py:211
  6.8 9.7 %collective-permute-start.1 = (bf16[4,128,128]{2,1,0:T(8,128)(2,1)}, bf16[4,128,128]{2,1,0:T(8,128)(2,1)S(1)}, u32[]{:S(2)}, u32[]{:S(2)}) collective-permute-start(bf16[4,128,128]{2,1,0:T(8,128)(2,1)} %bitcast.8), channel_id=1, source_target_pairs={{0,32},{32,0},{1,33},{33,1},{2,34},{34,2},{3,35},{35,3},{4,36},{36... | collective-permute-start | bytes 393224 | tf_op jit(solution)/shard_map/ppermute | solution.py:211
  14.1 3.4 %collective-permute-start.2 = (bf16[4,128,128]{2,1,0:T(8,128)(2,1)S(1)}, bf16[4,128,128]{2,1,0:T(8,128)(2,1)S(1)}, u32[]{:S(2)}, u32[]{:S(2)}) collective-permute-start(bf16[4,128,128]{2,1,0:T(8,128)(2,1)S(1)} %collective-permute-done), channel_id=1, source_target_pairs={{0,32},{32,0},{1,33},{33,1},{2,34},{34,2},{3,35},{35,3},{4,36},{36... | collective-permute-start | bytes 393224 | tf_op jit(solution)/shard_map/ppermute | solution.py:211
  18.5 116.1 %collective-permute-start.3 = (bf16[16,128,128]{2,1,0:T(8,128)(2,1)S(1)}, bf16[16,128,128]{2,1,0:T(8,128)(2,1)S(1)}, u32[]{:S(2)}, u32[]{:S(2)}) collective-permute-start(bf16[16,128,128]{2,1,0:T(8,128)(2,1)S(1)} %pad_maximum_fusion.part_0), channel_id=1, source_target_pairs={{0,64},{64,128},{128,192},{192,0},{1,65},{65,129},{129,193},{193,1... | collective-permute-start | bytes 1572872 | tf_op jit(solution)/shard_map/ppermute | solution.py:220
  21.9 112.7 %collective-permute-start.4 = (bf16[16,128,128]{2,1,0:T(8,128)(2,1)S(1)}, bf16[16,128,128]{2,1,0:T(8,128)(2,1)S(1)}, u32[]{:S(2)}, u32[]{:S(2)}) collective-permute-start(bf16[16,128,128]{2,1,0:T(8,128)(2,1)S(1)} %pad_maximum_fusion.part_0), channel_id=1, source_target_pairs={{0,128},{64,192},{128,0},{192,64},{1,129},{65,193},{129,1},{193,65... | collective-permute-start | bytes 1572872 | tf_op jit(solution)/shard_map/ppermute | solution.py:220
  24.9 109.6 %collective-permute-start.5 = (bf16[16,128,128]{2,1,0:T(8,128)(2,1)S(1)}, bf16[16,128,128]{2,1,0:T(8,128)(2,1)S(1)}, u32[]{:S(2)}, u32[]{:S(2)}) collective-permute-start(bf16[16,128,128]{2,1,0:T(8,128)(2,1)S(1)} %pad_maximum_fusion.part_0), channel_id=1, source_target_pairs={{0,192},{64,0},{128,64},{192,128},{1,193},{65,1},{129,65},{193,129... | collective-permute-start | bytes 1572872 | tf_op jit(solution)/shard_map/ppermute | solution.py:220
  29.6 105.0 %copy-start = (bf16[26,128,128]{2,1,0:T(8,128)(2,1)S(1)}, bf16[26,128,128]{2,1,0:T(8,128)(2,1)}, u32[]{:S(2)}) copy-start(bf16[26,128,128]{2,1,0:T(8,128)(2,1)} %rights.1) | copy-start | bytes 2555908
  29.6 105.0 %copy-start.1 = (s32[517]{0:T(1024)S(1)}, s32[517]{0:T(1024)}, u32[]{:S(2)}) copy-start(s32[517]{0:T(1024)} %get-tuple-element.34.picked) | copy-start | bytes 6208
  29.6 105.0 %copy-start.2 = (s32[512]{0:T(512)S(1)}, s32[512]{0:T(512)}, u32[]{:S(2)}) copy-start(s32[512]{0:T(512)} %source.1) | copy-start | bytes 6148
  29.6 105.0 %copy-start.3 = (s32[512]{0:T(512)S(1)}, s32[512]{0:T(512)}, u32[]{:S(2)}) copy-start(s32[512]{0:T(512)} %target.1) | copy-start | bytes 6148
  29.6 105.0 %copy-start.4 = (s32[512]{0:T(512)S(1)}, s32[512]{0:T(512)}, u32[]{:S(2)}) copy-start(s32[512]{0:T(512)} %index.1) | copy-start | bytes 6148
  149.3 4.3 %collective-permute-start.10 = (bf16[16,128,128]{2,1,0:T(8,128)(2,1)S(1)}, bf16[16,128,128]{2,1,0:T(8,128)(2,1)S(1)}, u32[]{:S(2)}, u32[]{:S(2)}) collective-permute-start(bf16[16,128,128]{2,1,0:T(8,128)(2,1)S(1)} %get-tuple-element.53), channel_id=1, source_target_pairs={{0,32},{32,0},{1,33},{33,1},{2,34},{34,2},{3,35},{35,3},{4,36},{36... | collective-permute-start | bytes 1572872 | tf_op jit(solution)/shard_map/ppermute | solution.py:211
  151.3 8.6 %collective-permute-start.6 = (bf16[16,128,128]{2,1,0:T(8,128)(2,1)}, bf16[16,128,128]{2,1,0:T(8,128)(2,1)S(1)}, u32[]{:S(2)}, u32[]{:S(2)}) collective-permute-start(bf16[16,128,128]{2,1,0:T(8,128)(2,1)} %get-tuple-element.51), channel_id=1, source_target_pairs={{0,32},{32,0},{1,33},{33,1},{2,34},{34,2},{3,35},{35,3},{4,36},{36... | collective-permute-start | bytes 1572872 | tf_op jit(solution)/shard_map/ppermute | solution.py:211
  154.6 15.9 %all-to-all-start.4 = ((bf16[16,128,128]{2,1,0:T(8,128)(2,1)}), bf16[16,128,128]{2,1,0:T(8,128)(2,1)S(1)}, u32[]{:S(2)}, u32[]{:S(2)}) async-start(bf16[16,128,128]{2,1,0:T(8,128)(2,1)} %add_convert_fusion), calls=%async_computation.4 | async-start | bytes 1048576 | tf_op jit(solution)/shard_map/all_to_all | solution.py:310
  160.1 15.4 %collective-permute-start.9 = (bf16[4,128,128]{2,1,0:T(8,128)(2,1)S(1)}, bf16[4,128,128]{2,1,0:T(8,128)(2,1)S(1)}, u32[]{:S(2)}, u32[]{:S(2)}) collective-permute-start(bf16[4,128,128]{2,1,0:T(8,128)(2,1)S(1)} %get-tuple-element.55), channel_id=1, source_target_pairs={{0,192},{64,0},{128,64},{192,128},{1,193},{65,1},{129,65},{193,129... | collective-permute-start | bytes 393224 | tf_op jit(solution)/shard_map/ppermute | solution.py:220
  162.1 13.4 %collective-permute-start.8 = (bf16[4,128,128]{2,1,0:T(8,128)(2,1)S(1)}, bf16[4,128,128]{2,1,0:T(8,128)(2,1)S(1)}, u32[]{:S(2)}, u32[]{:S(2)}) collective-permute-start(bf16[4,128,128]{2,1,0:T(8,128)(2,1)S(1)} %get-tuple-element.56), channel_id=1, source_target_pairs={{0,128},{64,192},{128,0},{192,64},{1,129},{65,193},{129,1},{193,65... | collective-permute-start | bytes 393224 | tf_op jit(solution)/shard_map/ppermute | solution.py:220
  166.9 8.6 %collective-permute-start.7 = (bf16[4,128,128]{2,1,0:T(8,128)(2,1)S(1)}, bf16[4,128,128]{2,1,0:T(8,128)(2,1)S(1)}, u32[]{:S(2)}, u32[]{:S(2)}) collective-permute-start(bf16[4,128,128]{2,1,0:T(8,128)(2,1)S(1)} %get-tuple-element.54), channel_id=1, source_target_pairs={{0,64},{64,128},{128,192},{192,0},{1,65},{65,129},{129,193},{193,1... | collective-permute-start | bytes 393224 | tf_op jit(solution)/shard_map/ppermute | solution.py:220
  170.7 10.8 %collective-permute-start.11 = (bf16[4,128,128]{2,1,0:T(8,128)(2,1)S(1)}, bf16[4,128,128]{2,1,0:T(8,128)(2,1)S(1)}, u32[]{:S(2)}, u32[]{:S(2)}) collective-permute-start(bf16[4,128,128]{2,1,0:T(8,128)(2,1)S(1)} %reduce_sum.12), channel_id=1, source_target_pairs={{0,256},{256,0},{1,257},{257,1},{2,258},{258,2},{3,259},{259,3},{4... | collective-permute-start | bytes 393224 | tf_op jit(solution)/shard_map/ppermute | solution.py:211

commit v6 on v5

--- a/solution.py
+++ b/solution.py
@@ -12,7 +12,7 @@
 DEEP, LOW = 8, 4
 ROWS_DEV = 4
 SLOTS = 4
-UNROLL = 4
+UNROLL = 16
 LANES = 128
 
 
@@ -124,6 +124,7 @@
     target,
     index,
     picked,
+    need,
     tiles,
     part_0,
     part_1,
@@ -139,7 +140,19 @@
     blocks,
     copied,
 ):
-    loads = [pltpu.make_async_copy(tiles, held, copied.at[XS])]
+    size = tiles.shape[0] // SLOTS
+
+    def load_slot(slot):
+        at = pl.ds(slot * size, size)
+        return pltpu.make_async_copy(tiles.at[at], held.at[at], copied.at[XS + slot])
+
+    for slot in range(SLOTS):
+
+        @pl.when(need[0] > slot)
+        def _(slot=slot):
+            load_slot(slot).start()
+
+    loads = []
     for x, part in enumerate((part_0, part_1, part_2, part_3)):
         at = blocks.at[pl.ds(x * part.shape[0], part.shape[0])]
         loads.append(pltpu.make_async_copy(part, at, copied.at[x]))
@@ -171,22 +184,30 @@
     lax.fori_loop(0, count, clear, 0, unroll=4)
     for load in loads:
         load.wait()
+    for slot in range(SLOTS):
+
+        @pl.when(need[0] > slot)
+        def _(slot=slot):
+            load_slot(slot).wait()
 
     def terms(j, carry):
-        for u in range(UNROLL):
-            entry = picked[1 + j * UNROLL + u]
-            kept = jnp.maximum(entry, 0)
-            t = kept // LANES
-            slot = kept % LANES
-            row = jnp.where(entry < 0, count, write_place(target[t]))
-            product = jnp.dot(
-                held[slot],
+        entries = [picked[1 + j * UNROLL + u] for u in range(UNROLL)]
+        kept = [jnp.maximum(entry, 0) for entry in entries]
+        numbers = [entry // LANES for entry in kept]
+        products = [
+            jnp.dot(
+                held[entry % LANES],
                 blocks[read_place(source[t])],
                 preferred_element_type=jnp.float32,
             ).astype(jnp.bfloat16)
-            acc[row] += jnp.dot(
-                product, rights[index[t]], preferred_element_type=jnp.float32
-            )
+            for entry, t in zip(kept, numbers)
+        ]
+        images = [
+            jnp.dot(product, rights[index[t]], preferred_element_type=jnp.float32)
+            for product, t in zip(products, numbers)
+        ]
+        for entry, t, image in zip(entries, numbers, images):
+            acc[jnp.where(entry < 0, count, write_place(target[t]))] += image
         return carry
 
     lax.fori_loop(0, (picked[0] + UNROLL - 1) // UNROLL, terms, 0)
@@ -288,13 +309,13 @@
     stay, cross, other_stay, other_cross = pl.pallas_call(
         apply_kernel,
         out_shape=[block] * 4,
-        in_specs=[smem] * 4 + [anywhere] * (1 + XS) + [vmem],
+        in_specs=[smem] * 5 + [anywhere] * (1 + XS) + [vmem],
         out_specs=[vmem] * 4,
         scratch_shapes=[
             pltpu.VMEM(packing.shape, jnp.bfloat16),
             pltpu.VMEM((4 * quarter + 1, size, size), jnp.float32),
             pltpu.VMEM((4 * quarter, size, size), jnp.bfloat16),
-            pltpu.SemaphoreType.DMA((1 + XS,)),
+            pltpu.SemaphoreType.DMA((SLOTS + XS,)),
         ],
         compiler_params=pltpu.CompilerParams(vmem_limit_bytes=40 * 2**20),
     )(
@@ -302,6 +323,7 @@
         term_target,
         right_index,
         picked,
+        need,
         tiles,
         *parts,
         right_tiles,
@@ -309,12 +331,16 @@
     cross = add(cross, swap(other_cross, "core"))
     cross = lax.all_to_all(cross, "x", 0, 0, tiled=True)
     cross = jnp.sum(cross.reshape((XS,) + psi.shape).astype(jnp.float32), axis=0)
-    crossed = swap(cross.astype(jnp.bfloat16), "y_hi")
+    cross = cross.astype(jnp.bfloat16)
     stay = add(stay, swap(other_stay, "core")).reshape((XS,) + psi.shape)
-    total = stay[0].astype(jnp.float32)
-    for step in range(1, XS):
-        total = total + step_x(stay[step], step).astype(jnp.float32)
-    total = total + crossed.astype(jnp.float32)
+    *early, last = stay
+    cross, last = lax.optimization_barrier((cross, last))
+    crossed = swap(cross, "y_hi")
+    got = [step_x(early[step], step) for step in range(1, XS - 1)]
+    got += [step_x(last, XS - 1), crossed]
+    total = early[0].astype(jnp.float32)
+    for value in got:
+        total = total + value.astype(jnp.float32)
     return total.astype(jnp.bfloat16).reshape(wavefunction.shape)
 
 

time: 183 us -> 112 us (0.61)
  the two profiles are of different devices: /device:TPU:138 before, /device:TPU:56 now
where the time goes in v6:
time: 112 us; the launch traced here: 111 us
  starting transfers between devices  43.3 us (39%)
  blocking collectives  41.1 us (37%)
  Pallas kernels  12.2 us (11%)
  waiting for transfers between devices  10.3 us (9%)
  other arithmetic  2.88 us (3%)
    all_to_all x1, blocking collectives, run(): got = lax.all_to_all(packed[slots - 1], ENV, 0, 0, tiled=True)  41.1 us
    ppermute x6, starting transfers between devices, step_x(): return lax.ppermute(value, 'x', [(i, (i + step) % XS) for i in range(XS)])  22.3 us
    ppermute x6, starting transfers between devices, swap(): return lax.ppermute(value, axis, [(0, 1), (1, 0)])  17.6 us
    ppermute x6, waiting for transfers between devices, swap(): return lax.ppermute(value, axis, [(0, 1), (1, 0)])  7.54 us
    pallas_call x1, Pallas kernels, shards(): pl.pallas_call(lambda *refs: pack_kernel(per, *refs), out_shape=(*[jax.Sh...  5.41 us
    pallas_call x1, Pallas kernels, shards(): pl.pallas_call(apply_kernel, out_shape=[block] * 4, in_specs=[smem] * 5 +...  4.58 us
    all_to_all x1, starting transfers between devices, shards(): cross = lax.all_to_all(cross, 'x', 0, 0, tiled=True)  3.47 us
    all_to_all x1, waiting for transfers between devices, shards(): cross = lax.all_to_all(cross, 'x', 0, 0, tiled=True)  2.72 us
  transfers between devices with their start and end apart: 13, of which 4 were waited for; matrix products, arithmetic and copies ran while one was open for 1% of the time, Pallas kernels for 7%

profile of v6, /device:TPU:56, one launch (start us, length us, event | category | flops | bytes accessed | tf_op | source)
XLA Modules:
  0.0 110.8 jit_solution(17164406077586916025)
XLA Ops:
  0.0 4.7 %collective-permute-start = (bf16[4,128,128]{2,1,0:T(8,128)(2,1)}, bf16[4,128,128]{2,1,0:T(8,128)(2,1)S(1)}, u32[]{:S(2)}, u32[]{:S(2)}) collective-permute-start(bf16[4,128,128]{2,1,0:T(8,128)(2,1)} %bitcast.7), channel_id=1, source_target_pairs={{0,256},{256,0},{1,257},{257,1},{2,258},{258,2},{3,259},{259,3},{4... | collective-permute-start | bytes 393224 | tf_op jit(solution)/shard_map/ppermute | solution.py:232
  4.7 1.9 %collective-permute-start.1 = (bf16[4,128,128]{2,1,0:T(8,128)(2,1)}, bf16[4,128,128]{2,1,0:T(8,128)(2,1)S(1)}, u32[]{:S(2)}, u32[]{:S(2)}) collective-permute-start(bf16[4,128,128]{2,1,0:T(8,128)(2,1)} %bitcast.8), channel_id=1, source_target_pairs={{0,32},{32,0},{1,33},{33,1},{2,34},{34,2},{3,35},{35,3},{4,36},{36... | collective-permute-start | bytes 393224 | tf_op jit(solution)/shard_map/ppermute | solution.py:232
  6.6 5.4 %shard_map.82 = (bf16[32,128,128]{2,1,0:T(8,128)(2,1)}, bf16[64,128,128]{2,1,0:T(8,128)(2,1)}, bf16[96,128,128]{2,1,0:T(8,128)(2,1)}, bf16[128,128,128]{2,1,0:T(8,128)(2,1)}, s32[1]{0:T(128)}, /*index=5*/s32[529]{0:T(1024)}) custom-call(s32[512]{0:T(512)} %bitcast.10, s32[32]{0:T(128)} %refs_1_.1, s32[4,128]{1,0:T(4,128)} %bitcast.11, ...), custom_call_target="tpu_custom_call" | custom-call | bytes 8388608 | tf_op jit(solution)/shard_map/pallas_call | solution.py:282
  12.1 1.6 %collective-permute-done = bf16[4,128,128]{2,1,0:T(8,128)(2,1)S(1)} collective-permute-done((bf16[4,128,128]{2,1,0:T(8,128)(2,1)}, bf16[4,128,128]{2,1,0:T(8,128)(2,1)S(1)}, u32[]{:S(2)}, u32[]{:S(2)}) %collective-permute-start) | collective-permute-done | bytes 131104 | tf_op jit(solution)/shard_map/ppermute | solution.py:232
  13.7 1.9 %collective-permute-start.2 = (bf16[4,128,128]{2,1,0:T(8,128)(2,1)S(1)}, bf16[4,128,128]{2,1,0:T(8,128)(2,1)S(1)}, u32[]{:S(2)}, u32[]{:S(2)}) collective-permute-start(bf16[4,128,128]{2,1,0:T(8,128)(2,1)S(1)} %collective-permute-done), channel_id=1, source_target_pairs={{0,32},{32,0},{1,33},{33,1},{2,34},{34,2},{3,35},{35,3},{4,36},{36... | collective-permute-start | bytes 393224 | tf_op jit(solution)/shard_map/ppermute | solution.py:232
  15.6 1.3 %collective-permute-done.2 = bf16[4,128,128]{2,1,0:T(8,128)(2,1)S(1)} collective-permute-done((bf16[4,128,128]{2,1,0:T(8,128)(2,1)S(1)}, bf16[4,128,128]{2,1,0:T(8,128)(2,1)S(1)}, u32[]{:S(2)}, u32[]{:S(2)}) %collective-permute-start.2) | collective-permute-done | bytes 131104 | tf_op jit(solution)/shard_map/ppermute | solution.py:232
  16.9 1.0 pad_maximum_fusion.part_0
  17.9 3.4 %collective-permute-start.3 = (bf16[16,128,128]{2,1,0:T(8,128)(2,1)S(1)}, bf16[16,128,128]{2,1,0:T(8,128)(2,1)S(1)}, u32[]{:S(2)}, u32[]{:S(2)}) collective-permute-start(bf16[16,128,128]{2,1,0:T(8,128)(2,1)S(1)} %pad_maximum_fusion.part_0), channel_id=1, source_target_pairs={{0,64},{64,128},{128,192},{192,0},{1,65},{65,129},{129,193},{193,1... | collective-permute-start | bytes 1572872 | tf_op jit(solution)/shard_map/ppermute | solution.py:241
  21.3 4.6 %collective-permute-start.4 = (bf16[16,128,128]{2,1,0:T(8,128)(2,1)S(1)}, bf16[16,128,128]{2,1,0:T(8,128)(2,1)S(1)}, u32[]{:S(2)}, u32[]{:S(2)}) collective-permute-start(bf16[16,128,128]{2,1,0:T(8,128)(2,1)S(1)} %pad_maximum_fusion.part_0), channel_id=1, source_target_pairs={{0,128},{64,192},{128,0},{192,64},{1,129},{65,193},{129,1},{193,65... | collective-permute-start | bytes 1572872 | tf_op jit(solution)/shard_map/ppermute | solution.py:241
  25.9 3.3 %collective-permute-start.5 = (bf16[16,128,128]{2,1,0:T(8,128)(2,1)S(1)}, bf16[16,128,128]{2,1,0:T(8,128)(2,1)S(1)}, u32[]{:S(2)}, u32[]{:S(2)}) collective-permute-start(bf16[16,128,128]{2,1,0:T(8,128)(2,1)S(1)} %pad_maximum_fusion.part_0), channel_id=1, source_target_pairs={{0,192},{64,0},{128,64},{192,128},{1,193},{65,1},{129,65},{193,129... | collective-permute-start | bytes 1572872 | tf_op jit(solution)/shard_map/ppermute | solution.py:241
  30.0 43.3 %conditional.1 = (bf16[128,128,128]{2,1,0:T(8,128)(2,1)}) conditional(s32[]{:T(128)} %bitcast.2, bf16[32,128,128]{2,1,0:T(8,128)(2,1)} %get-tuple-element.42, bf16[64,128,128]{2,1,0:T(8,128)(2,1)} %get-tuple-element.43, bf16[96,128,128]{2,1,0:T(8,128)(2,1)} %get-tuple-element.44, ...), branch_computations={%region_0.0_spmd, %region_1.0_spmd, %region_2.0_spmd, %region_3.0_... | conditional | bytes 8388616 | solution.py:303
  30.0 41.1 %all_to_all.21.got = bf16[32,128,128]{2,1,0:T(8,128)(2,1)} all-to-all(bf16[32,128,128]{2,1,0:T(8,128)(2,1)} %param), channel_id=1, replica_groups=mesh['y_hi'=2,'x'=4,'core'=2,'z'=8,'y_lo'=4] {'z','y_lo'}, dimensions={0} | all-to-all | bytes 2097152 | tf_op jit(solution)/shard_map/cond/branch_0_fun/all_to_all | solution.py:246
  71.1 2.2 %branch_0_fun.1 = bf16[128,128,128]{2,1,0:T(8,128)(2,1)} custom-call(bf16[32,128,128]{2,1,0:T(8,128)(2,1)} %all_to_all.21.got), custom_call_target="tpu_custom_call" | custom-call | tf_op jit(solution)/shard_map/cond/branch_0_fun/pallas_call | solution.py:249
  73.4 4.6 %shard_map.83 = (bf16[16,128,128]{2,1,0:T(8,128)(2,1)S(1)}, bf16[16,128,128]{2,1,0:T(8,128)(2,1)S(1)}, bf16[16,128,128]{2,1,0:T(8,128)(2,1)}, bf16[16,128,128]{2,1,0:T(8,128)(2,1)S(1)}) custom-call(s32[512]{0:T(512)S(1)} %copy-done.2, s32[512]{0:T(512)S(1)} %copy-done.3, s32[512]{0:T(512)S(1)} %copy-done.4, s32[529]{0:T(1024)S(1)} %copy-done.1, ...), custom_call_target="tpu_custom_call" | custom-call | tf_op jit(solution)/shard_map/pallas_call | solution.py:309
  78.0 2.3 %collective-permute-start.9 = (bf16[16,128,128]{2,1,0:T(8,128)(2,1)S(1)}, bf16[16,128,128]{2,1,0:T(8,128)(2,1)S(1)}, u32[]{:S(2)}, u32[]{:S(2)}) collective-permute-start(bf16[16,128,128]{2,1,0:T(8,128)(2,1)S(1)} %get-tuple-element.55), channel_id=1, source_target_pairs={{0,32},{32,0},{1,33},{33,1},{2,34},{34,2},{3,35},{35,3},{4,36},{36... | collective-permute-start | bytes 1572872 | tf_op jit(solution)/shard_map/ppermute | solution.py:232
  80.3 2.1 %collective-permute-start.6 = (bf16[16,128,128]{2,1,0:T(8,128)(2,1)}, bf16[16,128,128]{2,1,0:T(8,128)(2,1)S(1)}, u32[]{:S(2)}, u32[]{:S(2)}) collective-permute-start(bf16[16,128,128]{2,1,0:T(8,128)(2,1)} %get-tuple-element.53), channel_id=1, source_target_pairs={{0,32},{32,0},{1,33},{33,1},{2,34},{34,2},{3,35},{35,3},{4,36},{36... | collective-permute-start | bytes 1572872 | tf_op jit(solution)/shard_map/ppermute | solution.py:232
  82.3 0.9 add_convert_fusion
  83.3 3.5 %all-to-all-start.4 = ((bf16[16,128,128]{2,1,0:T(8,128)(2,1)}), bf16[16,128,128]{2,1,0:T(8,128)(2,1)S(1)}, u32[]{:S(2)}, u32[]{:S(2)}) async-start(bf16[16,128,128]{2,1,0:T(8,128)(2,1)} %add_convert_fusion), calls=%async_computation.4 | async-start | bytes 1048576 | tf_op jit(solution)/shard_map/all_to_all | solution.py:332
  87.0 5.4 %collective-permute-start.8 = (bf16[4,128,128]{2,1,0:T(8,128)(2,1)S(1)}, bf16[4,128,128]{2,1,0:T(8,128)(2,1)S(1)}, u32[]{:S(2)}, u32[]{:S(2)}) collective-permute-start(bf16[4,128,128]{2,1,0:T(8,128)(2,1)S(1)} %get-tuple-element.60), channel_id=1, source_target_pairs={{0,128},{64,192},{128,0},{192,64},{1,129},{65,193},{129,1},{193,65... | collective-permute-start | bytes 393224 | tf_op jit(solution)/shard_map/ppermute | solution.py:241
  92.4 2.5 %collective-permute-start.7 = (bf16[4,128,128]{2,1,0:T(8,128)(2,1)S(1)}, bf16[4,128,128]{2,1,0:T(8,128)(2,1)S(1)}, u32[]{:S(2)}, u32[]{:S(2)}) collective-permute-start(bf16[4,128,128]{2,1,0:T(8,128)(2,1)S(1)} %get-tuple-element.58), channel_id=1, source_target_pairs={{0,64},{64,128},{128,192},{192,0},{1,65},{65,129},{129,193},{193,1... | collective-permute-start | bytes 393224 | tf_op jit(solution)/shard_map/ppermute | solution.py:241
  94.8 2.7 %all-to-all-done.4 = bf16[16,128,128]{2,1,0:T(8,128)(2,1)S(1)} async-done(((bf16[16,128,128]{2,1,0:T(8,128)(2,1)}), bf16[16,128,128]{2,1,0:T(8,128)(2,1)S(1)}, u32[]{:S(2)}, u32[]{:S(2)}) %all-to-all-start.4) | async-done | bytes 524320 | tf_op jit(solution)/shard_map/all_to_all | solution.py:332
  97.6 4.7 %collective-permute-start.11 = (bf16[4,128,128]{2,1,0:T(8,128)(2,1)S(1)}, bf16[4,128,128]{2,1,0:T(8,128)(2,1)S(1)}, u32[]{:S(2)}, u32[]{:S(2)}) collective-permute-start(bf16[4,128,128]{2,1,0:T(8,128)(2,1)S(1)} %reduce_sum.12), channel_id=1, source_target_pairs={{0,256},{256,0},{1,257},{257,1},{2,258},{258,2},{3,259},{259,3},{4... | collective-permute-start | bytes 393224 | tf_op jit(solution)/shard_map/ppermute | solution.py:232
  102.3 3.1 %collective-permute-start.10 = (bf16[4,128,128]{2,1,0:T(8,128)(2,1)S(1)}, bf16[4,128,128]{2,1,0:T(8,128)(2,1)S(1)}, u32[]{:S(2)}, u32[]{:S(2)}) collective-permute-start(bf16[4,128,128]{2,1,0:T(8,128)(2,1)S(1)} %get-tuple-element.56), channel_id=1, source_target_pairs={{0,192},{64,0},{128,64},{192,128},{1,193},{65,1},{129,65},{193,129... | collective-permute-start | bytes 393224 | tf_op jit(solution)/shard_map/ppermute | solution.py:241
  105.4 4.6 %collective-permute-done.11 = bf16[4,128,128]{2,1,0:T(8,128)(2,1)S(1)} collective-permute-done((bf16[4,128,128]{2,1,0:T(8,128)(2,1)S(1)}, bf16[4,128,128]{2,1,0:T(8,128)(2,1)S(1)}, u32[]{:S(2)}, u32[]{:S(2)}) %collective-permute-start.11) | collective-permute-done | bytes 131104 | tf_op jit(solution)/shard_map/ppermute | solution.py:232
  (23 shorter events, 1.1 us)
Async XLA Ops:
  0.0 13.7 %collective-permute-start = (bf16[4,128,128]{2,1,0:T(8,128)(2,1)}, bf16[4,128,128]{2,1,0:T(8,128)(2,1)S(1)}, u32[]{:S(2)}, u32[]{:S(2)}) collective-permute-start(bf16[4,128,128]{2,1,0:T(8,128)(2,1)} %bitcast.7), channel_id=1, source_target_pairs={{0,256},{256,0},{1,257},{257,1},{2,258},{258,2},{3,259},{259,3},{4... | collective-permute-start | bytes 393224 | tf_op jit(solution)/shard_map/ppermute | solution.py:232
  4.7 10.9 %collective-permute-start.1 = (bf16[4,128,128]{2,1,0:T(8,128)(2,1)}, bf16[4,128,128]{2,1,0:T(8,128)(2,1)S(1)}, u32[]{:S(2)}, u32[]{:S(2)}) collective-permute-start(bf16[4,128,128]{2,1,0:T(8,128)(2,1)} %bitcast.8), channel_id=1, source_target_pairs={{0,32},{32,0},{1,33},{33,1},{2,34},{34,2},{3,35},{35,3},{4,36},{36... | collective-permute-start | bytes 393224 | tf_op jit(solution)/shard_map/ppermute | solution.py:232
  13.7 3.2 %collective-permute-start.2 = (bf16[4,128,128]{2,1,0:T(8,128)(2,1)S(1)}, bf16[4,128,128]{2,1,0:T(8,128)(2,1)S(1)}, u32[]{:S(2)}, u32[]{:S(2)}) collective-permute-start(bf16[4,128,128]{2,1,0:T(8,128)(2,1)S(1)} %collective-permute-done), channel_id=1, source_target_pairs={{0,32},{32,0},{1,33},{33,1},{2,34},{34,2},{3,35},{35,3},{4,36},{36... | collective-permute-start | bytes 393224 | tf_op jit(solution)/shard_map/ppermute | solution.py:232
  17.9 55.4 %collective-permute-start.3 = (bf16[16,128,128]{2,1,0:T(8,128)(2,1)S(1)}, bf16[16,128,128]{2,1,0:T(8,128)(2,1)S(1)}, u32[]{:S(2)}, u32[]{:S(2)}) collective-permute-start(bf16[16,128,128]{2,1,0:T(8,128)(2,1)S(1)} %pad_maximum_fusion.part_0), channel_id=1, source_target_pairs={{0,64},{64,128},{128,192},{192,0},{1,65},{65,129},{129,193},{193,1... | collective-permute-start | bytes 1572872 | tf_op jit(solution)/shard_map/ppermute | solution.py:241
  21.3 52.0 %collective-permute-start.4 = (bf16[16,128,128]{2,1,0:T(8,128)(2,1)S(1)}, bf16[16,128,128]{2,1,0:T(8,128)(2,1)S(1)}, u32[]{:S(2)}, u32[]{:S(2)}) collective-permute-start(bf16[16,128,128]{2,1,0:T(8,128)(2,1)S(1)} %pad_maximum_fusion.part_0), channel_id=1, source_target_pairs={{0,128},{64,192},{128,0},{192,64},{1,129},{65,193},{129,1},{193,65... | collective-permute-start | bytes 1572872 | tf_op jit(solution)/shard_map/ppermute | solution.py:241
  25.9 47.4 %collective-permute-start.5 = (bf16[16,128,128]{2,1,0:T(8,128)(2,1)S(1)}, bf16[16,128,128]{2,1,0:T(8,128)(2,1)S(1)}, u32[]{:S(2)}, u32[]{:S(2)}) collective-permute-start(bf16[16,128,128]{2,1,0:T(8,128)(2,1)S(1)} %pad_maximum_fusion.part_0), channel_id=1, source_target_pairs={{0,192},{64,0},{128,64},{192,128},{1,193},{65,1},{129,65},{193,129... | collective-permute-start | bytes 1572872 | tf_op jit(solution)/shard_map/ppermute | solution.py:241
  29.9 43.4 %copy-start = (bf16[26,128,128]{2,1,0:T(8,128)(2,1)S(1)}, bf16[26,128,128]{2,1,0:T(8,128)(2,1)}, u32[]{:S(2)}) copy-start(bf16[26,128,128]{2,1,0:T(8,128)(2,1)} %rights.1) | copy-start | bytes 2555908
  29.9 43.4 %copy-start.1 = (s32[529]{0:T(1024)S(1)}, s32[529]{0:T(1024)}, u32[]{:S(2)}) copy-start(s32[529]{0:T(1024)} %get-tuple-element.36.picked) | copy-start | bytes 6352
  30.0 43.4 %copy-start.2 = (s32[512]{0:T(512)S(1)}, s32[512]{0:T(512)}, u32[]{:S(2)}) copy-start(s32[512]{0:T(512)} %source.1) | copy-start | bytes 6148
  30.0 43.4 %copy-start.3 = (s32[512]{0:T(512)S(1)}, s32[512]{0:T(512)}, u32[]{:S(2)}) copy-start(s32[512]{0:T(512)} %target.1) | copy-start | bytes 6148
  30.0 43.4 %copy-start.4 = (s32[512]{0:T(512)S(1)}, s32[512]{0:T(512)}, u32[]{:S(2)}) copy-start(s32[512]{0:T(512)} %index.1) | copy-start | bytes 6148
  78.0 4.3 %collective-permute-start.9 = (bf16[16,128,128]{2,1,0:T(8,128)(2,1)S(1)}, bf16[16,128,128]{2,1,0:T(8,128)(2,1)S(1)}, u32[]{:S(2)}, u32[]{:S(2)}) collective-permute-start(bf16[16,128,128]{2,1,0:T(8,128)(2,1)S(1)} %get-tuple-element.55), channel_id=1, source_target_pairs={{0,32},{32,0},{1,33},{33,1},{2,34},{34,2},{3,35},{35,3},{4,36},{36... | collective-permute-start | bytes 1572872 | tf_op jit(solution)/shard_map/ppermute | solution.py:232
  80.3 6.5 %collective-permute-start.6 = (bf16[16,128,128]{2,1,0:T(8,128)(2,1)}, bf16[16,128,128]{2,1,0:T(8,128)(2,1)S(1)}, u32[]{:S(2)}, u32[]{:S(2)}) collective-permute-start(bf16[16,128,128]{2,1,0:T(8,128)(2,1)} %get-tuple-element.53), channel_id=1, source_target_pairs={{0,32},{32,0},{1,33},{33,1},{2,34},{34,2},{3,35},{35,3},{4,36},{36... | collective-permute-start | bytes 1572872 | tf_op jit(solution)/shard_map/ppermute | solution.py:232
  83.3 14.3 %all-to-all-start.4 = ((bf16[16,128,128]{2,1,0:T(8,128)(2,1)}), bf16[16,128,128]{2,1,0:T(8,128)(2,1)S(1)}, u32[]{:S(2)}, u32[]{:S(2)}) async-start(bf16[16,128,128]{2,1,0:T(8,128)(2,1)} %add_convert_fusion), calls=%async_computation.4 | async-start | bytes 1048576 | tf_op jit(solution)/shard_map/all_to_all | solution.py:332
  87.0 18.5 %collective-permute-start.8 = (bf16[4,128,128]{2,1,0:T(8,128)(2,1)S(1)}, bf16[4,128,128]{2,1,0:T(8,128)(2,1)S(1)}, u32[]{:S(2)}, u32[]{:S(2)}) collective-permute-start(bf16[4,128,128]{2,1,0:T(8,128)(2,1)S(1)} %get-tuple-element.60), channel_id=1, source_target_pairs={{0,128},{64,192},{128,0},{192,64},{1,129},{65,193},{129,1},{193,65... | collective-permute-start | bytes 393224 | tf_op jit(solution)/shard_map/ppermute | solution.py:241
  92.4 13.1 %collective-permute-start.7 = (bf16[4,128,128]{2,1,0:T(8,128)(2,1)S(1)}, bf16[4,128,128]{2,1,0:T(8,128)(2,1)S(1)}, u32[]{:S(2)}, u32[]{:S(2)}) collective-permute-start(bf16[4,128,128]{2,1,0:T(8,128)(2,1)S(1)} %get-tuple-element.58), channel_id=1, source_target_pairs={{0,64},{64,128},{128,192},{192,0},{1,65},{65,129},{129,193},{193,1... | collective-permute-start | bytes 393224 | tf_op jit(solution)/shard_map/ppermute | solution.py:241
  97.6 12.4 %collective-permute-start.11 = (bf16[4,128,128]{2,1,0:T(8,128)(2,1)S(1)}, bf16[4,128,128]{2,1,0:T(8,128)(2,1)S(1)}, u32[]{:S(2)}, u32[]{:S(2)}) collective-permute-start(bf16[4,128,128]{2,1,0:T(8,128)(2,1)S(1)} %reduce_sum.12), channel_id=1, source_target_pairs={{0,256},{256,0},{1,257},{257,1},{2,258},{258,2},{3,259},{259,3},{4... | collective-permute-start | bytes 393224 | tf_op jit(solution)/shard_map/ppermute | solution.py:232
  102.3 7.7 %collective-permute-start.10 = (bf16[4,128,128]{2,1,0:T(8,128)(2,1)S(1)}, bf16[4,128,128]{2,1,0:T(8,128)(2,1)S(1)}, u32[]{:S(2)}, u32[]{:S(2)}) collective-permute-start(bf16[4,128,128]{2,1,0:T(8,128)(2,1)S(1)} %get-tuple-element.56), channel_id=1, source_target_pairs={{0,192},{64,0},{128,64},{192,128},{1,193},{65,1},{129,65},{193,129... | collective-permute-start | bytes 393224 | tf_op jit(solution)/shard_map/ppermute | solution.py:241

commit v7 on v6

--- a/solution.py
+++ b/solution.py
@@ -184,13 +184,14 @@
     lax.fori_loop(0, count, clear, 0, unroll=4)
     for load in loads:
         load.wait()
-    for slot in range(SLOTS):
-
-        @pl.when(need[0] > slot)
-        def _(slot=slot):
-            load_slot(slot).wait()
-
-    def terms(j, carry):
+    def arrive(slot, carry):
+        load_slot(slot).wait()
+        return carry
+
+    def terms(j, here):
+        last = picked[jnp.minimum((j + 1) * UNROLL, picked[0])]
+        wanted = (last % LANES) // size + 1
+        lax.fori_loop(here, wanted, arrive, 0)
         entries = [picked[1 + j * UNROLL + u] for u in range(UNROLL)]
         kept = [jnp.maximum(entry, 0) for entry in entries]
         numbers = [entry // LANES for entry in kept]
@@ -208,9 +209,12 @@
         ]
         for entry, t, image in zip(entries, numbers, images):
             acc[jnp.where(entry < 0, count, write_place(target[t]))] += image
-        return carry
-
-    lax.fori_loop(0, (picked[0] + UNROLL - 1) // UNROLL, terms, 0)
+        return jnp.maximum(here, wanted)
+
+    here = lax.fori_loop(
+        0, (picked[0] + UNROLL - 1) // UNROLL, terms, jnp.int32(0)
+    )
+    lax.fori_loop(here, need[0], arrive, 0)
 
     def finish(r, carry):
         for place, out in enumerate(

time: 112 us -> 181 us (1.62); the launches traced: 111 us -> 177 us
  blocking collectives: 41.1 us -> 109 us
    all_to_all x1, blocking collectives: 41.1 us -> 109 us  [run(): got = lax.all_to_all(packed[slots - 1], ENV, 0, 0, tiled=True)]
    pallas_call x1 -> x0, Pallas kernels: 2.21 us -> none  [run(): pl.pallas_call(place_kernel, out_shape=packing, in_specs=[pl.BlockSpec(me...]
  transfers between devices with their start and end apart: 13 -> 13, of which waited for: 4 -> 4; matrix products, arithmetic and copies ran while one was open for 1% -> 1% of each run, Pallas kernels for 7% -> 3%
where the time goes in v7:
time: 181 us; the launch traced here: 177 us
  blocking collectives  109 us (60%)
  starting transfers between devices  43 us (24%)
  Pallas kernels  10.9 us (6%)
  waiting for transfers between devices  10.3 us (6%)
  other arithmetic  2.88 us (2%)
    all_to_all x1, blocking collectives, run(): got = lax.all_to_all(packed[slots - 1], ENV, 0, 0, tiled=True)  109 us
    ppermute x6, starting transfers between devices, step_x(): return lax.ppermute(value, 'x', [(i, (i + step) % XS) for i in range(XS)])  22.3 us
    ppermute x6, starting transfers between devices, swap(): return lax.ppermute(value, axis, [(0, 1), (1, 0)])  17.2 us
    ppermute x6, waiting for transfers between devices, swap(): return lax.ppermute(value, axis, [(0, 1), (1, 0)])  7.53 us
    pallas_call x1, Pallas kernels, shards(): pl.pallas_call(apply_kernel, out_shape=[block] * 4, in_specs=[smem] * 5 +...  5.51 us
    pallas_call x1, Pallas kernels, shards(): pl.pallas_call(lambda *refs: pack_kernel(per, *refs), out_shape=(*[jax.Sh...  5.35 us
  transfers between devices with their start and end apart: 13, of which 4 were waited for; matrix products, arithmetic and copies ran while one was open for 1% of the time, Pallas kernels for 3%

profile of v7, /device:TPU:56, one launch (start us, length us, event | category | flops | bytes accessed | tf_op | source)
XLA Modules:
  0.0 177.0 jit_solution(3427354859834124091)
XLA Ops:
  0.0 4.7 %collective-permute-start = (bf16[4,128,128]{2,1,0:T(8,128)(2,1)}, bf16[4,128,128]{2,1,0:T(8,128)(2,1)S(1)}, u32[]{:S(2)}, u32[]{:S(2)}) collective-permute-start(bf16[4,128,128]{2,1,0:T(8,128)(2,1)} %bitcast.7), channel_id=1, source_target_pairs={{0,256},{256,0},{1,257},{257,1},{2,258},{258,2},{3,259},{259,3},{4... | collective-permute-start | bytes 393224 | tf_op jit(solution)/shard_map/ppermute | solution.py:236
  4.7 1.9 %collective-permute-start.1 = (bf16[4,128,128]{2,1,0:T(8,128)(2,1)}, bf16[4,128,128]{2,1,0:T(8,128)(2,1)S(1)}, u32[]{:S(2)}, u32[]{:S(2)}) collective-permute-start(bf16[4,128,128]{2,1,0:T(8,128)(2,1)} %bitcast.8), channel_id=1, source_target_pairs={{0,32},{32,0},{1,33},{33,1},{2,34},{34,2},{3,35},{35,3},{4,36},{36... | collective-permute-start | bytes 393224 | tf_op jit(solution)/shard_map/ppermute | solution.py:236
  6.6 5.3 %shard_map.82 = (bf16[32,128,128]{2,1,0:T(8,128)(2,1)}, bf16[64,128,128]{2,1,0:T(8,128)(2,1)}, bf16[96,128,128]{2,1,0:T(8,128)(2,1)}, bf16[128,128,128]{2,1,0:T(8,128)(2,1)}, s32[1]{0:T(128)}, /*index=5*/s32[529]{0:T(1024)}) custom-call(s32[512]{0:T(512)} %bitcast.10, s32[32]{0:T(128)} %refs_1_.1, s32[4,128]{1,0:T(4,128)} %bitcast.11, ...), custom_call_target="tpu_custom_call" | custom-call | bytes 8388608 | tf_op jit(solution)/shard_map/pallas_call | solution.py:286
  12.0 1.7 collective-permute-done
  13.7 1.9 %collective-permute-start.2 = (bf16[4,128,128]{2,1,0:T(8,128)(2,1)S(1)}, bf16[4,128,128]{2,1,0:T(8,128)(2,1)S(1)}, u32[]{:S(2)}, u32[]{:S(2)}) collective-permute-start(bf16[4,128,128]{2,1,0:T(8,128)(2,1)S(1)} %collective-permute-done), channel_id=1, source_target_pairs={{0,32},{32,0},{1,33},{33,1},{2,34},{34,2},{3,35},{35,3},{4,36},{36... | collective-permute-start | bytes 393224 | tf_op jit(solution)/shard_map/ppermute | solution.py:236
  15.6 1.3 collective-permute-done.2
  16.9 1.0 pad_maximum_fusion.part_0
  17.9 3.4 %collective-permute-start.3 = (bf16[16,128,128]{2,1,0:T(8,128)(2,1)S(1)}, bf16[16,128,128]{2,1,0:T(8,128)(2,1)S(1)}, u32[]{:S(2)}, u32[]{:S(2)}) collective-permute-start(bf16[16,128,128]{2,1,0:T(8,128)(2,1)S(1)} %pad_maximum_fusion.part_0), channel_id=1, source_target_pairs={{0,64},{64,128},{128,192},{192,0},{1,65},{65,129},{129,193},{193,1... | collective-permute-start | bytes 1572872 | tf_op jit(solution)/shard_map/ppermute | solution.py:245
  21.3 4.6 %collective-permute-start.4 = (bf16[16,128,128]{2,1,0:T(8,128)(2,1)S(1)}, bf16[16,128,128]{2,1,0:T(8,128)(2,1)S(1)}, u32[]{:S(2)}, u32[]{:S(2)}) collective-permute-start(bf16[16,128,128]{2,1,0:T(8,128)(2,1)S(1)} %pad_maximum_fusion.part_0), channel_id=1, source_target_pairs={{0,128},{64,192},{128,0},{192,64},{1,129},{65,193},{129,1},{193,65... | collective-permute-start | bytes 1572872 | tf_op jit(solution)/shard_map/ppermute | solution.py:245
  25.9 3.3 %collective-permute-start.5 = (bf16[16,128,128]{2,1,0:T(8,128)(2,1)S(1)}, bf16[16,128,128]{2,1,0:T(8,128)(2,1)S(1)}, u32[]{:S(2)}, u32[]{:S(2)}) collective-permute-start(bf16[16,128,128]{2,1,0:T(8,128)(2,1)S(1)} %pad_maximum_fusion.part_0), channel_id=1, source_target_pairs={{0,192},{64,0},{128,64},{192,128},{1,193},{65,1},{129,65},{193,129... | collective-permute-start | bytes 1572872 | tf_op jit(solution)/shard_map/ppermute | solution.py:245
  30.0 109.0 %conditional.1 = (bf16[128,128,128]{2,1,0:T(8,128)(2,1)}) conditional(s32[]{:T(128)} %bitcast.2, bf16[32,128,128]{2,1,0:T(8,128)(2,1)} %get-tuple-element.42, bf16[64,128,128]{2,1,0:T(8,128)(2,1)} %get-tuple-element.43, bf16[96,128,128]{2,1,0:T(8,128)(2,1)} %get-tuple-element.44, ...), branch_computations={%region_0.0_spmd, %region_1.0_spmd, %region_2.0_spmd, %region_3.0_... | conditional | bytes 8388616 | solution.py:307
  30.0 109.0 %all_to_all.24 = bf16[128,128,128]{2,1,0:T(8,128)(2,1)} all-to-all(bf16[128,128,128]{2,1,0:T(8,128)(2,1)} %param.3), channel_id=1, replica_groups=mesh['y_hi'=2,'x'=4,'core'=2,'z'=8,'y_lo'=4] {'z','y_lo'}, dimensions={0} | all-to-all | bytes 8388608 | tf_op jit(solution)/shard_map/cond/branch_3_fun/all_to_all | solution.py:250
  139.0 5.5 %shard_map.83 = (bf16[16,128,128]{2,1,0:T(8,128)(2,1)S(1)}, bf16[16,128,128]{2,1,0:T(8,128)(2,1)S(1)}, bf16[16,128,128]{2,1,0:T(8,128)(2,1)}, bf16[16,128,128]{2,1,0:T(8,128)(2,1)S(1)}) custom-call(s32[512]{0:T(512)S(1)} %copy-done.2, s32[512]{0:T(512)S(1)} %copy-done.3, s32[512]{0:T(512)S(1)} %copy-done.4, s32[529]{0:T(1024)S(1)} %copy-done.1, ...), custom_call_target="tpu_custom_call" | custom-call | tf_op jit(solution)/shard_map/pallas_call | solution.py:313
  144.6 1.9 %collective-permute-start.9 = (bf16[16,128,128]{2,1,0:T(8,128)(2,1)S(1)}, bf16[16,128,128]{2,1,0:T(8,128)(2,1)S(1)}, u32[]{:S(2)}, u32[]{:S(2)}) collective-permute-start(bf16[16,128,128]{2,1,0:T(8,128)(2,1)S(1)} %get-tuple-element.55), channel_id=1, source_target_pairs={{0,32},{32,0},{1,33},{33,1},{2,34},{34,2},{3,35},{35,3},{4,36},{36... | collective-permute-start | bytes 1572872 | tf_op jit(solution)/shard_map/ppermute | solution.py:236
  146.5 2.4 %collective-permute-start.6 = (bf16[16,128,128]{2,1,0:T(8,128)(2,1)}, bf16[16,128,128]{2,1,0:T(8,128)(2,1)S(1)}, u32[]{:S(2)}, u32[]{:S(2)}) collective-permute-start(bf16[16,128,128]{2,1,0:T(8,128)(2,1)} %get-tuple-element.53), channel_id=1, source_target_pairs={{0,32},{32,0},{1,33},{33,1},{2,34},{34,2},{3,35},{35,3},{4,36},{36... | collective-permute-start | bytes 1572872 | tf_op jit(solution)/shard_map/ppermute | solution.py:236
  148.9 0.9 add_convert_fusion
  149.9 3.5 %all-to-all-start.4 = ((bf16[16,128,128]{2,1,0:T(8,128)(2,1)}), bf16[16,128,128]{2,1,0:T(8,128)(2,1)S(1)}, u32[]{:S(2)}, u32[]{:S(2)}) async-start(bf16[16,128,128]{2,1,0:T(8,128)(2,1)} %add_convert_fusion), calls=%async_computation.4 | async-start | bytes 1048576 | tf_op jit(solution)/shard_map/all_to_all | solution.py:336
  153.5 5.4 %collective-permute-start.8 = (bf16[4,128,128]{2,1,0:T(8,128)(2,1)S(1)}, bf16[4,128,128]{2,1,0:T(8,128)(2,1)S(1)}, u32[]{:S(2)}, u32[]{:S(2)}) collective-permute-start(bf16[4,128,128]{2,1,0:T(8,128)(2,1)S(1)} %get-tuple-element.60), channel_id=1, source_target_pairs={{0,128},{64,192},{128,0},{192,64},{1,129},{65,193},{129,1},{193,65... | collective-permute-start | bytes 393224 | tf_op jit(solution)/shard_map/ppermute | solution.py:245
  158.9 2.5 %collective-permute-start.7 = (bf16[4,128,128]{2,1,0:T(8,128)(2,1)S(1)}, bf16[4,128,128]{2,1,0:T(8,128)(2,1)S(1)}, u32[]{:S(2)}, u32[]{:S(2)}) collective-permute-start(bf16[4,128,128]{2,1,0:T(8,128)(2,1)S(1)} %get-tuple-element.58), channel_id=1, source_target_pairs={{0,64},{64,128},{128,192},{192,0},{1,65},{65,129},{129,193},{193,1... | collective-permute-start | bytes 393224 | tf_op jit(solution)/shard_map/ppermute | solution.py:245
  161.4 2.8 %all-to-all-done.4 = bf16[16,128,128]{2,1,0:T(8,128)(2,1)S(1)} async-done(((bf16[16,128,128]{2,1,0:T(8,128)(2,1)}), bf16[16,128,128]{2,1,0:T(8,128)(2,1)S(1)}, u32[]{:S(2)}, u32[]{:S(2)}) %all-to-all-start.4) | async-done | bytes 524320 | tf_op jit(solution)/shard_map/all_to_all | solution.py:336
  164.3 4.4 %collective-permute-start.11 = (bf16[4,128,128]{2,1,0:T(8,128)(2,1)S(1)}, bf16[4,128,128]{2,1,0:T(8,128)(2,1)S(1)}, u32[]{:S(2)}, u32[]{:S(2)}) collective-permute-start(bf16[4,128,128]{2,1,0:T(8,128)(2,1)S(1)} %reduce_sum.12), channel_id=1, source_target_pairs={{0,256},{256,0},{1,257},{257,1},{2,258},{258,2},{3,259},{259,3},{4... | collective-permute-start | bytes 393224 | tf_op jit(solution)/shard_map/ppermute | solution.py:236
  168.6 3.1 %collective-permute-start.10 = (bf16[4,128,128]{2,1,0:T(8,128)(2,1)S(1)}, bf16[4,128,128]{2,1,0:T(8,128)(2,1)S(1)}, u32[]{:S(2)}, u32[]{:S(2)}) collective-permute-start(bf16[4,128,128]{2,1,0:T(8,128)(2,1)S(1)} %get-tuple-element.56), channel_id=1, source_target_pairs={{0,192},{64,0},{128,64},{192,128},{1,193},{65,1},{129,65},{193,129... | collective-permute-start | bytes 393224 | tf_op jit(solution)/shard_map/ppermute | solution.py:245
  171.7 4.5 %collective-permute-done.11 = bf16[4,128,128]{2,1,0:T(8,128)(2,1)S(1)} collective-permute-done((bf16[4,128,128]{2,1,0:T(8,128)(2,1)S(1)}, bf16[4,128,128]{2,1,0:T(8,128)(2,1)S(1)}, u32[]{:S(2)}, u32[]{:S(2)}) %collective-permute-start.11) | collective-permute-done | bytes 131104 | tf_op jit(solution)/shard_map/ppermute | solution.py:236
  176.3 0.7 add_convert_fusion.2
  (22 shorter events, 0.3 us)
Async XLA Ops:
  0.0 13.7 %collective-permute-start = (bf16[4,128,128]{2,1,0:T(8,128)(2,1)}, bf16[4,128,128]{2,1,0:T(8,128)(2,1)S(1)}, u32[]{:S(2)}, u32[]{:S(2)}) collective-permute-start(bf16[4,128,128]{2,1,0:T(8,128)(2,1)} %bitcast.7), channel_id=1, source_target_pairs={{0,256},{256,0},{1,257},{257,1},{2,258},{258,2},{3,259},{259,3},{4... | collective-permute-start | bytes 393224 | tf_op jit(solution)/shard_map/ppermute | solution.py:236
  4.7 10.9 %collective-permute-start.1 = (bf16[4,128,128]{2,1,0:T(8,128)(2,1)}, bf16[4,128,128]{2,1,0:T(8,128)(2,1)S(1)}, u32[]{:S(2)}, u32[]{:S(2)}) collective-permute-start(bf16[4,128,128]{2,1,0:T(8,128)(2,1)} %bitcast.8), channel_id=1, source_target_pairs={{0,32},{32,0},{1,33},{33,1},{2,34},{34,2},{3,35},{35,3},{4,36},{36... | collective-permute-start | bytes 393224 | tf_op jit(solution)/shard_map/ppermute | solution.py:236
  13.7 3.2 %collective-permute-start.2 = (bf16[4,128,128]{2,1,0:T(8,128)(2,1)S(1)}, bf16[4,128,128]{2,1,0:T(8,128)(2,1)S(1)}, u32[]{:S(2)}, u32[]{:S(2)}) collective-permute-start(bf16[4,128,128]{2,1,0:T(8,128)(2,1)S(1)} %collective-permute-done), channel_id=1, source_target_pairs={{0,32},{32,0},{1,33},{33,1},{2,34},{34,2},{3,35},{35,3},{4,36},{36... | collective-permute-start | bytes 393224 | tf_op jit(solution)/shard_map/ppermute | solution.py:236
  17.9 121.1 %collective-permute-start.3 = (bf16[16,128,128]{2,1,0:T(8,128)(2,1)S(1)}, bf16[16,128,128]{2,1,0:T(8,128)(2,1)S(1)}, u32[]{:S(2)}, u32[]{:S(2)}) collective-permute-start(bf16[16,128,128]{2,1,0:T(8,128)(2,1)S(1)} %pad_maximum_fusion.part_0), channel_id=1, source_target_pairs={{0,64},{64,128},{128,192},{192,0},{1,65},{65,129},{129,193},{193,1... | collective-permute-start | bytes 1572872 | tf_op jit(solution)/shard_map/ppermute | solution.py:245
  21.3 117.7 %collective-permute-start.4 = (bf16[16,128,128]{2,1,0:T(8,128)(2,1)S(1)}, bf16[16,128,128]{2,1,0:T(8,128)(2,1)S(1)}, u32[]{:S(2)}, u32[]{:S(2)}) collective-permute-start(bf16[16,128,128]{2,1,0:T(8,128)(2,1)S(1)} %pad_maximum_fusion.part_0), channel_id=1, source_target_pairs={{0,128},{64,192},{128,0},{192,64},{1,129},{65,193},{129,1},{193,65... | collective-permute-start | bytes 1572872 | tf_op jit(solution)/shard_map/ppermute | solution.py:245
  25.9 113.0 %collective-permute-start.5 = (bf16[16,128,128]{2,1,0:T(8,128)(2,1)S(1)}, bf16[16,128,128]{2,1,0:T(8,128)(2,1)S(1)}, u32[]{:S(2)}, u32[]{:S(2)}) collective-permute-start(bf16[16,128,128]{2,1,0:T(8,128)(2,1)S(1)} %pad_maximum_fusion.part_0), channel_id=1, source_target_pairs={{0,192},{64,0},{128,64},{192,128},{1,193},{65,1},{129,65},{193,129... | collective-permute-start | bytes 1572872 | tf_op jit(solution)/shard_map/ppermute | solution.py:245
  29.9 109.1 %copy-start = (bf16[26,128,128]{2,1,0:T(8,128)(2,1)S(1)}, bf16[26,128,128]{2,1,0:T(8,128)(2,1)}, u32[]{:S(2)}) copy-start(bf16[26,128,128]{2,1,0:T(8,128)(2,1)} %rights.1) | copy-start | bytes 2555908
  29.9 109.1 %copy-start.1 = (s32[529]{0:T(1024)S(1)}, s32[529]{0:T(1024)}, u32[]{:S(2)}) copy-start(s32[529]{0:T(1024)} %get-tuple-element.36.picked) | copy-start | bytes 6352
  30.0 109.1 %copy-start.2 = (s32[512]{0:T(512)S(1)}, s32[512]{0:T(512)}, u32[]{:S(2)}) copy-start(s32[512]{0:T(512)} %source.1) | copy-start | bytes 6148
  30.0 109.1 %copy-start.3 = (s32[512]{0:T(512)S(1)}, s32[512]{0:T(512)}, u32[]{:S(2)}) copy-start(s32[512]{0:T(512)} %target.1) | copy-start | bytes 6148
  30.0 109.1 %copy-start.4 = (s32[512]{0:T(512)S(1)}, s32[512]{0:T(512)}, u32[]{:S(2)}) copy-start(s32[512]{0:T(512)} %index.1) | copy-start | bytes 6148
  144.6 4.3 %collective-permute-start.9 = (bf16[16,128,128]{2,1,0:T(8,128)(2,1)S(1)}, bf16[16,128,128]{2,1,0:T(8,128)(2,1)S(1)}, u32[]{:S(2)}, u32[]{:S(2)}) collective-permute-start(bf16[16,128,128]{2,1,0:T(8,128)(2,1)S(1)} %get-tuple-element.55), channel_id=1, source_target_pairs={{0,32},{32,0},{1,33},{33,1},{2,34},{34,2},{3,35},{35,3},{4,36},{36... | collective-permute-start | bytes 1572872 | tf_op jit(solution)/shard_map/ppermute | solution.py:236
  146.5 6.8 %collective-permute-start.6 = (bf16[16,128,128]{2,1,0:T(8,128)(2,1)}, bf16[16,128,128]{2,1,0:T(8,128)(2,1)S(1)}, u32[]{:S(2)}, u32[]{:S(2)}) collective-permute-start(bf16[16,128,128]{2,1,0:T(8,128)(2,1)} %get-tuple-element.53), channel_id=1, source_target_pairs={{0,32},{32,0},{1,33},{33,1},{2,34},{34,2},{3,35},{35,3},{4,36},{36... | collective-permute-start | bytes 1572872 | tf_op jit(solution)/shard_map/ppermute | solution.py:236
  149.9 14.3 %all-to-all-start.4 = ((bf16[16,128,128]{2,1,0:T(8,128)(2,1)}), bf16[16,128,128]{2,1,0:T(8,128)(2,1)S(1)}, u32[]{:S(2)}, u32[]{:S(2)}) async-start(bf16[16,128,128]{2,1,0:T(8,128)(2,1)} %add_convert_fusion), calls=%async_computation.4 | async-start | bytes 1048576 | tf_op jit(solution)/shard_map/all_to_all | solution.py:336
  153.5 18.2 %collective-permute-start.8 = (bf16[4,128,128]{2,1,0:T(8,128)(2,1)S(1)}, bf16[4,128,128]{2,1,0:T(8,128)(2,1)S(1)}, u32[]{:S(2)}, u32[]{:S(2)}) collective-permute-start(bf16[4,128,128]{2,1,0:T(8,128)(2,1)S(1)} %get-tuple-element.60), channel_id=1, source_target_pairs={{0,128},{64,192},{128,0},{192,64},{1,129},{65,193},{129,1},{193,65... | collective-permute-start | bytes 393224 | tf_op jit(solution)/shard_map/ppermute | solution.py:245
  158.9 12.8 %collective-permute-start.7 = (bf16[4,128,128]{2,1,0:T(8,128)(2,1)S(1)}, bf16[4,128,128]{2,1,0:T(8,128)(2,1)S(1)}, u32[]{:S(2)}, u32[]{:S(2)}) collective-permute-start(bf16[4,128,128]{2,1,0:T(8,128)(2,1)S(1)} %get-tuple-element.58), channel_id=1, source_target_pairs={{0,64},{64,128},{128,192},{192,0},{1,65},{65,129},{129,193},{193,1... | collective-permute-start | bytes 393224 | tf_op jit(solution)/shard_map/ppermute | solution.py:245
  164.3 12.0 %collective-permute-start.11 = (bf16[4,128,128]{2,1,0:T(8,128)(2,1)S(1)}, bf16[4,128,128]{2,1,0:T(8,128)(2,1)S(1)}, u32[]{:S(2)}, u32[]{:S(2)}) collective-permute-start(bf16[4,128,128]{2,1,0:T(8,128)(2,1)S(1)} %reduce_sum.12), channel_id=1, source_target_pairs={{0,256},{256,0},{1,257},{257,1},{2,258},{258,2},{3,259},{259,3},{4... | collective-permute-start | bytes 393224 | tf_op jit(solution)/shard_map/ppermute | solution.py:236
  168.6 7.6 %collective-permute-start.10 = (bf16[4,128,128]{2,1,0:T(8,128)(2,1)S(1)}, bf16[4,128,128]{2,1,0:T(8,128)(2,1)S(1)}, u32[]{:S(2)}, u32[]{:S(2)}) collective-permute-start(bf16[4,128,128]{2,1,0:T(8,128)(2,1)S(1)} %get-tuple-element.56), channel_id=1, source_target_pairs={{0,192},{64,0},{128,64},{192,128},{1,193},{65,1},{129,65},{193,129... | collective-permute-start | bytes 393224 | tf_op jit(solution)/shard_map/ppermute | solution.py:245

commit v8 on v7

--- a/solution.py
+++ b/solution.py
@@ -20,10 +20,39 @@
     return lax.axis_index("z") * LOW + lax.axis_index("y_lo")
 
 
+def split(row):
+    return row >> 5, row >> 3 & 3, row >> 2 & 1, row & 3
+
+
+def read_place(row):
+    half_at, x_at, _ = (lax.axis_index(a) for a in GRP)
+    y, x, core, rest = split(row)
+    return (x_at - x & 3) << 4 | core << 3 | (y ^ half_at) << 2 | rest
+
+
+def write_place(row):
+    half_at, x_at, core_at = (lax.axis_index(a) for a in GRP)
+    y, x, core, rest = split(row)
+    y = y ^ half_at
+    x = jnp.where(y == 0, x - x_at & 3, x)
+    return (core ^ core_at) << 5 | y << 4 | x << 2 | rest
+
+
+def word_of(slot, index, row, block):
+    return slot | index << 7 | row << 12 | block << 19
+
+
+def parts_of(word):
+    return word & 127, word >> 7 & 31, word >> 12 & 127, word >> 19
+
+
 def pack_kernel(
     per,
     sector,
     column,
+    source,
+    target,
+    index,
     sector_rows,
     tiles,
     out_1,
@@ -108,9 +137,18 @@
         return n
 
     n = lax.fori_loop(0, sector.shape[0] // per, scan, jnp.int32(1))
+    spare = HALVES * XS * CORES * ROWS_DEV
     for j in range(UNROLL):
-        picked[n + j] = -1
+        picked[n + j] = word_of(0, 0, spare, 0)
     picked[0] = n - 1
+
+    def resolve(j, carry):
+        t = picked[j] >> 7
+        row, block = write_place(target[t]), read_place(source[t])
+        picked[j] = word_of(picked[j] & 127, index[t], row, block)
+        return carry
+
+    lax.fori_loop(1, n, resolve, 0)
 
     def finish(j, carry):
         move(0, out_1, started[j], 0).wait()
@@ -120,9 +158,6 @@
 
 
 def apply_kernel(
-    source,
-    target,
-    index,
     picked,
     need,
     tiles,
@@ -158,24 +193,8 @@
         loads.append(pltpu.make_async_copy(part, at, copied.at[x]))
     for load in loads:
         load.start()
-    half_at, x_at, core_at = (lax.axis_index(a) for a in GRP)
     quarter = out_stay.shape[0]
     count = 4 * quarter
-
-    def read_place(row):
-        group = row // ROWS_DEV
-        core = (group % CORES) ^ core_at
-        x = (x_at - (group // CORES) % XS + XS) % XS
-        y = group // (CORES * XS) ^ half_at
-        return ((x * CORES + core) * HALVES + y) * ROWS_DEV + row % ROWS_DEV
-
-    def write_place(row):
-        group = row // ROWS_DEV
-        core = (group % CORES) ^ core_at
-        y = group // (CORES * XS) ^ half_at
-        x = (group // CORES) % XS
-        x = jnp.where(y == 0, (x - x_at + XS) % XS, x)
-        return ((core * HALVES + y) * XS + x) * ROWS_DEV + row % ROWS_DEV
 
     def clear(r, carry):
         acc[r] = jnp.zeros(acc.shape[1:], acc.dtype)
@@ -184,31 +203,28 @@
     lax.fori_loop(0, count, clear, 0, unroll=4)
     for load in loads:
         load.wait()
+
     def arrive(slot, carry):
         load_slot(slot).wait()
         return carry
 
     def terms(j, here):
         last = picked[jnp.minimum((j + 1) * UNROLL, picked[0])]
-        wanted = (last % LANES) // size + 1
+        wanted = lax.div(parts_of(last)[0], jnp.int32(size)) + 1
         lax.fori_loop(here, wanted, arrive, 0)
-        entries = [picked[1 + j * UNROLL + u] for u in range(UNROLL)]
-        kept = [jnp.maximum(entry, 0) for entry in entries]
-        numbers = [entry // LANES for entry in kept]
+        words = [parts_of(picked[1 + j * UNROLL + u]) for u in range(UNROLL)]
         products = [
             jnp.dot(
-                held[entry % LANES],
-                blocks[read_place(source[t])],
-                preferred_element_type=jnp.float32,
+                held[slot], blocks[block], preferred_element_type=jnp.float32
             ).astype(jnp.bfloat16)
-            for entry, t in zip(kept, numbers)
+            for slot, _, _, block in words
         ]
         images = [
-            jnp.dot(product, rights[index[t]], preferred_element_type=jnp.float32)
-            for product, t in zip(products, numbers)
+            jnp.dot(product, rights[tile], preferred_element_type=jnp.float32)
+            for product, (_, tile, _, _) in zip(products, words)
         ]
-        for entry, t, image in zip(entries, numbers, images):
-            acc[jnp.where(entry < 0, count, write_place(target[t]))] += image
+        for (_, _, row, _), image in zip(words, images):
+            acc[row] += image
         return jnp.maximum(here, wanted)
 
     here = lax.fori_loop(
@@ -282,7 +298,6 @@
 
     psi = wavefunction.reshape(-1, size, size)
     across = swap(psi, "y_hi")
-    beside = swap(psi, "core")
     *packed, need, picked = pl.pallas_call(
         lambda *refs: pack_kernel(per, *refs),
         out_shape=(
@@ -293,16 +308,25 @@
             jax.ShapeDtypeStruct((1,), jnp.int32),
             jax.ShapeDtypeStruct((sectors.shape[0] + 1 + UNROLL,), jnp.int32),
         ),
-        in_specs=[smem, smem, vmem, vmem],
+        in_specs=[smem] * 5 + [vmem] * 2,
         out_specs=(*[anywhere] * SLOTS, smem, smem),
         scratch_shapes=[pltpu.SMEM((columns,), jnp.int32)] * 3
         + [pltpu.SMEM((slots,), jnp.int32), pltpu.SemaphoreType.DMA((slots,))],
         cost_estimate=pl.CostEstimate(
             flops=0, bytes_accessed=8 * 2**20, transcendentals=0
         ),
-    )(sectors, column_sector, sectors.reshape(-1, LANES), left_tiles)
+    )(
+        sectors,
+        column_sector,
+        term_source,
+        term_target,
+        right_index,
+        sectors.reshape(-1, LANES),
+        left_tiles,
+    )
     packed, across = lax.optimization_barrier((packed, across))
-    quad = jnp.concatenate([psi, across, beside, swap(across, "core")])
+    pair = jnp.concatenate([psi, across])
+    quad = lax.all_gather(pair, "core", axis=0, tiled=True)
     parts = [quad] + [step_x(quad, step) for step in range(1, XS)]
     tiles = lax.switch(
         need[0] - 1, [exchange(k + 1, packing) for k in range(SLOTS)], *packed
@@ -313,7 +337,7 @@
     stay, cross, other_stay, other_cross = pl.pallas_call(
         apply_kernel,
         out_shape=[block] * 4,
-        in_specs=[smem] * 5 + [anywhere] * (1 + XS) + [vmem],
+        in_specs=[smem] * 2 + [anywhere] * (1 + XS) + [vmem],
         out_specs=[vmem] * 4,
         scratch_shapes=[
             pltpu.VMEM(packing.shape, jnp.bfloat16),
@@ -323,9 +347,6 @@
         ],
         compiler_params=pltpu.CompilerParams(vmem_limit_bytes=40 * 2**20),
     )(
-        term_source,
-        term_target,
-        right_index,
         picked,
         need,
         tiles,

time: 181 us -> 178 us (0.983); the launches traced: 177 us -> 177 us
  starting transfers between devices: 43 us -> 37.8 us
  waiting for transfers between devices: 10.3 us -> 13.7 us
  blocking collectives: 109 us -> 111 us
    ppermute x6 -> x4, starting transfers between devices: 17.2 us -> 13.5 us  [swap(): return lax.ppermute(value, axis, [(0, 1), (1, 0)])]
    ppermute x6 -> x4, waiting for transfers between devices: 7.53 us -> 11.1 us  [swap(): return lax.ppermute(value, axis, [(0, 1), (1, 0)])]
    all_gather x0 -> x1, blocking collectives: none -> 2.18 us  [shards(): quad = lax.all_gather(pair, 'core', axis=0, tiled=True)]
  transfers between devices with their start and end apart: 13 -> 11, of which waited for: 4 -> 4; matrix products, arithmetic and copies ran while one was open for 1% -> 1% of each run, Pallas kernels for 3% -> 3%
where the time goes in v8:
time: 178 us; the launch traced here: 177 us
  blocking collectives  111 us (62%)
  starting transfers between devices  37.8 us (21%)
  waiting for transfers between devices  13.7 us (8%)
  Pallas kernels  10.7 us (6%)
  other arithmetic  2.84 us (2%)
    all_to_all x1, blocking collectives, run(): got = lax.all_to_all(packed[slots - 1], ENV, 0, 0, tiled=True)  109 us
    ppermute x6, starting transfers between devices, step_x(): return lax.ppermute(value, 'x', [(i, (i + step) % XS) for i in range(XS)])  20.7 us
    ppermute x4, starting transfers between devices, swap(): return lax.ppermute(value, axis, [(0, 1), (1, 0)])  13.5 us
    ppermute x4, waiting for transfers between devices, swap(): return lax.ppermute(value, axis, [(0, 1), (1, 0)])  11.1 us
    pallas_call x1, Pallas kernels, shards(): pl.pallas_call(lambda *refs: pack_kernel(per, *refs), out_shape=(*[jax.Sh...  5.79 us
    pallas_call x1, Pallas kernels, shards(): pl.pallas_call(apply_kernel, out_shape=[block] * 4, in_specs=[smem] * 2 +...  4.94 us
    all_to_all x1, starting transfers between devices, shards(): cross = lax.all_to_all(cross, 'x', 0, 0, tiled=True)  3.62 us
  transfers between devices with their start and end apart: 11, of which 4 were waited for; matrix products, arithmetic and copies ran while one was open for 1% of the time, Pallas kernels for 3%

profile of v8, /device:TPU:56, one launch (start us, length us, event | category | flops | bytes accessed | tf_op | source)
XLA Modules:
  0.0 177.3 jit_solution(10994919463659550221)
XLA Ops:
  0.0 4.7 %collective-permute-start = (bf16[4,128,128]{2,1,0:T(8,128)(2,1)}, bf16[4,128,128]{2,1,0:T(8,128)(2,1)S(1)}, u32[]{:S(2)}, u32[]{:S(2)}) collective-permute-start(bf16[4,128,128]{2,1,0:T(8,128)(2,1)} %bitcast.7), channel_id=1, source_target_pairs={{0,256},{256,0},{1,257},{257,1},{2,258},{258,2},{3,259},{259,3},{4... | collective-permute-start | bytes 393224 | tf_op jit(solution)/shard_map/ppermute | solution.py:252
  4.7 5.8 %shard_map.82 = (bf16[32,128,128]{2,1,0:T(8,128)(2,1)}, bf16[64,128,128]{2,1,0:T(8,128)(2,1)}, bf16[96,128,128]{2,1,0:T(8,128)(2,1)}, bf16[128,128,128]{2,1,0:T(8,128)(2,1)}, s32[1]{0:T(128)}, /*index=5*/s32[529]{0:T(1024)}) custom-call(s32[512]{0:T(512)} %bitcast.9, s32[32]{0:T(128)} %refs_1_.1, s32[512]{0:T(512)} %refs_2_.1, s32[512]{0:T(512)} %refs_3_.1, ...), custom_call_target="tpu_custom_call" | custom-call | bytes 8388608 | tf_op jit(solution)/shard_map/pallas_call | solution.py:301
  10.5 3.2 %collective-permute-done = bf16[4,128,128]{2,1,0:T(8,128)(2,1)S(1)} collective-permute-done((bf16[4,128,128]{2,1,0:T(8,128)(2,1)}, bf16[4,128,128]{2,1,0:T(8,128)(2,1)S(1)}, u32[]{:S(2)}, u32[]{:S(2)}) %collective-permute-start) | collective-permute-done | bytes 131104 | tf_op jit(solution)/shard_map/ppermute | solution.py:252
  13.7 0.9 pad_maximum_fusion
  14.6 2.2 %all_gather.3.part_0 = bf16[16,128,128]{2,1,0:T(8,128)(2,1)S(1)} all-gather(bf16[8,128,128]{2,1,0:T(8,128)(2,1)S(1)} %pad_maximum_fusion), channel_id=1, replica_groups=mesh['y_hi'=2,'x'=4,'core'=2,'z'=8,'y_lo'=4] {'core'}, dimensions={0}, use_global_device_ids=true | all-gather | bytes 786432 | tf_op jit(solution)/shard_map/all_gather | solution.py:329
  16.8 4.7 %collective-permute-start.3 = (bf16[16,128,128]{2,1,0:T(8,128)(2,1)S(1)}, bf16[16,128,128]{2,1,0:T(8,128)(2,1)S(1)}, u32[]{:S(2)}, u32[]{:S(2)}) collective-permute-start(bf16[16,128,128]{2,1,0:T(8,128)(2,1)S(1)} %all_gather.3.part_0), channel_id=1, source_target_pairs={{0,192},{64,0},{128,64},{192,128},{1,193},{65,1},{129,65},{193,129... | collective-permute-start | bytes 1572872 | tf_op jit(solution)/shard_map/ppermute | solution.py:261
  21.5 2.7 %collective-permute-start.2 = (bf16[16,128,128]{2,1,0:T(8,128)(2,1)S(1)}, bf16[16,128,128]{2,1,0:T(8,128)(2,1)S(1)}, u32[]{:S(2)}, u32[]{:S(2)}) collective-permute-start(bf16[16,128,128]{2,1,0:T(8,128)(2,1)S(1)} %all_gather.3.part_0), channel_id=1, source_target_pairs={{0,128},{64,192},{128,0},{192,64},{1,129},{65,193},{129,1},{193,65... | collective-permute-start | bytes 1572872 | tf_op jit(solution)/shard_map/ppermute | solution.py:261
  24.2 2.8 %collective-permute-start.1 = (bf16[16,128,128]{2,1,0:T(8,128)(2,1)S(1)}, bf16[16,128,128]{2,1,0:T(8,128)(2,1)S(1)}, u32[]{:S(2)}, u32[]{:S(2)}) collective-permute-start(bf16[16,128,128]{2,1,0:T(8,128)(2,1)S(1)} %all_gather.3.part_0), channel_id=1, source_target_pairs={{0,64},{64,128},{128,192},{192,0},{1,65},{65,129},{129,193},{193,1... | collective-permute-start | bytes 1572872 | tf_op jit(solution)/shard_map/ppermute | solution.py:261
  27.6 109.3 %conditional.1 = (bf16[128,128,128]{2,1,0:T(8,128)(2,1)}) conditional(s32[]{:T(128)} %bitcast.2, bf16[32,128,128]{2,1,0:T(8,128)(2,1)} %get-tuple-element.42, bf16[64,128,128]{2,1,0:T(8,128)(2,1)} %get-tuple-element.43, bf16[96,128,128]{2,1,0:T(8,128)(2,1)} %get-tuple-element.44, ...), branch_computations={%region_0.0_spmd, %region_1.0_spmd, %region_2.0_spmd, %region_3.0_... | conditional | bytes 8388616 | solution.py:331
  27.7 109.2 %all_to_all.24 = bf16[128,128,128]{2,1,0:T(8,128)(2,1)} all-to-all(bf16[128,128,128]{2,1,0:T(8,128)(2,1)} %param.3), channel_id=1, replica_groups=mesh['y_hi'=2,'x'=4,'core'=2,'z'=8,'y_lo'=4] {'z','y_lo'}, dimensions={0} | all-to-all | bytes 8388608 | tf_op jit(solution)/shard_map/cond/branch_3_fun/all_to_all | solution.py:266
  136.9 4.9 %shard_map.83 = (bf16[16,128,128]{2,1,0:T(8,128)(2,1)S(1)}, bf16[16,128,128]{2,1,0:T(8,128)(2,1)S(1)}, bf16[16,128,128]{2,1,0:T(8,128)(2,1)}, bf16[16,128,128]{2,1,0:T(8,128)(2,1)S(1)}) custom-call(s32[529]{0:T(1024)S(1)} %copy-done.1, s32[1]{0:T(128)} %get-tuple-element.37.need, bf16[128,128,128]{2,1,0:T(8,128)(2,1)} %get-tuple-element.61.tiles, ...), custom_call_target="tpu_custom_call" | custom-call | tf_op jit(solution)/shard_map/pallas_call | solution.py:337
  141.9 1.9 %collective-permute-start.7 = (bf16[16,128,128]{2,1,0:T(8,128)(2,1)S(1)}, bf16[16,128,128]{2,1,0:T(8,128)(2,1)S(1)}, u32[]{:S(2)}, u32[]{:S(2)}) collective-permute-start(bf16[16,128,128]{2,1,0:T(8,128)(2,1)S(1)} %get-tuple-element.55), channel_id=1, source_target_pairs={{0,32},{32,0},{1,33},{33,1},{2,34},{34,2},{3,35},{35,3},{4,36},{36... | collective-permute-start | bytes 1572872 | tf_op jit(solution)/shard_map/ppermute | solution.py:252
  143.8 2.4 %collective-permute-start.4 = (bf16[16,128,128]{2,1,0:T(8,128)(2,1)}, bf16[16,128,128]{2,1,0:T(8,128)(2,1)S(1)}, u32[]{:S(2)}, u32[]{:S(2)}) collective-permute-start(bf16[16,128,128]{2,1,0:T(8,128)(2,1)} %get-tuple-element.53), channel_id=1, source_target_pairs={{0,32},{32,0},{1,33},{33,1},{2,34},{34,2},{3,35},{35,3},{4,36},{36... | collective-permute-start | bytes 1572872 | tf_op jit(solution)/shard_map/ppermute | solution.py:252
  146.2 0.9 add_convert_fusion
  147.2 3.6 %all-to-all-start.4 = ((bf16[16,128,128]{2,1,0:T(8,128)(2,1)}), bf16[16,128,128]{2,1,0:T(8,128)(2,1)S(1)}, u32[]{:S(2)}, u32[]{:S(2)}) async-start(bf16[16,128,128]{2,1,0:T(8,128)(2,1)} %add_convert_fusion), calls=%async_computation.4 | async-start | bytes 1048576 | tf_op jit(solution)/shard_map/all_to_all | solution.py:357
  150.8 0.1 add_convert_fusion.1
  151.0 3.9 %collective-permute-start.5 = (bf16[4,128,128]{2,1,0:T(8,128)(2,1)S(1)}, bf16[4,128,128]{2,1,0:T(8,128)(2,1)S(1)}, u32[]{:S(2)}, u32[]{:S(2)}) collective-permute-start(bf16[4,128,128]{2,1,0:T(8,128)(2,1)S(1)} %get-tuple-element.58), channel_id=1, source_target_pairs={{0,64},{64,128},{128,192},{192,0},{1,65},{65,129},{129,193},{193,1... | collective-permute-start | bytes 393224 | tf_op jit(solution)/shard_map/ppermute | solution.py:261
  154.9 4.6 %collective-permute-start.6 = (bf16[4,128,128]{2,1,0:T(8,128)(2,1)S(1)}, bf16[4,128,128]{2,1,0:T(8,128)(2,1)S(1)}, u32[]{:S(2)}, u32[]{:S(2)}) collective-permute-start(bf16[4,128,128]{2,1,0:T(8,128)(2,1)S(1)} %get-tuple-element.60), channel_id=1, source_target_pairs={{0,128},{64,192},{128,0},{192,64},{1,129},{65,193},{129,1},{193,65... | collective-permute-start | bytes 393224 | tf_op jit(solution)/shard_map/ppermute | solution.py:261
  159.5 2.2 %all-to-all-done.4 = bf16[16,128,128]{2,1,0:T(8,128)(2,1)S(1)} async-done(((bf16[16,128,128]{2,1,0:T(8,128)(2,1)}), bf16[16,128,128]{2,1,0:T(8,128)(2,1)S(1)}, u32[]{:S(2)}, u32[]{:S(2)}) %all-to-all-start.4) | async-done | bytes 524320 | tf_op jit(solution)/shard_map/all_to_all | solution.py:357
  161.8 2.0 %collective-permute-start.8 = (bf16[4,128,128]{2,1,0:T(8,128)(2,1)S(1)}, bf16[4,128,128]{2,1,0:T(8,128)(2,1)S(1)}, u32[]{:S(2)}, u32[]{:S(2)}) collective-permute-start(bf16[4,128,128]{2,1,0:T(8,128)(2,1)S(1)} %get-tuple-element.56), channel_id=1, source_target_pairs={{0,192},{64,0},{128,64},{192,128},{1,193},{65,1},{129,65},{193,129... | collective-permute-start | bytes 393224 | tf_op jit(solution)/shard_map/ppermute | solution.py:261
  163.8 4.5 %collective-permute-start.9 = (bf16[4,128,128]{2,1,0:T(8,128)(2,1)S(1)}, bf16[4,128,128]{2,1,0:T(8,128)(2,1)S(1)}, u32[]{:S(2)}, u32[]{:S(2)}) collective-permute-start(bf16[4,128,128]{2,1,0:T(8,128)(2,1)S(1)} %reduce_sum.12), channel_id=1, source_target_pairs={{0,256},{256,0},{1,257},{257,1},{2,258},{258,2},{3,259},{259,3},{4... | collective-permute-start | bytes 393224 | tf_op jit(solution)/shard_map/ppermute | solution.py:252
  168.3 0.4 collective-permute-done.8
  168.6 7.9 %collective-permute-done.9 = bf16[4,128,128]{2,1,0:T(8,128)(2,1)S(1)} collective-permute-done((bf16[4,128,128]{2,1,0:T(8,128)(2,1)S(1)}, bf16[4,128,128]{2,1,0:T(8,128)(2,1)S(1)}, u32[]{:S(2)}, u32[]{:S(2)}) %collective-permute-start.9) | collective-permute-done | bytes 131104 | tf_op jit(solution)/shard_map/ppermute | solution.py:252
  176.5 0.7 add_convert_fusion.2
  (13 shorter events, 0.1 us)
Async XLA Ops:
  0.0 13.7 %collective-permute-start = (bf16[4,128,128]{2,1,0:T(8,128)(2,1)}, bf16[4,128,128]{2,1,0:T(8,128)(2,1)S(1)}, u32[]{:S(2)}, u32[]{:S(2)}) collective-permute-start(bf16[4,128,128]{2,1,0:T(8,128)(2,1)} %bitcast.7), channel_id=1, source_target_pairs={{0,256},{256,0},{1,257},{257,1},{2,258},{258,2},{3,259},{259,3},{4... | collective-permute-start | bytes 393224 | tf_op jit(solution)/shard_map/ppermute | solution.py:252
  16.8 120.1 %collective-permute-start.3 = (bf16[16,128,128]{2,1,0:T(8,128)(2,1)S(1)}, bf16[16,128,128]{2,1,0:T(8,128)(2,1)S(1)}, u32[]{:S(2)}, u32[]{:S(2)}) collective-permute-start(bf16[16,128,128]{2,1,0:T(8,128)(2,1)S(1)} %all_gather.3.part_0), channel_id=1, source_target_pairs={{0,192},{64,0},{128,64},{192,128},{1,193},{65,1},{129,65},{193,129... | collective-permute-start | bytes 1572872 | tf_op jit(solution)/shard_map/ppermute | solution.py:261
  21.5 115.4 %collective-permute-start.2 = (bf16[16,128,128]{2,1,0:T(8,128)(2,1)S(1)}, bf16[16,128,128]{2,1,0:T(8,128)(2,1)S(1)}, u32[]{:S(2)}, u32[]{:S(2)}) collective-permute-start(bf16[16,128,128]{2,1,0:T(8,128)(2,1)S(1)} %all_gather.3.part_0), channel_id=1, source_target_pairs={{0,128},{64,192},{128,0},{192,64},{1,129},{65,193},{129,1},{193,65... | collective-permute-start | bytes 1572872 | tf_op jit(solution)/shard_map/ppermute | solution.py:261
  24.2 112.7 %collective-permute-start.1 = (bf16[16,128,128]{2,1,0:T(8,128)(2,1)S(1)}, bf16[16,128,128]{2,1,0:T(8,128)(2,1)S(1)}, u32[]{:S(2)}, u32[]{:S(2)}) collective-permute-start(bf16[16,128,128]{2,1,0:T(8,128)(2,1)S(1)} %all_gather.3.part_0), channel_id=1, source_target_pairs={{0,64},{64,128},{128,192},{192,0},{1,65},{65,129},{129,193},{193,1... | collective-permute-start | bytes 1572872 | tf_op jit(solution)/shard_map/ppermute | solution.py:261
  27.6 109.3 %copy-start = (bf16[26,128,128]{2,1,0:T(8,128)(2,1)S(1)}, bf16[26,128,128]{2,1,0:T(8,128)(2,1)}, u32[]{:S(2)}) copy-start(bf16[26,128,128]{2,1,0:T(8,128)(2,1)} %rights.1) | copy-start | bytes 2555908
  27.6 109.3 %copy-start.1 = (s32[529]{0:T(1024)S(1)}, s32[529]{0:T(1024)}, u32[]{:S(2)}) copy-start(s32[529]{0:T(1024)} %get-tuple-element.36.picked) | copy-start | bytes 6352
  141.9 4.3 %collective-permute-start.7 = (bf16[16,128,128]{2,1,0:T(8,128)(2,1)S(1)}, bf16[16,128,128]{2,1,0:T(8,128)(2,1)S(1)}, u32[]{:S(2)}, u32[]{:S(2)}) collective-permute-start(bf16[16,128,128]{2,1,0:T(8,128)(2,1)S(1)} %get-tuple-element.55), channel_id=1, source_target_pairs={{0,32},{32,0},{1,33},{33,1},{2,34},{34,2},{3,35},{35,3},{4,36},{36... | collective-permute-start | bytes 1572872 | tf_op jit(solution)/shard_map/ppermute | solution.py:252
  143.8 7.0 %collective-permute-start.4 = (bf16[16,128,128]{2,1,0:T(8,128)(2,1)}, bf16[16,128,128]{2,1,0:T(8,128)(2,1)S(1)}, u32[]{:S(2)}, u32[]{:S(2)}) collective-permute-start(bf16[16,128,128]{2,1,0:T(8,128)(2,1)} %get-tuple-element.53), channel_id=1, source_target_pairs={{0,32},{32,0},{1,33},{33,1},{2,34},{34,2},{3,35},{35,3},{4,36},{36... | collective-permute-start | bytes 1572872 | tf_op jit(solution)/shard_map/ppermute | solution.py:252
  147.2 14.5 %all-to-all-start.4 = ((bf16[16,128,128]{2,1,0:T(8,128)(2,1)}), bf16[16,128,128]{2,1,0:T(8,128)(2,1)S(1)}, u32[]{:S(2)}, u32[]{:S(2)}) async-start(bf16[16,128,128]{2,1,0:T(8,128)(2,1)} %add_convert_fusion), calls=%async_computation.4 | async-start | bytes 1048576 | tf_op jit(solution)/shard_map/all_to_all | solution.py:357
  151.0 17.3 %collective-permute-start.5 = (bf16[4,128,128]{2,1,0:T(8,128)(2,1)S(1)}, bf16[4,128,128]{2,1,0:T(8,128)(2,1)S(1)}, u32[]{:S(2)}, u32[]{:S(2)}) collective-permute-start(bf16[4,128,128]{2,1,0:T(8,128)(2,1)S(1)} %get-tuple-element.58), channel_id=1, source_target_pairs={{0,64},{64,128},{128,192},{192,0},{1,65},{65,129},{129,193},{193,1... | collective-permute-start | bytes 393224 | tf_op jit(solution)/shard_map/ppermute | solution.py:261
  154.9 13.3 %collective-permute-start.6 = (bf16[4,128,128]{2,1,0:T(8,128)(2,1)S(1)}, bf16[4,128,128]{2,1,0:T(8,128)(2,1)S(1)}, u32[]{:S(2)}, u32[]{:S(2)}) collective-permute-start(bf16[4,128,128]{2,1,0:T(8,128)(2,1)S(1)} %get-tuple-element.60), channel_id=1, source_target_pairs={{0,128},{64,192},{128,0},{192,64},{1,129},{65,193},{129,1},{193,65... | collective-permute-start | bytes 393224 | tf_op jit(solution)/shard_map/ppermute | solution.py:261
  161.8 6.9 %collective-permute-start.8 = (bf16[4,128,128]{2,1,0:T(8,128)(2,1)S(1)}, bf16[4,128,128]{2,1,0:T(8,128)(2,1)S(1)}, u32[]{:S(2)}, u32[]{:S(2)}) collective-permute-start(bf16[4,128,128]{2,1,0:T(8,128)(2,1)S(1)} %get-tuple-element.56), channel_id=1, source_target_pairs={{0,192},{64,0},{128,64},{192,128},{1,193},{65,1},{129,65},{193,129... | collective-permute-start | bytes 393224 | tf_op jit(solution)/shard_map/ppermute | solution.py:261
  163.8 12.8 %collective-permute-start.9 = (bf16[4,128,128]{2,1,0:T(8,128)(2,1)S(1)}, bf16[4,128,128]{2,1,0:T(8,128)(2,1)S(1)}, u32[]{:S(2)}, u32[]{:S(2)}) collective-permute-start(bf16[4,128,128]{2,1,0:T(8,128)(2,1)S(1)} %reduce_sum.12), channel_id=1, source_target_pairs={{0,256},{256,0},{1,257},{257,1},{2,258},{258,2},{3,259},{259,3},{4... | collective-permute-start | bytes 393224 | tf_op jit(solution)/shard_map/ppermute | solution.py:252

commit v9 on v8

--- a/solution.py
+++ b/solution.py
@@ -359,13 +359,13 @@
     cross = cross.astype(jnp.bfloat16)
     stay = add(stay, swap(other_stay, "core")).reshape((XS,) + psi.shape)
     *early, last = stay
-    cross, last = lax.optimization_barrier((cross, last))
     crossed = swap(cross, "y_hi")
-    got = [step_x(early[step], step) for step in range(1, XS - 1)]
-    got += [step_x(last, XS - 1), crossed]
     total = early[0].astype(jnp.float32)
-    for value in got:
-        total = total + value.astype(jnp.float32)
+    for step in range(1, XS - 1):
+        total = total + step_x(early[step], step).astype(jnp.float32)
+    cross, total, last = lax.optimization_barrier((cross, total, last))
+    total = total + step_x(last, XS - 1).astype(jnp.float32)
+    total = total + crossed.astype(jnp.float32)
     return total.astype(jnp.bfloat16).reshape(wavefunction.shape)
 
 

time: 178 us -> 114 us (0.64)
  blocking collectives: 111 us -> 43.3 us
  waiting for transfers between devices: 13.7 us -> 17 us
    all_to_all x1, blocking collectives: 109 us -> 41.1 us  [run(): got = lax.all_to_all(packed[slots - 1], ENV, 0, 0, tiled=True)]
    ppermute x6, waiting for transfers between devices: 0.39 us -> 7.28 us  [step_x(): return lax.ppermute(value, 'x', [(i, (i + step) % XS) for i in range(XS)])]
    pallas_call x0 -> x1, Pallas kernels: none -> 2.2 us  [run(): pl.pallas_call(place_kernel, out_shape=packing, in_specs=[pl.BlockSpec(me...]
    all_to_all x1, waiting for transfers between devices: 2.19 us -> 0.01 us  [shards(): cross = lax.all_to_all(cross, 'x', 0, 0, tiled=True)]
  transfers between devices with their start and end apart: 11 -> 11, of which waited for: 4 -> 4; matrix products, arithmetic and copies ran while one was open for 1% -> 1% of each run, Pallas kernels for 3% -> 7%
where the time goes in v9:
time: 114 us
  blocking collectives  43.3 us (38%)
  starting transfers between devices  37.8 us (33%)
  waiting for transfers between devices  17 us (15%)
  Pallas kernels  12 us (11%)
  other arithmetic  2.85 us (2%)
    all_to_all x1, blocking collectives, run(): got = lax.all_to_all(packed[slots - 1], ENV, 0, 0, tiled=True)  41.1 us
    ppermute x6, starting transfers between devices, step_x(): return lax.ppermute(value, 'x', [(i, (i + step) % XS) for i in range(XS)])  20.5 us
    ppermute x4, starting transfers between devices, swap(): return lax.ppermute(value, axis, [(0, 1), (1, 0)])  13.7 us
    ppermute x4, waiting for transfers between devices, swap(): return lax.ppermute(value, axis, [(0, 1), (1, 0)])  9.68 us
    ppermute x6, waiting for transfers between devices, step_x(): return lax.ppermute(value, 'x', [(i, (i + step) % XS) for i in range(XS)])  7.28 us
    pallas_call x1, Pallas kernels, shards(): pl.pallas_call(lambda *refs: pack_kernel(per, *refs), out_shape=(*[jax.Sh...  5.79 us
    pallas_call x1, Pallas kernels, shards(): pl.pallas_call(apply_kernel, out_shape=[block] * 4, in_specs=[smem] * 2 +...  4 us
    all_to_all x1, starting transfers between devices, shards(): cross = lax.all_to_all(cross, 'x', 0, 0, tiled=True)  3.61 us
  transfers between devices with their start and end apart: 11, of which 4 were waited for; matrix products, arithmetic and copies ran while one was open for 1% of the time, Pallas kernels for 7%

profile of v9, /device:TPU:56, one launch (start us, length us, event | category | flops | bytes accessed | tf_op | source)
XLA Modules:
  0.0 113.8 jit_solution(13253297689567703794)
XLA Ops:
  0.0 4.7 %collective-permute-start = (bf16[4,128,128]{2,1,0:T(8,128)(2,1)}, bf16[4,128,128]{2,1,0:T(8,128)(2,1)S(1)}, u32[]{:S(2)}, u32[]{:S(2)}) collective-permute-start(bf16[4,128,128]{2,1,0:T(8,128)(2,1)} %bitcast.7), channel_id=1, source_target_pairs={{0,256},{256,0},{1,257},{257,1},{2,258},{258,2},{3,259},{259,3},{4... | collective-permute-start | bytes 393224 | tf_op jit(solution)/shard_map/ppermute | solution.py:252
  4.7 5.8 %shard_map.82 = (bf16[32,128,128]{2,1,0:T(8,128)(2,1)}, bf16[64,128,128]{2,1,0:T(8,128)(2,1)}, bf16[96,128,128]{2,1,0:T(8,128)(2,1)}, bf16[128,128,128]{2,1,0:T(8,128)(2,1)}, s32[1]{0:T(128)}, /*index=5*/s32[529]{0:T(1024)}) custom-call(s32[512]{0:T(512)} %bitcast.9, s32[32]{0:T(128)} %refs_1_.1, s32[512]{0:T(512)} %refs_2_.1, s32[512]{0:T(512)} %refs_3_.1, ...), custom_call_target="tpu_custom_call" | custom-call | bytes 8388608 | tf_op jit(solution)/shard_map/pallas_call | solution.py:301
  10.5 3.2 %collective-permute-done = bf16[4,128,128]{2,1,0:T(8,128)(2,1)S(1)} collective-permute-done((bf16[4,128,128]{2,1,0:T(8,128)(2,1)}, bf16[4,128,128]{2,1,0:T(8,128)(2,1)S(1)}, u32[]{:S(2)}, u32[]{:S(2)}) %collective-permute-start) | collective-permute-done | bytes 131104 | tf_op jit(solution)/shard_map/ppermute | solution.py:252
  13.7 0.9 pad_maximum_fusion
  14.6 2.2 %all_gather.3.part_0 = bf16[16,128,128]{2,1,0:T(8,128)(2,1)S(1)} all-gather(bf16[8,128,128]{2,1,0:T(8,128)(2,1)S(1)} %pad_maximum_fusion), channel_id=1, replica_groups=mesh['y_hi'=2,'x'=4,'core'=2,'z'=8,'y_lo'=4] {'core'}, dimensions={0}, use_global_device_ids=true | all-gather | bytes 786432 | tf_op jit(solution)/shard_map/all_gather | solution.py:329
  16.8 4.7 %collective-permute-start.3 = (bf16[16,128,128]{2,1,0:T(8,128)(2,1)S(1)}, bf16[16,128,128]{2,1,0:T(8,128)(2,1)S(1)}, u32[]{:S(2)}, u32[]{:S(2)}) collective-permute-start(bf16[16,128,128]{2,1,0:T(8,128)(2,1)S(1)} %all_gather.3.part_0), channel_id=1, source_target_pairs={{0,192},{64,0},{128,64},{192,128},{1,193},{65,1},{129,65},{193,129... | collective-permute-start | bytes 1572872 | tf_op jit(solution)/shard_map/ppermute | solution.py:261
  21.5 2.7 %collective-permute-start.2 = (bf16[16,128,128]{2,1,0:T(8,128)(2,1)S(1)}, bf16[16,128,128]{2,1,0:T(8,128)(2,1)S(1)}, u32[]{:S(2)}, u32[]{:S(2)}) collective-permute-start(bf16[16,128,128]{2,1,0:T(8,128)(2,1)S(1)} %all_gather.3.part_0), channel_id=1, source_target_pairs={{0,128},{64,192},{128,0},{192,64},{1,129},{65,193},{129,1},{193,65... | collective-permute-start | bytes 1572872 | tf_op jit(solution)/shard_map/ppermute | solution.py:261
  24.2 2.8 %collective-permute-start.1 = (bf16[16,128,128]{2,1,0:T(8,128)(2,1)S(1)}, bf16[16,128,128]{2,1,0:T(8,128)(2,1)S(1)}, u32[]{:S(2)}, u32[]{:S(2)}) collective-permute-start(bf16[16,128,128]{2,1,0:T(8,128)(2,1)S(1)} %all_gather.3.part_0), channel_id=1, source_target_pairs={{0,64},{64,128},{128,192},{192,0},{1,65},{65,129},{129,193},{193,1... | collective-permute-start | bytes 1572872 | tf_op jit(solution)/shard_map/ppermute | solution.py:261
  27.6 43.3 %conditional.1 = (bf16[128,128,128]{2,1,0:T(8,128)(2,1)}) conditional(s32[]{:T(128)} %bitcast.2, bf16[32,128,128]{2,1,0:T(8,128)(2,1)} %get-tuple-element.42, bf16[64,128,128]{2,1,0:T(8,128)(2,1)} %get-tuple-element.43, bf16[96,128,128]{2,1,0:T(8,128)(2,1)} %get-tuple-element.44, ...), branch_computations={%region_0.0_spmd, %region_1.0_spmd, %region_2.0_spmd, %region_3.0_... | conditional | bytes 8388616 | solution.py:331
  27.6 41.1 %all_to_all.21.got = bf16[32,128,128]{2,1,0:T(8,128)(2,1)} all-to-all(bf16[32,128,128]{2,1,0:T(8,128)(2,1)} %param), channel_id=1, replica_groups=mesh['y_hi'=2,'x'=4,'core'=2,'z'=8,'y_lo'=4] {'z','y_lo'}, dimensions={0} | all-to-all | bytes 2097152 | tf_op jit(solution)/shard_map/cond/branch_0_fun/all_to_all | solution.py:266
  68.7 2.2 %branch_0_fun.1 = bf16[128,128,128]{2,1,0:T(8,128)(2,1)} custom-call(bf16[32,128,128]{2,1,0:T(8,128)(2,1)} %all_to_all.21.got), custom_call_target="tpu_custom_call" | custom-call | tf_op jit(solution)/shard_map/cond/branch_0_fun/pallas_call | solution.py:269
  71.0 4.0 %shard_map.83 = (bf16[16,128,128]{2,1,0:T(8,128)(2,1)S(1)}, bf16[16,128,128]{2,1,0:T(8,128)(2,1)S(1)}, bf16[16,128,128]{2,1,0:T(8,128)(2,1)}, bf16[16,128,128]{2,1,0:T(8,128)(2,1)S(1)}) custom-call(s32[529]{0:T(1024)S(1)} %copy-done.1, s32[1]{0:T(128)} %get-tuple-element.37.need, bf16[128,128,128]{2,1,0:T(8,128)(2,1)} %get-tuple-element.61.tiles, ...), custom_call_target="tpu_custom_call" | custom-call | tf_op jit(solution)/shard_map/pallas_call | solution.py:337
  75.0 1.9 %collective-permute-start.4 = (bf16[16,128,128]{2,1,0:T(8,128)(2,1)S(1)}, bf16[16,128,128]{2,1,0:T(8,128)(2,1)S(1)}, u32[]{:S(2)}, u32[]{:S(2)}) collective-permute-start(bf16[16,128,128]{2,1,0:T(8,128)(2,1)S(1)} %get-tuple-element.53), channel_id=1, source_target_pairs={{0,32},{32,0},{1,33},{33,1},{2,34},{34,2},{3,35},{35,3},{4,36},{36... | collective-permute-start | bytes 1572872 | tf_op jit(solution)/shard_map/ppermute | solution.py:252
  76.9 2.4 %collective-permute-start.5 = (bf16[16,128,128]{2,1,0:T(8,128)(2,1)}, bf16[16,128,128]{2,1,0:T(8,128)(2,1)S(1)}, u32[]{:S(2)}, u32[]{:S(2)}) collective-permute-start(bf16[16,128,128]{2,1,0:T(8,128)(2,1)} %get-tuple-element.55), channel_id=1, source_target_pairs={{0,32},{32,0},{1,33},{33,1},{2,34},{34,2},{3,35},{35,3},{4,36},{36... | collective-permute-start | bytes 1572872 | tf_op jit(solution)/shard_map/ppermute | solution.py:252
  79.4 0.9 add_convert_fusion.1
  80.3 3.6 %all-to-all-start.4 = ((bf16[16,128,128]{2,1,0:T(8,128)(2,1)}), bf16[16,128,128]{2,1,0:T(8,128)(2,1)S(1)}, u32[]{:S(2)}, u32[]{:S(2)}) async-start(bf16[16,128,128]{2,1,0:T(8,128)(2,1)} %add_convert_fusion.1), calls=%async_computation.4 | async-start | bytes 1048576 | tf_op jit(solution)/shard_map/all_to_all | solution.py:357
  84.1 5.4 %collective-permute-start.7 = (bf16[4,128,128]{2,1,0:T(8,128)(2,1)S(1)}, bf16[4,128,128]{2,1,0:T(8,128)(2,1)S(1)}, u32[]{:S(2)}, u32[]{:S(2)}) collective-permute-start(bf16[4,128,128]{2,1,0:T(8,128)(2,1)S(1)} %get-tuple-element.59), channel_id=1, source_target_pairs={{0,128},{64,192},{128,0},{192,64},{1,129},{65,193},{129,1},{193,65... | collective-permute-start | bytes 393224 | tf_op jit(solution)/shard_map/ppermute | solution.py:261
  89.5 2.5 %collective-permute-start.6 = (bf16[4,128,128]{2,1,0:T(8,128)(2,1)S(1)}, bf16[4,128,128]{2,1,0:T(8,128)(2,1)S(1)}, u32[]{:S(2)}, u32[]{:S(2)}) collective-permute-start(bf16[4,128,128]{2,1,0:T(8,128)(2,1)S(1)} %get-tuple-element.60), channel_id=1, source_target_pairs={{0,64},{64,128},{128,192},{192,0},{1,65},{65,129},{129,193},{193,1... | collective-permute-start | bytes 393224 | tf_op jit(solution)/shard_map/ppermute | solution.py:261
  92.0 5.6 %collective-permute-done.7 = bf16[4,128,128]{2,1,0:T(8,128)(2,1)S(1)} collective-permute-done((bf16[4,128,128]{2,1,0:T(8,128)(2,1)S(1)}, bf16[4,128,128]{2,1,0:T(8,128)(2,1)S(1)}, u32[]{:S(2)}, u32[]{:S(2)}) %collective-permute-start.7) | collective-permute-done | bytes 131104 | tf_op jit(solution)/shard_map/ppermute | solution.py:261
  97.6 1.7 %collective-permute-done.6 = bf16[4,128,128]{2,1,0:T(8,128)(2,1)S(1)} collective-permute-done((bf16[4,128,128]{2,1,0:T(8,128)(2,1)S(1)}, bf16[4,128,128]{2,1,0:T(8,128)(2,1)S(1)}, u32[]{:S(2)}, u32[]{:S(2)}) %collective-permute-start.6) | collective-permute-done | bytes 131104 | tf_op jit(solution)/shard_map/ppermute | solution.py:261
  99.4 4.6 %collective-permute-start.9 = (bf16[4,128,128]{2,1,0:T(8,128)(2,1)S(1)}, bf16[4,128,128]{2,1,0:T(8,128)(2,1)S(1)}, u32[]{:S(2)}, u32[]{:S(2)}) collective-permute-start(bf16[4,128,128]{2,1,0:T(8,128)(2,1)S(1)} %reduce_sum.12), channel_id=1, source_target_pairs={{0,256},{256,0},{1,257},{257,1},{2,258},{258,2},{3,259},{259,3},{4... | collective-permute-start | bytes 393224 | tf_op jit(solution)/shard_map/ppermute | solution.py:252
  104.1 2.5 %collective-permute-start.8 = (bf16[4,128,128]{2,1,0:T(8,128)(2,1)S(1)}, bf16[4,128,128]{2,1,0:T(8,128)(2,1)S(1)}, u32[]{:S(2)}, u32[]{:S(2)}) collective-permute-start(bf16[4,128,128]{2,1,0:T(8,128)(2,1)S(1)} %get-tuple-element.57), channel_id=1, source_target_pairs={{0,192},{64,0},{128,64},{192,128},{1,193},{65,1},{129,65},{193,129... | collective-permute-start | bytes 393224 | tf_op jit(solution)/shard_map/ppermute | solution.py:261
  106.6 6.5 %collective-permute-done.9 = bf16[4,128,128]{2,1,0:T(8,128)(2,1)S(1)} collective-permute-done((bf16[4,128,128]{2,1,0:T(8,128)(2,1)S(1)}, bf16[4,128,128]{2,1,0:T(8,128)(2,1)S(1)}, u32[]{:S(2)}, u32[]{:S(2)}) %collective-permute-start.9) | collective-permute-done | bytes 131104 | tf_op jit(solution)/shard_map/ppermute | solution.py:252
  113.1 0.7 add_convert_fusion.2
  (15 shorter events, 0.3 us)
Async XLA Ops:
  0.0 13.7 %collective-permute-start = (bf16[4,128,128]{2,1,0:T(8,128)(2,1)}, bf16[4,128,128]{2,1,0:T(8,128)(2,1)S(1)}, u32[]{:S(2)}, u32[]{:S(2)}) collective-permute-start(bf16[4,128,128]{2,1,0:T(8,128)(2,1)} %bitcast.7), channel_id=1, source_target_pairs={{0,256},{256,0},{1,257},{257,1},{2,258},{258,2},{3,259},{259,3},{4... | collective-permute-start | bytes 393224 | tf_op jit(solution)/shard_map/ppermute | solution.py:252
  16.8 54.1 %collective-permute-start.3 = (bf16[16,128,128]{2,1,0:T(8,128)(2,1)S(1)}, bf16[16,128,128]{2,1,0:T(8,128)(2,1)S(1)}, u32[]{:S(2)}, u32[]{:S(2)}) collective-permute-start(bf16[16,128,128]{2,1,0:T(8,128)(2,1)S(1)} %all_gather.3.part_0), channel_id=1, source_target_pairs={{0,192},{64,0},{128,64},{192,128},{1,193},{65,1},{129,65},{193,129... | collective-permute-start | bytes 1572872 | tf_op jit(solution)/shard_map/ppermute | solution.py:261
  21.5 49.5 %collective-permute-start.2 = (bf16[16,128,128]{2,1,0:T(8,128)(2,1)S(1)}, bf16[16,128,128]{2,1,0:T(8,128)(2,1)S(1)}, u32[]{:S(2)}, u32[]{:S(2)}) collective-permute-start(bf16[16,128,128]{2,1,0:T(8,128)(2,1)S(1)} %all_gather.3.part_0), channel_id=1, source_target_pairs={{0,128},{64,192},{128,0},{192,64},{1,129},{65,193},{129,1},{193,65... | collective-permute-start | bytes 1572872 | tf_op jit(solution)/shard_map/ppermute | solution.py:261
  24.2 46.8 %collective-permute-start.1 = (bf16[16,128,128]{2,1,0:T(8,128)(2,1)S(1)}, bf16[16,128,128]{2,1,0:T(8,128)(2,1)S(1)}, u32[]{:S(2)}, u32[]{:S(2)}) collective-permute-start(bf16[16,128,128]{2,1,0:T(8,128)(2,1)S(1)} %all_gather.3.part_0), channel_id=1, source_target_pairs={{0,64},{64,128},{128,192},{192,0},{1,65},{65,129},{129,193},{193,1... | collective-permute-start | bytes 1572872 | tf_op jit(solution)/shard_map/ppermute | solution.py:261
  27.6 43.4 %copy-start = (bf16[26,128,128]{2,1,0:T(8,128)(2,1)S(1)}, bf16[26,128,128]{2,1,0:T(8,128)(2,1)}, u32[]{:S(2)}) copy-start(bf16[26,128,128]{2,1,0:T(8,128)(2,1)} %rights.1) | copy-start | bytes 2555908
  27.6 43.4 %copy-start.1 = (s32[529]{0:T(1024)S(1)}, s32[529]{0:T(1024)}, u32[]{:S(2)}) copy-start(s32[529]{0:T(1024)} %get-tuple-element.36.picked) | copy-start | bytes 6352
  75.0 4.3 %collective-permute-start.4 = (bf16[16,128,128]{2,1,0:T(8,128)(2,1)S(1)}, bf16[16,128,128]{2,1,0:T(8,128)(2,1)S(1)}, u32[]{:S(2)}, u32[]{:S(2)}) collective-permute-start(bf16[16,128,128]{2,1,0:T(8,128)(2,1)S(1)} %get-tuple-element.53), channel_id=1, source_target_pairs={{0,32},{32,0},{1,33},{33,1},{2,34},{34,2},{3,35},{35,3},{4,36},{36... | collective-permute-start | bytes 1572872 | tf_op jit(solution)/shard_map/ppermute | solution.py:252
  76.9 7.0 %collective-permute-start.5 = (bf16[16,128,128]{2,1,0:T(8,128)(2,1)}, bf16[16,128,128]{2,1,0:T(8,128)(2,1)S(1)}, u32[]{:S(2)}, u32[]{:S(2)}) collective-permute-start(bf16[16,128,128]{2,1,0:T(8,128)(2,1)} %get-tuple-element.55), channel_id=1, source_target_pairs={{0,32},{32,0},{1,33},{33,1},{2,34},{34,2},{3,35},{35,3},{4,36},{36... | collective-permute-start | bytes 1572872 | tf_op jit(solution)/shard_map/ppermute | solution.py:252
  80.3 19.0 %all-to-all-start.4 = ((bf16[16,128,128]{2,1,0:T(8,128)(2,1)}), bf16[16,128,128]{2,1,0:T(8,128)(2,1)S(1)}, u32[]{:S(2)}, u32[]{:S(2)}) async-start(bf16[16,128,128]{2,1,0:T(8,128)(2,1)} %add_convert_fusion.1), calls=%async_computation.4 | async-start | bytes 1048576 | tf_op jit(solution)/shard_map/all_to_all | solution.py:357
  84.1 13.5 %collective-permute-start.7 = (bf16[4,128,128]{2,1,0:T(8,128)(2,1)S(1)}, bf16[4,128,128]{2,1,0:T(8,128)(2,1)S(1)}, u32[]{:S(2)}, u32[]{:S(2)}) collective-permute-start(bf16[4,128,128]{2,1,0:T(8,128)(2,1)S(1)} %get-tuple-element.59), channel_id=1, source_target_pairs={{0,128},{64,192},{128,0},{192,64},{1,129},{65,193},{129,1},{193,65... | collective-permute-start | bytes 393224 | tf_op jit(solution)/shard_map/ppermute | solution.py:261
  89.5 9.7 %collective-permute-start.6 = (bf16[4,128,128]{2,1,0:T(8,128)(2,1)S(1)}, bf16[4,128,128]{2,1,0:T(8,128)(2,1)S(1)}, u32[]{:S(2)}, u32[]{:S(2)}) collective-permute-start(bf16[4,128,128]{2,1,0:T(8,128)(2,1)S(1)} %get-tuple-element.60), channel_id=1, source_target_pairs={{0,64},{64,128},{128,192},{192,0},{1,65},{65,129},{129,193},{193,1... | collective-permute-start | bytes 393224 | tf_op jit(solution)/shard_map/ppermute | solution.py:261
  99.4 13.6 %collective-permute-start.9 = (bf16[4,128,128]{2,1,0:T(8,128)(2,1)S(1)}, bf16[4,128,128]{2,1,0:T(8,128)(2,1)S(1)}, u32[]{:S(2)}, u32[]{:S(2)}) collective-permute-start(bf16[4,128,128]{2,1,0:T(8,128)(2,1)S(1)} %reduce_sum.12), channel_id=1, source_target_pairs={{0,256},{256,0},{1,257},{257,1},{2,258},{258,2},{3,259},{259,3},{4... | collective-permute-start | bytes 393224 | tf_op jit(solution)/shard_map/ppermute | solution.py:252
  104.1 9.0 %collective-permute-start.8 = (bf16[4,128,128]{2,1,0:T(8,128)(2,1)S(1)}, bf16[4,128,128]{2,1,0:T(8,128)(2,1)S(1)}, u32[]{:S(2)}, u32[]{:S(2)}) collective-permute-start(bf16[4,128,128]{2,1,0:T(8,128)(2,1)S(1)} %get-tuple-element.57), channel_id=1, source_target_pairs={{0,192},{64,0},{128,64},{192,128},{1,193},{65,1},{129,65},{193,129... | collective-permute-start | bytes 393224 | tf_op jit(solution)/shard_map/ppermute | solution.py:261
